TPU v7x, 32 devices: a whole 2x2x4 slice. The times are simulated.
32 devices in a mesh: sec: 2 (over y), row: 4 (over x, core), col: 4 (over z).
Axes of the slice: x: 2, y: 2, z: 4, core: 2. Of those that a mesh axis runs over, the one named last changes fastest.
Arguments:
- sketch: float32 [32, 64, 2048], P(None, ('sec', 'row'), 'col'), parts along dimension 1, may hold values from -6 to 6
- weights: float32 [8, 64, 2048], P(None, ('sec', 'row'), 'col'), parts along dimension 1, may hold values from 0.05 to 1
Outputs:
- basis: float32 [32, 64, 2048], P(None, ('sec', 'row'), 'col'), parts along dimension 1
- factor: float32 [64, 32], P('sec'), parts along dimension 0
There are 2 independent parts, one for each index of `sec`. A program takes and returns all parts, laid end to end along the dimension named above; each array names one. Nothing has to cross between parts.
All inputs are finite; a program needn't handle non-finite values.
Results may differ from a plain program's by a relative error of at most 0.0001.
Values sent between devices are 32-bit elements; how exact they have to be, the bound alone decides.
No kernel may reach another device: no remote copies, remote signals or barrier semaphores. Data moves between devices by JAX's collectives and lax.ppermute only.
A program may use at most 64 MiB of HBM per device.

v0:
```python
import functools
import itertools

import jax
import jax.numpy as jnp
from jax import lax
from jax.experimental import pallas as pl
from jax.experimental.pallas import tpu as pltpu
from jax.sharding import PartitionSpec as P

NEIGHBOURS = ((-1, -1), (-1, 0), (-1, 1), (0, -1), (0, 1), (1, -1), (1, 0), (1, 1))
LANES = 128
PITCH = 8
HIGHEST = lax.Precision.HIGHEST


def call(kernel, out_shapes, *operands, memory=pltpu.VMEM, scratch=(), cost=None):
    return pl.pallas_call(
        kernel,
        out_shape=out_shapes,
        in_specs=[pl.BlockSpec(memory_space=memory)] * len(operands),
        out_specs=[pl.BlockSpec(memory_space=pltpu.VMEM)] * len(out_shapes),
        scratch_shapes=scratch,
        cost_estimate=cost,
        compiler_params=pltpu.CompilerParams(vmem_limit_bytes=40 * 1024 * 1024),
    )(*operands)


def f32(*shape):
    return jax.ShapeDtypeStruct(shape, jnp.float32)


def sides_of(axis):
    place = lax.axis_index(axis)
    return place % 2 == 1, place > 0, place < lax.axis_size(axis) - 1


def pack_rows_kernel(sketch, weights, by_row, weights_by_row, left, right, *rest):
    corner_messages, bulk_messages = rest[:2], rest[2:4]
    tile, weight_tile, arrived = rest[4:]
    copies = [
        pltpu.make_async_copy(sketch, tile, arrived.at[0]),
        pltpu.make_async_copy(weights, weight_tile, arrived.at[1]),
    ]
    for copy in copies:
        copy.start()
    for copy in copies:
        copy.wait()
    rows, planes, width = by_row.shape
    odd_row, _, _ = sides_of("row")
    lane = lax.broadcasted_iota(jnp.int32, (1, LANES), 1)
    own = PITCH - 2
    for target, start, low, at in ((left, 0, 2, 0), (right, width - LANES, 0, LANES - own)):
        total = None
        for row in range(rows):
            place = PITCH * (row + 2) + low
            window = slice(start, start + LANES)
            value = jnp.concatenate([tile[:, row, window], weight_tile[:, row, window]], axis=0)
            moved = rolled(value, place - at)
            moved = jnp.where((lane >= place) & (lane < place + own), moved, 0.0)
            total = moved if total is None else total + moved
        target[...] = total
    pair = 2 * PITCH
    for message, up in zip(corner_messages, (odd_row, jnp.logical_not(odd_row))):
        pieces = []
        for group in range(planes // 8 + 1):
            piece = None
            for side, strip in enumerate((left, right)):
                target = (2 * group + side) * pair if group < planes // 8 else side * pair
                value = strip[8 * group : 8 * (group + 1)]
                moved = jnp.where(up, rolled(value, target - PITCH * rows), rolled(value, target - 2 * PITCH))
                moved = jnp.where(lane // pair == target // pair, moved, 0.0)
                piece = moved if piece is None else piece + moved
            pieces.append(piece)
        message[:8] = functools.reduce(jnp.add, pieces[:-1])
        message[8:] = pieces[-1]
    for row in range(rows):
        weights_by_row[row] = weight_tile[:, row, :]
        by_row[row] = tile[:, row, :]
    for message, up in zip(bulk_messages, (odd_row, jnp.logical_not(odd_row))):
        start = jnp.where(up, rows - 2, 0)
        for slot in range(2):
            message[slot * planes : (slot + 1) * planes] = by_row[start + slot]
        message[2 * planes :] = weights_by_row[jnp.where(up, rows - 1, 0)]


def strips_kernel(rows, own_left, own_right, first_message, second_message, left, right, *col_messages):
    planes = own_left.shape[0] - 8
    odd_row, has_below, has_above = sides_of("row")
    odd_col, _, _ = sides_of("col")
    one, other = first_message[...], second_message[...]
    lane = lax.broadcasted_iota(jnp.int32, (1, LANES), 1)
    pair = 2 * PITCH
    halos = (
        (jnp.where(has_below, jnp.where(odd_row, other, one), 0.0), 0),
        (jnp.where(has_above, jnp.where(odd_row, one, other), 0.0), PITCH * (rows + 2)),
    )
    for side, (strip, target) in enumerate(((own_left, left), (own_right, right))):
        total = strip[...]
        for halo, place in halos:
            pieces = [rolled(halo[:8], place - (2 * group + side) * pair) for group in range(planes // 8)]
            pieces.append(rolled(halo[8:], place - side * pair))
            total = total + jnp.where(lane // pair == place // pair, jnp.concatenate(pieces, axis=0), 0.0)
        target[...] = total
    to_left, to_right = folded(left[...], 2), folded(right[...], PITCH - 4)
    for message, up in zip(col_messages, (odd_col, jnp.logical_not(odd_col))):
        message[...] = jnp.where(up, to_right, to_left)


def folded(strip, spot):
    lane = lax.broadcasted_iota(jnp.int32, (1, LANES), 1)
    groups = strip.shape[0] // 8
    pieces = []
    for group in range(groups):
        target = 2 * group if group < groups - 1 else 0
        moved = rolled(strip[8 * group : 8 * (group + 1)], target - spot)
        pieces.append(jnp.where((lane % PITCH) // 2 == target // 2, moved, 0.0))
    return jnp.concatenate([functools.reduce(jnp.add, pieces[:-1]), pieces[-1]], axis=0)


def unfolded(message, spot, planes):
    lane = lax.broadcasted_iota(jnp.int32, (1, LANES), 1)
    pieces = [rolled(message[:8], spot - 2 * group) for group in range(planes // 8)] + [rolled(message[8:], spot)]
    return jnp.where((lane % PITCH) // 2 == spot // 2, jnp.concatenate(pieces, axis=0), 0.0)


def rolled(value, shift):
    return pltpu.roll(value, shift % LANES, 1) if shift % LANES else value


def apply_operator(rows3, weight_rows):
    width = rows3[1].shape[1]
    total = jnp.sum(weight_rows, axis=0, keepdims=True) * rows3[1]
    for across in (0, -1, 1):
        moved = pltpu.roll(weight_rows, across % width, 1) if across else weight_rows
        terms = [
            moved[position : position + 1] * rows3[up + 1]
            for position, (up, side) in enumerate(NEIGHBOURS)
            if side == across
        ]
        part = functools.reduce(jnp.add, terms)
        total = total + (pltpu.roll(part, -across % width, 1) if across else part)
    return total


def gram_of(value, other):
    return lax.dot_general(
        value, other, (((1,), (1,)), ((), ())), precision=HIGHEST, preferred_element_type=jnp.float32
    )


def split(value):
    high = value.astype(jnp.bfloat16)
    rest = value - high.astype(jnp.float32)
    middle = rest.astype(jnp.bfloat16)
    low = (rest - middle.astype(jnp.float32)).astype(jnp.bfloat16)
    return high, middle, low


def inner_parts(image):
    width = image.shape[1]
    lane = lax.broadcasted_iota(jnp.int32, (1, LANES), 1)
    kept = [
        jnp.where(lane >= 2, image[:, :LANES], 0.0),
        image[:, LANES : width - LANES],
        jnp.where(lane < LANES - 2, image[:, width - LANES :], 0.0),
    ]
    return jnp.concatenate(split(jnp.concatenate(kept, axis=1)), axis=0)


def products_of(parts):
    return lax.dot_general(parts, parts, (((1,), (1,)), ((), ())), preferred_element_type=jnp.float32)


def images_of(middle, weights, wanted, second, products):
    for at, row in enumerate(wanted):
        parts = inner_parts(apply_operator([middle(row - 1), middle(row), middle(row + 1)], weights(row)))
        second[at] = parts
        products = products + products_of(parts)
    return products


def inner_rows_kernel(by_row, weights_by_row, middle, second, first_products, second_products):
    rows = by_row.shape[0]
    products = jnp.zeros(first_products.shape, jnp.float32)
    for row in range(1, rows - 1):
        image = apply_operator([by_row[row - 1], by_row[row], by_row[row + 1]], weights_by_row[row])
        middle[row - 1] = image
        products = products + products_of(inner_parts(image))
    first_products[...] = products
    second_products[...] = images_of(
        lambda row: middle[row - 1],
        lambda row: weights_by_row[row],
        range(2, rows - 2),
        second,
        jnp.zeros(second_products.shape, jnp.float32),
    )


def outer_rows_kernel(
    by_row,
    weights_by_row,
    first_message,
    second_message,
    middle,
    first_products,
    second_products,
    second,
    grams,
    outer,
):
    rows, planes, _ = by_row.shape
    odd_row, has_below, has_above = sides_of("row")
    one, other = first_message[...], second_message[...]
    below = jnp.where(has_below, jnp.where(odd_row, other, one), 0.0)
    above = jnp.where(has_above, jnp.where(odd_row, one, other), 0.0)

    def field(row):
        if 0 <= row < rows:
            return by_row[row]
        at = (row + 2 if row < 0 else row - rows) * planes
        return (below if row < 0 else above)[at : at + planes]

    def weights(row):
        if 0 <= row < rows:
            return weights_by_row[row]
        return (below if row < 0 else above)[2 * planes :]

    products = first_products[...]
    places = (-1, 0, rows - 1, rows)
    for at, row in enumerate(places):
        image = apply_operator([field(row - 1), field(row), field(row + 1)], weights(row))
        outer[at] = image
        if 0 <= row < rows:
            products = products + products_of(inner_parts(image))
    both = [products]
    both.append(
        images_of(
            lambda row: outer[places.index(row)] if row in places else middle[row - 1],
            weights,
            (0, 1, rows - 2, rows - 1),
            second,
            second_products[...],
        )
    )
    for at, products in enumerate(both):
        some = products[:planes] + products[planes : 2 * planes] + products[2 * planes :]
        total = some[:, :planes] + some[:, planes : 2 * planes] + some[:, 2 * planes :]
        grams[:, at * planes : (at + 1) * planes] = total


def apply_on_strip(values, weights):
    total = jnp.sum(weights, axis=0, keepdims=True) * values
    for position, (up, across) in enumerate(NEIGHBOURS):
        moved = pltpu.roll(values, (-PITCH * up - across) % LANES, 1)
        total = total + weights[position : position + 1] * moved
    return total


def late_kernel(rows, left, right, first_message, second_message, early_grams, grams, edges):
    planes = early_grams.shape[0]
    odd_col, has_left, has_right = sides_of("col")
    one, other = first_message[...], second_message[...]
    lane = lax.broadcasted_iota(jnp.int32, (1, LANES), 1)
    spot, row = lane % PITCH, lane // PITCH
    strips, masks = [], []
    for side, (strip, present, halo) in enumerate(
        ((left, has_left, jnp.where(odd_col, other, one)), (right, has_right, jnp.where(odd_col, one, other)))
    ):
        strips.append(strip[...] + jnp.where(present, unfolded(halo, side * (PITCH - 2), planes), 0.0))
        low = 2 if side == 0 else PITCH - 4
        masks.append((spot >= low) & (spot < low + 2) & (row >= 2) & (row < rows + 2))
    values = [strip[:planes] for strip in strips]
    gram = []
    for at in range(2):
        values = [apply_on_strip(value, strip[planes:]) for value, strip in zip(values, strips)]
        kept = jnp.concatenate([jnp.where(mask, value, 0.0) for mask, value in zip(masks, values)], axis=1)
        both = jnp.concatenate(values, axis=1)
        gram.append(early_grams[:, at * planes : (at + 1) * planes] + gram_of(kept, both))
    edges[...] = both
    at_row = lax.broadcasted_iota(jnp.int32, (planes, planes), 0)
    at_col = lax.broadcasted_iota(jnp.int32, (planes, planes), 1)
    mixed = jnp.where(at_row >= at_col, gram[0], gram[1])
    diagonal = jnp.sum(jnp.where(at_row == at_col, gram[1], 0.0), axis=0, keepdims=True)
    block = jnp.concatenate([mixed[8 * g : 8 * (g + 1)] for g in range(planes // 8)], axis=1)
    last = jnp.concatenate([diagonal] * (LANES // planes), axis=1)
    for target in range(grams.shape[0]):
        for at in range(8):
            grams[target, :, at * LANES : (at + 1) * LANES] = block[at : at + 1]
        grams[target, :, 8 * LANES :] = last


def eliminate(grams, planes):
    lane = lax.broadcasted_iota(jnp.int32, (8, LANES), 1)
    sub = lax.broadcasted_iota(jnp.int32, (8, LANES), 0)
    first_half = lane < 2 * planes
    groups = planes // 8
    sources = [[gram[8 * g : 8 * (g + 1)] for g in range(groups)] for gram in grams]
    state = []
    for g in range(groups):
        unit = jnp.where(sub + 8 * g == lane % (2 * planes) - planes, 1.0, 0.0)
        unit = unit[:, planes : 2 * planes]
        state.append(jnp.concatenate([sources[0][g], unit, sources[1][g], unit], axis=1))
    columns = []
    for j in range(planes):
        columns.append(
            {
                g: jnp.where(
                    first_half,
                    jnp.broadcast_to(sources[0][g][:, j : j + 1], (8, LANES)),
                    jnp.broadcast_to(sources[1][g][:, j : j + 1], (8, LANES)),
                )
                for g in range(j // 8, groups)
            }
        )
    scale = [jnp.ones((8, LANES), jnp.float32)] * groups
    for step in range(planes):
        own, at = step // 8, step % 8
        column = columns[step]
        root = lax.rsqrt(jnp.broadcast_to(column[own][at : at + 1], (8, LANES)))
        inverse = root * root
        scale[own] = jnp.where(sub == at, root, scale[own])
        factors = {g: value * inverse for g, value in column.items()}
        factors[own] = jnp.where(sub > at, factors[own], 0.0)
        for j in range(step + 1, planes):
            entry = jnp.broadcast_to(column[j // 8][j % 8 : j % 8 + 1], (8, LANES))
            for g in columns[j]:
                columns[j][g] = columns[j][g] - factors[g] * entry
        pivot_row = jnp.broadcast_to(state[own][at : at + 1], (8, LANES))
        for g in range(own, groups):
            state[g] = state[g] - factors[g] * pivot_row
    return jnp.concatenate([state[g] * scale[g] for g in range(groups)], axis=0)


def finish_kernel(pixel_count, inner_second, outer_second, edges, parts, basis, factor):
    planes = factor.shape[0]
    _, rows, width = basis.shape
    at_row = lax.broadcasted_iota(jnp.int32, (planes, planes), 0)
    at_col = lax.broadcasted_iota(jnp.int32, (planes, planes), 1)
    block = tree_sum([parts[at] for at in range(parts.shape[0])]) / pixel_count
    block = [block[:, at * LANES : (at + 1) * LANES] for at in range(9)]
    mixed, diagonal = jnp.concatenate(block[:8], axis=0), block[8][:, :planes]
    mixed = jnp.concatenate([mixed[:, at * planes : (at + 1) * planes] for at in range(LANES // planes)], axis=0)
    flipped = mixed.T
    first = jnp.where(at_row >= at_col, mixed, flipped)
    second_gram = jnp.where(at_row < at_col, mixed, jnp.where(at_row > at_col, flipped, diagonal))
    state = eliminate([first, second_gram], planes)
    first_inverse = state[:, planes : 2 * planes]
    product_upper = jnp.where(at_col >= at_row, state[:, 2 * planes : 3 * planes], 0.0)
    product_inverse = jnp.where(at_col <= at_row, state[:, 3 * planes :], 0.0)
    factor[...] = jnp.where(at_col >= at_row, gram_of(product_upper, first_inverse), 0.0)
    high, middle, low = split(product_inverse)
    left_side = jnp.concatenate([high, high, middle, high, low, middle], axis=1)

    def solved(high, middle, low):
        right_side = jnp.concatenate([high, middle, high, low, high, middle], axis=0)
        return jnp.dot(left_side, right_side, preferred_element_type=jnp.float32)

    lane = lax.broadcasted_iota(jnp.int32, (1, LANES), 1)
    outer = solved(*split(edges[...]))
    for row in range(rows):
        if 2 <= row < rows - 2:
            held, spot = inner_second, row - 2
        else:
            held, spot = outer_second, row if row < 2 else row - rows + 4
        value = solved(*(held[spot, at * planes : (at + 1) * planes] for at in range(3)))
        place = PITCH * (row + 2)
        low_end = pltpu.roll(outer[:, :LANES], LANES - (place + 2), 1)
        high_end = pltpu.roll(outer[:, LANES:], (LANES - 2 - (place + PITCH - 4)) % LANES, 1)
        basis[:, row, :LANES] = jnp.where(lane < 2, low_end, value[:, :LANES])
        basis[:, row, LANES : width - LANES] = value[:, LANES : width - LANES]
        basis[:, row, width - LANES :] = jnp.where(lane >= LANES - 2, high_end, value[:, width - LANES :])


def tree_sum(parts):
    while len(parts) > 1:
        parts = [sum(parts[at + 1 : at + 2], parts[at]) for at in range(0, len(parts), 2)]
    return parts[0]


def swap(value, axis, pairing):
    names = ("sec", "row", "col")
    shape = [lax.axis_size(name) for name in names]
    at = names.index(axis)

    def number(place):
        return (place[0] * shape[1] + place[1]) * shape[2] + place[2]

    pairs = []
    for place in itertools.product(*(range(extent) for extent in shape)):
        partner = list(place)
        partner[at] += 1 if place[at] % 2 != pairing else -1
        if not 0 <= partner[at] < shape[at]:
            partner[at] = place[at]
            partner[at - 1] ^= 1
        pairs.append((number(place), number(partner)))
    return lax.ppermute(value, names, pairs)


def on_device(sketch, weights):
    planes, rows, width = sketch.shape
    group = lax.axis_size("row") * lax.axis_size("col")
    side = f32(planes + 8, LANES)
    by_row, weights_by_row, left, right, *messages = call(
        pack_rows_kernel,
        [f32(rows, planes, width), f32(rows, 8, width), side, side]
        + [f32(16, LANES)] * 2
        + [f32(2 * planes + 8, width)] * 2,
        pltpu.with_memory_space_constraint(sketch, pltpu.HBM),
        pltpu.with_memory_space_constraint(weights, pltpu.HBM),
        memory=pltpu.HBM,
        scratch=[
            pltpu.VMEM(sketch.shape, jnp.float32),
            pltpu.VMEM(weights.shape, jnp.float32),
            pltpu.SemaphoreType.DMA((2,)),
        ],
    )
    corners = [swap(message, "row", pairing) for pairing, message in enumerate(messages[:2])]
    from_rows = [swap(message, "row", pairing) for pairing, message in enumerate(messages[2:])]
    left, right, *messages = call(
        functools.partial(strips_kernel, rows), [side, side] + [f32(16, LANES)] * 2, left, right, *corners, cost=pl.CostEstimate(flops=2000000000, bytes_accessed=4000000, transcendentals=0)
    )
    from_cols = [swap(message, "col", pairing) for pairing, message in enumerate(messages)]
    parts_of = functools.partial(jax.ShapeDtypeStruct, dtype=jnp.bfloat16)
    products = f32(3 * planes, 3 * planes)
    middle, inner_second, *inner_products = call(
        inner_rows_kernel,
        [f32(rows - 2, planes, width), parts_of((rows - 4, 3 * planes, width)), products, products],
        by_row,
        weights_by_row,
    )
    outer_second, early_grams = call(
        outer_rows_kernel,
        [parts_of((4, 3 * planes, width)), f32(planes, 2 * planes)],
        by_row,
        weights_by_row,
        *from_rows,
        middle,
        *inner_products,
        scratch=[pltpu.VMEM((4, planes, width), jnp.float32)],
    )
    grams, edges = call(
        functools.partial(late_kernel, rows),
        [f32(group, 1, 9 * LANES), f32(planes, 2 * LANES)],
        left,
        right,
        *from_cols,
        early_grams,
    )
    parts = lax.all_to_all(grams, ("row", "col"), 0, 0, tiled=True)
    return call(
        functools.partial(finish_kernel, float(rows * width * group)),
        [f32(planes, rows, width), f32(planes, planes)],
        inner_second,
        outer_second,
        edges,
        parts,
    )


def solution(mesh):
    return jax.shard_map(
        on_device,
        mesh=mesh,
        in_specs=(P(None, ("sec", "row"), "col"), P(None, ("sec", "row"), "col")),
        out_specs=(P(None, ("sec", "row"), "col"), P("sec", None)),
        check_vma=False,
    )
```

profile of v0, /device:TPU:0, one launch (start us, length us, event | category | flops | bytes accessed | tf_op | source)
XLA Modules:
  0.0 26.0 jit_solution(7447264101697573052)
XLA Ops:
  0.6 1.4 %shard_map.41 = (f32[8,32,512]{2,1,0:T(8,128)S(1)}, f32[8,8,512]{2,1,0:T(8,128)S(1)}, f32[40,128]{1,0:T(8,128)S(1)}, f32[40,128]{1,0:T(8,128)S(1)}, f32[16,128]{...) custom-call(f32[32,8,512]{2,1,0:T(8,128)} %sketch.1, f32[8,8,512]{2,1,0:T(8,128)} %weights.1), custom_call_target="tpu_custom_call" | custom-call | tf_op jit(solution)/shard_map/pallas_call | solution.py:18
  2.1 3.0 %collective-permute-start.2 = (f32[16,128]{1,0:T(8,128)S(1)}, f32[16,128]{1,0:T(8,128)S(1)}, u32[]{:S(2)}, u32[]{:S(2)}) collective-permute-start(f32[16,128]{1,0:T(8,128)S(1)} %get-tuple-element.33), channel_id=1, source_target_pairs={{0,16},{1,17},{2,18},{3,19},{4,8},{5,9},{6,10},{7,11},{8,4},{9,5},... | collective-permute-start | bytes 24584 | tf_op jit(solution)/shard_map/ppermute | solution.py:397
  5.1 0.1 collective-permute-start.3
  5.2 1.5 %collective-permute-start = (f32[72,512]{1,0:T(8,128)S(1)}, f32[72,512]{1,0:T(8,128)S(1)}, u32[]{:S(2)}, u32[]{:S(2)}) collective-permute-start(f32[72,512]{1,0:T(8,128)S(1)} %get-tuple-element.25), channel_id=1, source_target_pairs={{0,16},{1,17},{2,18},{3,19},{4,8},{5,9},{6,10},{7,11},{8,4},{9,5},... | collective-permute-start | bytes 442376 | tf_op jit(solution)/shard_map/ppermute | solution.py:397
  6.7 0.0 collective-permute-start.1
  6.7 0.0 collective-permute-done.2.first_message
  6.7 0.0 collective-permute-done.3.second_message
  6.7 0.2 shard_map.44
  6.9 0.6 %collective-permute-start.4 = (f32[16,128]{1,0:T(8,128)S(1)}, f32[16,128]{1,0:T(8,128)S(1)}, u32[]{:S(2)}, u32[]{:S(2)}) collective-permute-start(f32[16,128]{1,0:T(8,128)S(1)} %get-tuple-element.37), channel_id=1, source_target_pairs={{0,4},{1,2},{2,1},{3,7},{4,0},{5,6},{6,5},{7,3},{8,12},{9,10},{10,... | collective-permute-start | bytes 24584 | tf_op jit(solution)/shard_map/ppermute | solution.py:397
  7.5 3.2 %collective-permute-start.5 = (f32[16,128]{1,0:T(8,128)S(1)}, f32[16,128]{1,0:T(8,128)S(1)}, u32[]{:S(2)}, u32[]{:S(2)}) collective-permute-start(f32[16,128]{1,0:T(8,128)S(1)} %get-tuple-element.38), channel_id=1, source_target_pairs={{0,1},{1,0},{2,3},{3,2},{4,5},{5,4},{6,7},{7,6},{8,9},{9,8},{10,11... | collective-permute-start | bytes 24584 | tf_op jit(solution)/shard_map/ppermute | solution.py:397
  10.6 1.0 %shard_map.42 = (f32[6,32,512]{2,1,0:T(8,128)S(1)}, bf16[4,96,512]{2,1,0:T(8,128)(2,1)S(1)}, f32[96,96]{1,0:T(8,128)S(1)}, f32[96,96]{1,0:T(8,128)S(1)}) custom-call(f32[8,32,512]{2,1,0:T(8,128)S(1)} %get-tuple-element.22.by_row, f32[8,8,512]{2,1,0:T(8,128)S(1)} %get-tuple-element.23.weights_by_row), custom_call_target="tpu_custom_call" | custom-call | tf_op jit(solution)/shard_map/pallas_call | solution.py:18
  11.6 0.0 collective-permute-done.first_message
  11.6 0.0 collective-permute-done.1.second_message
  11.6 0.9 %shard_map.43 = (bf16[4,96,512]{2,1,0:T(8,128)(2,1)S(1)}, f32[32,64]{1,0:T(8,128)S(1)}) custom-call(f32[8,32,512]{2,1,0:T(8,128)S(1)} %get-tuple-element.22.by_row, f32[8,8,512]{2,1,0:T(8,128)S(1)} %get-tuple-element.23.weights_by_row, f32[72,512]{1,0:T(8,128)S(1)} %collective-permute-done.first_message, ...), custom_call_target="tpu_custom_call" | custom-call | tf_op jit(solution)/shard_map/pallas_call | solution.py:18
  12.6 0.0 collective-permute-done.4.first_message
  12.6 0.0 collective-permute-done.5.second_message
  12.6 0.7 %shard_map.45 = (f32[16,1,1152]{2,1,0:T(1,128)S(1)}, f32[32,256]{1,0:T(8,128)S(1)}) custom-call(f32[40,128]{1,0:T(8,128)S(1)} %get-tuple-element.35.left, f32[40,128]{1,0:T(8,128)S(1)} %get-tuple-element.36.right, f32[16,128]{1,0:T(8,128)S(1)} %collective-permute-done.4.first_message, f32[16,128]{1,0:T(8,128)S(1)} %collective-permute-done.5.second_message, ...), custom_call_target="tpu_custom_call" | custom-call | tf_op jit(solution)/shard_map/pallas_call | solution.py:18
  13.3 10.5 %all_to_all.5.parts = f32[16,1,1152]{2,1,0:T(1,128)S(1)} all-to-all(f32[16,1,1152]{2,1,0:T(1,128)S(1)} %get-tuple-element.41), channel_id=1, replica_groups=mesh['sec'=2,'row'=4,'col'=4] {'row','col'}, dimensions={0} | all-to-all | bytes 147456 | tf_op jit(solution)/shard_map/all_to_all | solution.py:450
  23.8 2.2 %shard_map.46 = (f32[32,8,512]{2,1,0:T(8,128)}, f32[32,32]{1,0:T(8,128)}) custom-call(bf16[4,96,512]{2,1,0:T(8,128)(2,1)S(1)} %get-tuple-element.24.inner_second, bf16[4,96,512]{2,1,0:T(8,128)(2,1)S(1)} %get-tuple-element.30.outer_second, f32[32,256]{1,0:T(8,128)S(1)} %get-tuple-element.40.edges, f32[16,1,1152]{2,1,0:T(1,128)S(1)} %all_to_all.5.parts), custom_call_target="tpu_custom_call" | custom-call | tf_op jit(solution)/shard_map/pallas_call | solution.py:18
Async XLA Ops:
  2.1 4.7 %collective-permute-start.2 = (f32[16,128]{1,0:T(8,128)S(1)}, f32[16,128]{1,0:T(8,128)S(1)}, u32[]{:S(2)}, u32[]{:S(2)}) collective-permute-start(f32[16,128]{1,0:T(8,128)S(1)} %get-tuple-element.33), channel_id=1, source_target_pairs={{0,16},{1,17},{2,18},{3,19},{4,8},{5,9},{6,10},{7,11},{8,4},{9,5},... | collective-permute-start | bytes 24584 | tf_op jit(solution)/shard_map/ppermute | solution.py:397
  5.1 1.6 %collective-permute-start.3 = (f32[16,128]{1,0:T(8,128)S(1)}, f32[16,128]{1,0:T(8,128)S(1)}, u32[]{:S(2)}, u32[]{:S(2)}) collective-permute-start(f32[16,128]{1,0:T(8,128)S(1)} %get-tuple-element.34), channel_id=1, source_target_pairs={{0,4},{1,5},{2,6},{3,7},{4,0},{5,1},{6,2},{7,3},{8,12},{9,13},{10,... | collective-permute-start | bytes 24584 | tf_op jit(solution)/shard_map/ppermute | solution.py:397
  5.2 6.4 %collective-permute-start = (f32[72,512]{1,0:T(8,128)S(1)}, f32[72,512]{1,0:T(8,128)S(1)}, u32[]{:S(2)}, u32[]{:S(2)}) collective-permute-start(f32[72,512]{1,0:T(8,128)S(1)} %get-tuple-element.25), channel_id=1, source_target_pairs={{0,16},{1,17},{2,18},{3,19},{4,8},{5,9},{6,10},{7,11},{8,4},{9,5},... | collective-permute-start | bytes 442376 | tf_op jit(solution)/shard_map/ppermute | solution.py:397
  6.7 4.9 %collective-permute-start.1 = (f32[72,512]{1,0:T(8,128)S(1)}, f32[72,512]{1,0:T(8,128)S(1)}, u32[]{:S(2)}, u32[]{:S(2)}) collective-permute-start(f32[72,512]{1,0:T(8,128)S(1)} %get-tuple-element.26), channel_id=1, source_target_pairs={{0,4},{1,5},{2,6},{3,7},{4,0},{5,1},{6,2},{7,3},{8,12},{9,13},{10,... | collective-permute-start | bytes 442376 | tf_op jit(solution)/shard_map/ppermute | solution.py:397
  6.9 5.7 %collective-permute-start.4 = (f32[16,128]{1,0:T(8,128)S(1)}, f32[16,128]{1,0:T(8,128)S(1)}, u32[]{:S(2)}, u32[]{:S(2)}) collective-permute-start(f32[16,128]{1,0:T(8,128)S(1)} %get-tuple-element.37), channel_id=1, source_target_pairs={{0,4},{1,2},{2,1},{3,7},{4,0},{5,6},{6,5},{7,3},{8,12},{9,10},{10,... | collective-permute-start | bytes 24584 | tf_op jit(solution)/shard_map/ppermute | solution.py:397
  7.5 5.1 %collective-permute-start.5 = (f32[16,128]{1,0:T(8,128)S(1)}, f32[16,128]{1,0:T(8,128)S(1)}, u32[]{:S(2)}, u32[]{:S(2)}) collective-permute-start(f32[16,128]{1,0:T(8,128)S(1)} %get-tuple-element.38), channel_id=1, source_target_pairs={{0,1},{1,0},{2,3},{3,2},{4,5},{5,4},{6,7},{7,6},{8,9},{9,8},{10,11... | collective-permute-start | bytes 24584 | tf_op jit(solution)/shard_map/ppermute | solution.py:397
where the time goes:
time: 26.2 us; the launch traced here: 26 us
  blocking collectives  10.5 us (40%)
  starting transfers between devices  8.36 us (32%)
  Pallas kernels  6.44 us (25%)
  between operations  0.69 us (3%)
    all_to_all x1, blocking collectives, on_device(): parts = lax.all_to_all(grams, ('row', 'col'), 0, 0, tiled=True)  10.5 us
    ppermute x6, starting transfers between devices, swap(): return lax.ppermute(value, names, pairs)  8.36 us
    pallas_call x6, Pallas kernels, call(): pl.pallas_call(kernel, out_shape=out_shapes, in_specs=[pl.BlockSpec(memor...  6.44 us
  transfers between devices with their start and end apart: 6, of which 0 were waited for; matrix products, arithmetic and copies ran while one was open for 0% of the time, Pallas kernels for 8%

commit v1 on v0

--- a/solution.py
+++ b/solution.py
@@ -35,8 +35,16 @@
     return place % 2 == 1, place > 0, place < lax.axis_size(axis) - 1
 
 
+def edge_columns(first, last, place):
+    lane = lax.broadcasted_iota(jnp.int32, (1, LANES), 1)
+    own = PITCH - 2
+    left = jnp.where((lane >= place + 2) & (lane < place + PITCH), rolled(first, place + 2), 0.0)
+    right = jnp.where((lane >= place) & (lane < place + own), rolled(last, place - (LANES - own)), 0.0)
+    return left, right
+
+
 def pack_rows_kernel(sketch, weights, by_row, weights_by_row, left, right, *rest):
-    corner_messages, bulk_messages = rest[:2], rest[2:4]
+    bulk_messages, diagonal_messages = rest[:2], rest[2:4]
     tile, weight_tile, arrived = rest[4:]
     copies = [
         pltpu.make_async_copy(sketch, tile, arrived.at[0]),
@@ -48,32 +56,8 @@
         copy.wait()
     rows, planes, width = by_row.shape
     odd_row, _, _ = sides_of("row")
-    lane = lax.broadcasted_iota(jnp.int32, (1, LANES), 1)
-    own = PITCH - 2
-    for target, start, low, at in ((left, 0, 2, 0), (right, width - LANES, 0, LANES - own)):
-        total = None
-        for row in range(rows):
-            place = PITCH * (row + 2) + low
-            window = slice(start, start + LANES)
-            value = jnp.concatenate([tile[:, row, window], weight_tile[:, row, window]], axis=0)
-            moved = rolled(value, place - at)
-            moved = jnp.where((lane >= place) & (lane < place + own), moved, 0.0)
-            total = moved if total is None else total + moved
-        target[...] = total
-    pair = 2 * PITCH
-    for message, up in zip(corner_messages, (odd_row, jnp.logical_not(odd_row))):
-        pieces = []
-        for group in range(planes // 8 + 1):
-            piece = None
-            for side, strip in enumerate((left, right)):
-                target = (2 * group + side) * pair if group < planes // 8 else side * pair
-                value = strip[8 * group : 8 * (group + 1)]
-                moved = jnp.where(up, rolled(value, target - PITCH * rows), rolled(value, target - 2 * PITCH))
-                moved = jnp.where(lane // pair == target // pair, moved, 0.0)
-                piece = moved if piece is None else piece + moved
-            pieces.append(piece)
-        message[:8] = functools.reduce(jnp.add, pieces[:-1])
-        message[8:] = pieces[-1]
+    odd_col, _, _ = sides_of("col")
+    lane = lax.broadcasted_iota(jnp.int32, (1, LANES), 1)
     for row in range(rows):
         weights_by_row[row] = weight_tile[:, row, :]
         by_row[row] = tile[:, row, :]
@@ -81,26 +65,54 @@
         start = jnp.where(up, rows - 2, 0)
         for slot in range(2):
             message[slot * planes : (slot + 1) * planes] = by_row[start + slot]
-        message[2 * planes :] = weights_by_row[jnp.where(up, rows - 1, 0)]
-
-
-def strips_kernel(rows, own_left, own_right, first_message, second_message, left, right, *col_messages):
+        message[2 * planes : 2 * planes + 8] = weights_by_row[jnp.where(up, rows - 1, 0)]
+    strips = [None, None]
+    for row in range(rows):
+        first = jnp.concatenate([by_row[row, :, :LANES], weights_by_row[row, :, :LANES]], axis=0)
+        last = jnp.concatenate([by_row[row, :, width - LANES :], weights_by_row[row, :, width - LANES :]], axis=0)
+        parts = edge_columns(first, last, PITCH * (row + 2))
+        strips = [part if strip is None else strip + part for strip, part in zip(strips, parts)]
+    left[...], right[...] = strips
+    pair = 2 * PITCH
+    up = jnp.logical_not(odd_row)
+    pieces = []
+    for group in range(planes // 8 + 1):
+        piece = None
+        for side, strip in enumerate(strips):
+            target = (2 * group + side) * pair if group < planes // 8 else side * pair
+            value = strip[8 * group : 8 * (group + 1)]
+            moved = jnp.where(up, rolled(value, target - PITCH * rows), rolled(value, target - 2 * PITCH))
+            moved = jnp.where(lane // pair == target // pair, moved, 0.0)
+            piece = moved if piece is None else piece + moved
+        pieces.append(piece)
+    extra = bulk_messages[1].at[2 * planes + 8 :]
+    extra[:, :LANES] = functools.reduce(jnp.add, pieces[:-1])
+    extra[:, LANES : 2 * LANES] = pieces[-1]
+    extra[:, 2 * LANES :] = jnp.zeros((8, width - 2 * LANES), jnp.float32)
+    to_left, to_right = folded(strips[0], 2), folded(strips[1], PITCH - 4)
+    for message, up in zip(diagonal_messages, (odd_col, jnp.logical_not(odd_col))):
+        edge = jnp.where(up, to_right, to_left)
+        below = jnp.where(lane < pair, rolled(edge, -PITCH * rows), 0.0)
+        start = PITCH * (rows + 2)
+        above = jnp.where((lane >= start) & (lane < start + pair), rolled(edge, PITCH * rows), 0.0)
+        message[...] = jnp.where(odd_row, below, above)
+
+
+def strips_kernel(rows, own_left, own_right, bulk_message, left, right, *col_messages):
     planes = own_left.shape[0] - 8
     odd_row, has_below, has_above = sides_of("row")
     odd_col, _, _ = sides_of("col")
-    one, other = first_message[...], second_message[...]
+    extra = bulk_message[2 * planes + 8 :, : 2 * LANES]
     lane = lax.broadcasted_iota(jnp.int32, (1, LANES), 1)
     pair = 2 * PITCH
-    halos = (
-        (jnp.where(has_below, jnp.where(odd_row, other, one), 0.0), 0),
-        (jnp.where(has_above, jnp.where(odd_row, one, other), 0.0), PITCH * (rows + 2)),
-    )
+    halos = ((odd_row & has_below, 0), (jnp.logical_not(odd_row) & has_above, PITCH * (rows + 2)))
     for side, (strip, target) in enumerate(((own_left, left), (own_right, right))):
         total = strip[...]
-        for halo, place in halos:
-            pieces = [rolled(halo[:8], place - (2 * group + side) * pair) for group in range(planes // 8)]
-            pieces.append(rolled(halo[8:], place - side * pair))
-            total = total + jnp.where(lane // pair == place // pair, jnp.concatenate(pieces, axis=0), 0.0)
+        for present, place in halos:
+            pieces = [rolled(extra[:, :LANES], place - (2 * group + side) * pair) for group in range(planes // 8)]
+            pieces.append(rolled(extra[:, LANES:], place - side * pair))
+            halo = jnp.where(lane // pair == place // pair, jnp.concatenate(pieces, axis=0), 0.0)
+            total = total + jnp.where(present, halo, 0.0)
         target[...] = total
     to_left, to_right = folded(left[...], 2), folded(right[...], PITCH - 4)
     for message, up in zip(col_messages, (odd_col, jnp.logical_not(odd_col))):
@@ -207,13 +219,28 @@
     second_products,
     second,
     grams,
+    left_halo,
+    right_halo,
     outer,
 ):
-    rows, planes, _ = by_row.shape
+    rows, planes, width = by_row.shape
     odd_row, has_below, has_above = sides_of("row")
-    one, other = first_message[...], second_message[...]
+    one, other = first_message[...], second_message[: 2 * planes + 8]
     below = jnp.where(has_below, jnp.where(odd_row, other, one), 0.0)
     above = jnp.where(has_above, jnp.where(odd_row, one, other), 0.0)
+    halos = [None, None]
+    for side, (halo, present) in enumerate(
+        ((below, jnp.logical_not(odd_row)), (above, odd_row))
+    ):
+        for slot in range(2):
+            index = slot if side == 0 else rows + 2 + slot
+            blank = jnp.zeros((8, width), jnp.float32)
+            weight = halo[2 * planes :] if slot != side else blank
+            row_values = jnp.concatenate([halo[slot * planes : (slot + 1) * planes], weight], axis=0)
+            parts = edge_columns(row_values[:, :LANES], row_values[:, width - LANES :], PITCH * index)
+            parts = [jnp.where(present, part, 0.0) for part in parts]
+            halos = [part if total is None else total + part for total, part in zip(halos, parts)]
+    left_halo[...], right_halo[...] = halos
 
     def field(row):
         if 0 <= row < rows:
@@ -257,17 +284,26 @@
     return total
 
 
-def late_kernel(rows, left, right, first_message, second_message, early_grams, grams, edges):
+def late_kernel(rows, left, right, left_halo, right_halo, *rest):
+    diagonal_messages, col_messages, (early_grams, grams, edges) = rest[:2], rest[2:4], rest[4:]
     planes = early_grams.shape[0]
+    odd_row, has_below, has_above = sides_of("row")
     odd_col, has_left, has_right = sides_of("col")
-    one, other = first_message[...], second_message[...]
+    beyond = jnp.where(odd_row, has_above, has_below)
+    one, other = (
+        col[...] + jnp.where(beyond, diagonal[...], 0.0)
+        for col, diagonal in zip(col_messages, diagonal_messages)
+    )
     lane = lax.broadcasted_iota(jnp.int32, (1, LANES), 1)
     spot, row = lane % PITCH, lane // PITCH
     strips, masks = [], []
     for side, (strip, present, halo) in enumerate(
-        ((left, has_left, jnp.where(odd_col, other, one)), (right, has_right, jnp.where(odd_col, one, other)))
+        (
+            (left[...] + left_halo[...], has_left, jnp.where(odd_col, other, one)),
+            (right[...] + right_halo[...], has_right, jnp.where(odd_col, one, other)),
+        )
     ):
-        strips.append(strip[...] + jnp.where(present, unfolded(halo, side * (PITCH - 2), planes), 0.0))
+        strips.append(strip + jnp.where(present, unfolded(halo, side * (PITCH - 2), planes), 0.0))
         low = 2 if side == 0 else PITCH - 4
         masks.append((spot >= low) & (spot < low + 2) & (row >= 2) & (row < rows + 2))
     values = [strip[:planes] for strip in strips]
@@ -378,22 +414,24 @@
     return parts[0]
 
 
-def swap(value, axis, pairing):
+def swap(value, row_pairing=None, col_pairing=None):
     names = ("sec", "row", "col")
     shape = [lax.axis_size(name) for name in names]
-    at = names.index(axis)
-
-    def number(place):
-        return (place[0] * shape[1] + place[1]) * shape[2] + place[2]
+
+    def partner(at, place, pairing):
+        other = place if pairing is None else place + 1 if place % 2 != pairing else place - 1
+        return other if 0 <= other < shape[at] else None
 
     pairs = []
-    for place in itertools.product(*(range(extent) for extent in shape)):
-        partner = list(place)
-        partner[at] += 1 if place[at] % 2 != pairing else -1
-        if not 0 <= partner[at] < shape[at]:
-            partner[at] = place[at]
-            partner[at - 1] ^= 1
-        pairs.append((number(place), number(partner)))
+    for sec, row, col in itertools.product(*(range(extent) for extent in shape)):
+        other_row, other_col = partner(1, row, row_pairing), partner(2, col, col_pairing)
+        if other_col is None:
+            target = (sec, row ^ 1, col)
+        elif other_row is None:
+            target = (sec ^ 1, row, col)
+        else:
+            target = (sec, other_row, other_col)
+        pairs.append(tuple((a * shape[1] + b) * shape[2] + c for a, b, c in ((sec, row, col), target)))
     return lax.ppermute(value, names, pairs)
 
 
@@ -404,8 +442,8 @@
     by_row, weights_by_row, left, right, *messages = call(
         pack_rows_kernel,
         [f32(rows, planes, width), f32(rows, 8, width), side, side]
-        + [f32(16, LANES)] * 2
-        + [f32(2 * planes + 8, width)] * 2,
+        + [f32(2 * planes + 8, width), f32(2 * planes + 16, width)]
+        + [f32(16, LANES)] * 2,
         pltpu.with_memory_space_constraint(sketch, pltpu.HBM),
         pltpu.with_memory_space_constraint(weights, pltpu.HBM),
         memory=pltpu.HBM,
@@ -415,12 +453,12 @@
             pltpu.SemaphoreType.DMA((2,)),
         ],
     )
-    corners = [swap(message, "row", pairing) for pairing, message in enumerate(messages[:2])]
-    from_rows = [swap(message, "row", pairing) for pairing, message in enumerate(messages[2:])]
+    from_rows = [swap(messages[at], row_pairing=at) for at in range(2)]
+    from_diagonals = [swap(messages[2 + at], row_pairing=0, col_pairing=at) for at in range(2)]
     left, right, *messages = call(
-        functools.partial(strips_kernel, rows), [side, side] + [f32(16, LANES)] * 2, left, right, *corners, cost=pl.CostEstimate(flops=2000000000, bytes_accessed=4000000, transcendentals=0)
-    )
-    from_cols = [swap(message, "col", pairing) for pairing, message in enumerate(messages)]
+        functools.partial(strips_kernel, rows), [side, side] + [f32(16, LANES)] * 2, left, right, from_rows[1]
+    )
+    from_cols = [swap(messages[at], col_pairing=at) for at in range(2)]
     parts_of = functools.partial(jax.ShapeDtypeStruct, dtype=jnp.bfloat16)
     products = f32(3 * planes, 3 * planes)
     middle, inner_second, *inner_products = call(
@@ -429,9 +467,9 @@
         by_row,
         weights_by_row,
     )
-    outer_second, early_grams = call(
+    outer_second, early_grams, *halos = call(
         outer_rows_kernel,
-        [parts_of((4, 3 * planes, width)), f32(planes, 2 * planes)],
+        [parts_of((4, 3 * planes, width)), f32(planes, 2 * planes), side, side],
         by_row,
         weights_by_row,
         *from_rows,
@@ -444,6 +482,8 @@
         [f32(group, 1, 9 * LANES), f32(planes, 2 * LANES)],
         left,
         right,
+        *halos,
+        *from_diagonals,
         *from_cols,
         early_grams,
     )

time: 26.2 us -> 25.8 us (0.985)
  blocking collectives: 10.5 us -> 9.78 us
  waiting for transfers between devices: 0.03 us -> 0.33 us
    all_to_all x1, blocking collectives: 10.5 us -> 9.78 us  [on_device(): parts = lax.all_to_all(grams, ('row', 'col'), 0, 0, tiled=True)]
    ppermute x6, waiting for transfers between devices: 0.03 us -> 0.33 us  [swap(): return lax.ppermute(value, names, pairs)]
  transfers between devices with their start and end apart: 6 -> 6, of which waited for: 0 -> 1; matrix products, arithmetic and copies ran while one was open for 0% -> 0% of each run, Pallas kernels for 8% -> 8%
where the time goes in v1:
time: 25.8 us; the launch traced here: 25.6 us
  blocking collectives  9.78 us (38%)
  starting transfers between devices  8.35 us (32%)
  Pallas kernels  6.46 us (25%)
  between operations  0.68 us (3%)
  waiting for transfers between devices  0.33 us (1%)
    all_to_all x1, blocking collectives, on_device(): parts = lax.all_to_all(grams, ('row', 'col'), 0, 0, tiled=True)  9.78 us
    ppermute x6, starting transfers between devices, swap(): return lax.ppermute(value, names, pairs)  8.35 us
    pallas_call x6, Pallas kernels, call(): pl.pallas_call(kernel, out_shape=out_shapes, in_specs=[pl.BlockSpec(memor...  6.46 us
  transfers between devices with their start and end apart: 6, of which 1 were waited for; matrix products, arithmetic and copies ran while one was open for 0% of the time, Pallas kernels for 8%

profile of v1, /device:TPU:0, one launch (start us, length us, event | category | flops | bytes accessed | tf_op | source)
XLA Modules:
  0.0 25.6 jit_solution(12532511807051925379)
XLA Ops:
  0.6 1.4 %shard_map.41 = (f32[8,32,512]{2,1,0:T(8,128)S(1)}, f32[8,8,512]{2,1,0:T(8,128)S(1)}, f32[40,128]{1,0:T(8,128)S(1)}, f32[40,128]{1,0:T(8,128)S(1)}, f32[72,512]{...) custom-call(f32[32,8,512]{2,1,0:T(8,128)} %sketch.1, f32[8,8,512]{2,1,0:T(8,128)} %weights.1), custom_call_target="tpu_custom_call" | custom-call | tf_op jit(solution)/shard_map/pallas_call | solution.py:18
  2.0 0.5 %collective-permute-start.1 = (f32[80,512]{1,0:T(8,128)S(1)}, f32[80,512]{1,0:T(8,128)S(1)}, u32[]{:S(2)}, u32[]{:S(2)}) collective-permute-start(f32[80,512]{1,0:T(8,128)S(1)} %get-tuple-element.28), channel_id=1, source_target_pairs={{0,4},{1,5},{2,6},{3,7},{4,0},{5,1},{6,2},{7,3},{8,12},{9,13},{10,... | collective-permute-start | bytes 491528 | tf_op jit(solution)/shard_map/ppermute | solution.py:435
  2.6 2.6 %collective-permute-start = (f32[72,512]{1,0:T(8,128)S(1)}, f32[72,512]{1,0:T(8,128)S(1)}, u32[]{:S(2)}, u32[]{:S(2)}) collective-permute-start(f32[72,512]{1,0:T(8,128)S(1)} %get-tuple-element.27), channel_id=1, source_target_pairs={{0,16},{1,17},{2,18},{3,19},{4,8},{5,9},{6,10},{7,11},{8,4},{9,5},... | collective-permute-start | bytes 442376 | tf_op jit(solution)/shard_map/ppermute | solution.py:435
  5.2 0.1 collective-permute-start.2
  5.2 1.5 %collective-permute-start.3 = (f32[16,128]{1,0:T(8,128)S(1)}, f32[16,128]{1,0:T(8,128)S(1)}, u32[]{:S(2)}, u32[]{:S(2)}) collective-permute-start(f32[16,128]{1,0:T(8,128)S(1)} %get-tuple-element.40), channel_id=1, source_target_pairs={{0,16},{1,17},{2,18},{3,19},{4,9},{5,8},{6,11},{7,10},{8,5},{9,4},... | collective-permute-start | bytes 24584 | tf_op jit(solution)/shard_map/ppermute | solution.py:435
  6.8 0.0 collective-permute-done.1.second_message.bulk_message
  6.8 0.1 shard_map.44
  6.9 2.3 %collective-permute-start.4 = (f32[16,128]{1,0:T(8,128)S(1)}, f32[16,128]{1,0:T(8,128)S(1)}, u32[]{:S(2)}, u32[]{:S(2)}) collective-permute-start(f32[16,128]{1,0:T(8,128)S(1)} %get-tuple-element.41), channel_id=1, source_target_pairs={{0,4},{1,2},{2,1},{3,7},{4,0},{5,6},{6,5},{7,3},{8,12},{9,10},{10,... | collective-permute-start | bytes 24584 | tf_op jit(solution)/shard_map/ppermute | solution.py:435
  9.2 1.3 %collective-permute-start.5 = (f32[16,128]{1,0:T(8,128)S(1)}, f32[16,128]{1,0:T(8,128)S(1)}, u32[]{:S(2)}, u32[]{:S(2)}) collective-permute-start(f32[16,128]{1,0:T(8,128)S(1)} %get-tuple-element.42), channel_id=1, source_target_pairs={{0,1},{1,0},{2,3},{3,2},{4,5},{5,4},{6,7},{7,6},{8,9},{9,8},{10,11... | collective-permute-start | bytes 24584 | tf_op jit(solution)/shard_map/ppermute | solution.py:435
  10.6 1.0 %shard_map.42 = (f32[6,32,512]{2,1,0:T(8,128)S(1)}, bf16[4,96,512]{2,1,0:T(8,128)(2,1)S(1)}, f32[96,96]{1,0:T(8,128)S(1)}, f32[96,96]{1,0:T(8,128)S(1)}) custom-call(f32[8,32,512]{2,1,0:T(8,128)S(1)} %get-tuple-element.24.by_row, f32[8,8,512]{2,1,0:T(8,128)S(1)} %get-tuple-element.25.weights_by_row), custom_call_target="tpu_custom_call" | custom-call | tf_op jit(solution)/shard_map/pallas_call | solution.py:18
  11.6 0.0 collective-permute-done.first_message
  11.6 1.0 %shard_map.43 = (bf16[4,96,512]{2,1,0:T(8,128)(2,1)S(1)}, f32[32,64]{1,0:T(8,128)S(1)}, f32[40,128]{1,0:T(8,128)S(1)}, f32[40,128]{1,0:T(8,128)S(1)}) custom-call(f32[8,32,512]{2,1,0:T(8,128)S(1)} %get-tuple-element.24.by_row, f32[8,8,512]{2,1,0:T(8,128)S(1)} %get-tuple-element.25.weights_by_row, f32[72,512]{1,0:T(8,128)S(1)} %collective-permute-done.first_message, ...), custom_call_target="tpu_custom_call" | custom-call | tf_op jit(solution)/shard_map/pallas_call | solution.py:18
  12.6 0.0 collective-permute-done.2.rest_0_
  12.6 0.0 collective-permute-done.3.rest_1_
  12.6 0.0 collective-permute-done.4.rest_2_
  12.6 0.3 %collective-permute-done.5.rest_3_ = f32[16,128]{1,0:T(8,128)S(1)} collective-permute-done((f32[16,128]{1,0:T(8,128)S(1)}, f32[16,128]{1,0:T(8,128)S(1)}, u32[]{:S(2)}, u32[]{:S(2)}) %collective-permute-start.5) | collective-permute-done | bytes 8224 | tf_op jit(solution)/shard_map/ppermute | solution.py:435
  12.9 0.7 %shard_map.45 = (f32[16,1,1152]{2,1,0:T(1,128)S(1)}, f32[32,256]{1,0:T(8,128)S(1)}) custom-call(f32[40,128]{1,0:T(8,128)S(1)} %get-tuple-element.35.left, f32[40,128]{1,0:T(8,128)S(1)} %get-tuple-element.36.right, f32[40,128]{1,0:T(8,128)S(1)} %get-tuple-element.37.left_halo, f32[40,128]{1,0:T(8,128)S(1)} %get-tuple-element.38.right_halo, ...), custom_call_target="tpu_custom_call" | custom-call | tf_op jit(solution)/shard_map/pallas_call | solution.py:18
  13.6 9.8 %all_to_all.5.parts = f32[16,1,1152]{2,1,0:T(1,128)S(1)} all-to-all(f32[16,1,1152]{2,1,0:T(1,128)S(1)} %get-tuple-element.45), channel_id=1, replica_groups=mesh['sec'=2,'row'=4,'col'=4] {'row','col'}, dimensions={0} | all-to-all | bytes 147456 | tf_op jit(solution)/shard_map/all_to_all | solution.py:490
  23.4 2.2 %shard_map.46 = (f32[32,8,512]{2,1,0:T(8,128)}, f32[32,32]{1,0:T(8,128)}) custom-call(bf16[4,96,512]{2,1,0:T(8,128)(2,1)S(1)} %get-tuple-element.26.inner_second, bf16[4,96,512]{2,1,0:T(8,128)(2,1)S(1)} %get-tuple-element.32.outer_second, f32[32,256]{1,0:T(8,128)S(1)} %get-tuple-element.44.edges, f32[16,1,1152]{2,1,0:T(1,128)S(1)} %all_to_all.5.parts), custom_call_target="tpu_custom_call" | custom-call | tf_op jit(solution)/shard_map/pallas_call | solution.py:18
Async XLA Ops:
  2.0 4.7 %collective-permute-start.1 = (f32[80,512]{1,0:T(8,128)S(1)}, f32[80,512]{1,0:T(8,128)S(1)}, u32[]{:S(2)}, u32[]{:S(2)}) collective-permute-start(f32[80,512]{1,0:T(8,128)S(1)} %get-tuple-element.28), channel_id=1, source_target_pairs={{0,4},{1,5},{2,6},{3,7},{4,0},{5,1},{6,2},{7,3},{8,12},{9,13},{10,... | collective-permute-start | bytes 491528 | tf_op jit(solution)/shard_map/ppermute | solution.py:435
  2.6 9.0 %collective-permute-start = (f32[72,512]{1,0:T(8,128)S(1)}, f32[72,512]{1,0:T(8,128)S(1)}, u32[]{:S(2)}, u32[]{:S(2)}) collective-permute-start(f32[72,512]{1,0:T(8,128)S(1)} %get-tuple-element.27), channel_id=1, source_target_pairs={{0,16},{1,17},{2,18},{3,19},{4,8},{5,9},{6,10},{7,11},{8,4},{9,5},... | collective-permute-start | bytes 442376 | tf_op jit(solution)/shard_map/ppermute | solution.py:435
  5.2 7.4 %collective-permute-start.2 = (f32[16,128]{1,0:T(8,128)S(1)}, f32[16,128]{1,0:T(8,128)S(1)}, u32[]{:S(2)}, u32[]{:S(2)}) collective-permute-start(f32[16,128]{1,0:T(8,128)S(1)} %get-tuple-element.39), channel_id=1, source_target_pairs={{0,4},{1,17},{2,18},{3,7},{4,0},{5,10},{6,9},{7,3},{8,12},{9,6},{1... | collective-permute-start | bytes 24584 | tf_op jit(solution)/shard_map/ppermute | solution.py:435
  5.2 7.3 %collective-permute-start.3 = (f32[16,128]{1,0:T(8,128)S(1)}, f32[16,128]{1,0:T(8,128)S(1)}, u32[]{:S(2)}, u32[]{:S(2)}) collective-permute-start(f32[16,128]{1,0:T(8,128)S(1)} %get-tuple-element.40), channel_id=1, source_target_pairs={{0,16},{1,17},{2,18},{3,19},{4,9},{5,8},{6,11},{7,10},{8,5},{9,4},... | collective-permute-start | bytes 24584 | tf_op jit(solution)/shard_map/ppermute | solution.py:435
  6.9 5.6 %collective-permute-start.4 = (f32[16,128]{1,0:T(8,128)S(1)}, f32[16,128]{1,0:T(8,128)S(1)}, u32[]{:S(2)}, u32[]{:S(2)}) collective-permute-start(f32[16,128]{1,0:T(8,128)S(1)} %get-tuple-element.41), channel_id=1, source_target_pairs={{0,4},{1,2},{2,1},{3,7},{4,0},{5,6},{6,5},{7,3},{8,12},{9,10},{10,... | collective-permute-start | bytes 24584 | tf_op jit(solution)/shard_map/ppermute | solution.py:435
  9.2 3.7 %collective-permute-start.5 = (f32[16,128]{1,0:T(8,128)S(1)}, f32[16,128]{1,0:T(8,128)S(1)}, u32[]{:S(2)}, u32[]{:S(2)}) collective-permute-start(f32[16,128]{1,0:T(8,128)S(1)} %get-tuple-element.42), channel_id=1, source_target_pairs={{0,1},{1,0},{2,3},{3,2},{4,5},{5,4},{6,7},{7,6},{8,9},{9,8},{10,11... | collective-permute-start | bytes 24584 | tf_op jit(solution)/shard_map/ppermute | solution.py:435

commit v2 on v1

--- a/solution.py
+++ b/solution.py
@@ -14,12 +14,12 @@
 HIGHEST = lax.Precision.HIGHEST
 
 
-def call(kernel, out_shapes, *operands, memory=pltpu.VMEM, scratch=(), cost=None):
+def call(kernel, out_shapes, *operands, memory=pltpu.VMEM, out_memory=pltpu.VMEM, scratch=(), cost=None):
     return pl.pallas_call(
         kernel,
         out_shape=out_shapes,
         in_specs=[pl.BlockSpec(memory_space=memory)] * len(operands),
-        out_specs=[pl.BlockSpec(memory_space=pltpu.VMEM)] * len(out_shapes),
+        out_specs=[pl.BlockSpec(memory_space=out_memory)] * len(out_shapes),
         scratch_shapes=scratch,
         cost_estimate=cost,
         compiler_params=pltpu.CompilerParams(vmem_limit_bytes=40 * 1024 * 1024),
@@ -43,9 +43,8 @@
     return left, right
 
 
-def pack_rows_kernel(sketch, weights, by_row, weights_by_row, left, right, *rest):
-    bulk_messages, diagonal_messages = rest[:2], rest[2:4]
-    tile, weight_tile, arrived = rest[4:]
+def pack_rows_kernel(sketch, weights, tile, weight_tile, left, right, *rest):
+    bulk_messages, diagonal_messages, arrived = rest[:2], rest[2:4], rest[4]
     copies = [
         pltpu.make_async_copy(sketch, tile, arrived.at[0]),
         pltpu.make_async_copy(weights, weight_tile, arrived.at[1]),
@@ -54,22 +53,21 @@
         copy.start()
     for copy in copies:
         copy.wait()
-    rows, planes, width = by_row.shape
+    planes, rows, width = tile.shape
     odd_row, _, _ = sides_of("row")
     odd_col, _, _ = sides_of("col")
     lane = lax.broadcasted_iota(jnp.int32, (1, LANES), 1)
-    for row in range(rows):
-        weights_by_row[row] = weight_tile[:, row, :]
-        by_row[row] = tile[:, row, :]
+    for slot in range(2):
+        low, high = tile[:, slot, :], tile[:, rows - 2 + slot, :]
+        for message, up in zip(bulk_messages, (odd_row, jnp.logical_not(odd_row))):
+            message[slot * planes : (slot + 1) * planes] = jnp.where(up, high, low)
+    low, high = weight_tile[:, 0, :], weight_tile[:, rows - 1, :]
     for message, up in zip(bulk_messages, (odd_row, jnp.logical_not(odd_row))):
-        start = jnp.where(up, rows - 2, 0)
-        for slot in range(2):
-            message[slot * planes : (slot + 1) * planes] = by_row[start + slot]
-        message[2 * planes : 2 * planes + 8] = weights_by_row[jnp.where(up, rows - 1, 0)]
+        message[2 * planes : 2 * planes + 8] = jnp.where(up, high, low)
     strips = [None, None]
     for row in range(rows):
-        first = jnp.concatenate([by_row[row, :, :LANES], weights_by_row[row, :, :LANES]], axis=0)
-        last = jnp.concatenate([by_row[row, :, width - LANES :], weights_by_row[row, :, width - LANES :]], axis=0)
+        first = jnp.concatenate([tile[:, row, :LANES], weight_tile[:, row, :LANES]], axis=0)
+        last = jnp.concatenate([tile[:, row, width - LANES :], weight_tile[:, row, width - LANES :]], axis=0)
         parts = edge_columns(first, last, PITCH * (row + 2))
         strips = [part if strip is None else strip + part for strip, part in zip(strips, parts)]
     left[...], right[...] = strips
@@ -184,6 +182,12 @@
     return lax.dot_general(parts, parts, (((1,), (1,)), ((), ())), preferred_element_type=jnp.float32)
 
 
+def sum_of(products):
+    planes = products.shape[0] // 3
+    some = products[:planes] + products[planes : 2 * planes] + products[2 * planes :]
+    return some[:, :planes] + some[:, planes : 2 * planes] + some[:, 2 * planes :]
+
+
 def images_of(middle, weights, wanted, second, products):
     for at, row in enumerate(wanted):
         parts = inner_parts(apply_operator([middle(row - 1), middle(row), middle(row + 1)], weights(row)))
@@ -192,8 +196,13 @@
     return products
 
 
-def inner_rows_kernel(by_row, weights_by_row, middle, second, first_products, second_products):
+def inner_rows_kernel(
+    tile, weight_tile, by_row, weights_by_row, middle, second, first_products, second_products
+):
     rows = by_row.shape[0]
+    for row in range(rows):
+        weights_by_row[row] = weight_tile[:, row, :]
+        by_row[row] = tile[:, row, :]
     products = jnp.zeros(first_products.shape, jnp.float32)
     for row in range(1, rows - 1):
         image = apply_operator([by_row[row - 1], by_row[row], by_row[row + 1]], weights_by_row[row])
@@ -271,16 +280,20 @@
         )
     )
     for at, products in enumerate(both):
-        some = products[:planes] + products[planes : 2 * planes] + products[2 * planes :]
-        total = some[:, :planes] + some[:, planes : 2 * planes] + some[:, 2 * planes :]
-        grams[:, at * planes : (at + 1) * planes] = total
+        grams[:, at * planes : (at + 1) * planes] = sum_of(products)
 
 
 def apply_on_strip(values, weights):
+    near = {up: rolled(values, -PITCH * up) for up in (-1, 0, 1)}
     total = jnp.sum(weights, axis=0, keepdims=True) * values
-    for position, (up, across) in enumerate(NEIGHBOURS):
-        moved = pltpu.roll(values, (-PITCH * up - across) % LANES, 1)
-        total = total + weights[position : position + 1] * moved
+    for across in (0, -1, 1):
+        moved = rolled(weights, across)
+        terms = [
+            moved[position : position + 1] * near[up]
+            for position, (up, side) in enumerate(NEIGHBOURS)
+            if side == across
+        ]
+        total = total + rolled(functools.reduce(jnp.add, terms), -across)
     return total
 
 
@@ -312,7 +325,8 @@
         values = [apply_on_strip(value, strip[planes:]) for value, strip in zip(values, strips)]
         kept = jnp.concatenate([jnp.where(mask, value, 0.0) for mask, value in zip(masks, values)], axis=1)
         both = jnp.concatenate(values, axis=1)
-        gram.append(early_grams[:, at * planes : (at + 1) * planes] + gram_of(kept, both))
+        products = products_of(jnp.concatenate(split(kept), axis=0))
+        gram.append(early_grams[:, at * planes : (at + 1) * planes] + sum_of(products))
     edges[...] = both
     at_row = lax.broadcasted_iota(jnp.int32, (planes, planes), 0)
     at_col = lax.broadcasted_iota(jnp.int32, (planes, planes), 1)
@@ -326,7 +340,7 @@
         grams[target, :, 8 * LANES :] = last
 
 
-def eliminate(grams, planes):
+def eliminate(grams, planes, half_way):
     lane = lax.broadcasted_iota(jnp.int32, (8, LANES), 1)
     sub = lax.broadcasted_iota(jnp.int32, (8, LANES), 0)
     first_half = lane < 2 * planes
@@ -356,56 +370,81 @@
         root = lax.rsqrt(jnp.broadcast_to(column[own][at : at + 1], (8, LANES)))
         inverse = root * root
         scale[own] = jnp.where(sub == at, root, scale[own])
-        factors = {g: value * inverse for g, value in column.items()}
-        factors[own] = jnp.where(sub > at, factors[own], 0.0)
+        left = {g: jnp.where(sub > at, value, 0.0) if g == own else value for g, value in column.items()}
+        factors = {g: value * inverse for g, value in left.items()}
         for j in range(step + 1, planes):
             entry = jnp.broadcast_to(column[j // 8][j % 8 : j % 8 + 1], (8, LANES))
             for g in columns[j]:
-                columns[j][g] = columns[j][g] - factors[g] * entry
+                change = (left[g] * entry) * inverse if j == step + 1 else factors[g] * entry
+                columns[j][g] = columns[j][g] - change
         pivot_row = jnp.broadcast_to(state[own][at : at + 1], (8, LANES))
         for g in range(own, groups):
             state[g] = state[g] - factors[g] * pivot_row
+        if step + 1 == planes // 2:
+            half_way(jnp.concatenate([state[g] * scale[g] for g in range(groups // 2)], axis=0))
     return jnp.concatenate([state[g] * scale[g] for g in range(groups)], axis=0)
 
 
-def finish_kernel(pixel_count, inner_second, outer_second, edges, parts, basis, factor):
-    planes = factor.shape[0]
-    _, rows, width = basis.shape
+def finish_kernel(
+    pixel_count, inner_second, outer_second, edges, parts, basis_out, factor_out, basis, factor, written
+):
+    planes, rows, width = basis.shape
+    half = planes // 2
     at_row = lax.broadcasted_iota(jnp.int32, (planes, planes), 0)
     at_col = lax.broadcasted_iota(jnp.int32, (planes, planes), 1)
+    lane = lax.broadcasted_iota(jnp.int32, (1, LANES), 1)
+    outer_parts = split(edges[...])
+    copies = []
+
+    def solve(inverse, start):
+        stop = start + inverse.shape[0]
+        high, middle, low = split(inverse)
+        left_side = jnp.concatenate([high, high, middle, high, low, middle], axis=1)
+
+        def solved(high, middle, low):
+            right_side = jnp.concatenate([high, middle, high, low, high, middle], axis=0)
+            return jnp.dot(left_side, right_side, preferred_element_type=jnp.float32)
+
+        outer = solved(*(part[:stop] for part in outer_parts))
+        for row in range(rows):
+            if 2 <= row < rows - 2:
+                held, spot = inner_second, row - 2
+            else:
+                held, spot = outer_second, row if row < 2 else row - rows + 4
+            value = solved(*(held[spot, at * planes : at * planes + stop] for at in range(3)))
+            place = PITCH * (row + 2)
+            first = rolled(outer[:, :LANES], -(place + 2))
+            last = rolled(outer[:, LANES:], LANES - 2 - (place + PITCH - 4))
+            basis[start:stop, row, :LANES] = jnp.where(lane < 2, first, value[:, :LANES])
+            basis[start:stop, row, LANES : width - LANES] = value[:, LANES : width - LANES]
+            basis[start:stop, row, width - LANES :] = jnp.where(
+                lane >= LANES - 2, last, value[:, width - LANES :]
+            )
+        some = pl.ds(start, stop - start)
+        copies.append(pltpu.make_async_copy(basis.at[some], basis_out.at[some], written.at[len(copies)]))
+        copies[-1].start()
+
     block = tree_sum([parts[at] for at in range(parts.shape[0])]) / pixel_count
     block = [block[:, at * LANES : (at + 1) * LANES] for at in range(9)]
     mixed, diagonal = jnp.concatenate(block[:8], axis=0), block[8][:, :planes]
     mixed = jnp.concatenate([mixed[:, at * planes : (at + 1) * planes] for at in range(LANES // planes)], axis=0)
     flipped = mixed.T
     first = jnp.where(at_row >= at_col, mixed, flipped)
-    second_gram = jnp.where(at_row < at_col, mixed, jnp.where(at_row > at_col, flipped, diagonal))
-    state = eliminate([first, second_gram], planes)
+    second = jnp.where(at_row < at_col, mixed, jnp.where(at_row > at_col, flipped, diagonal))
+    low_half = (at_col <= at_row)[:half, :half]
+    state = eliminate(
+        [first, second],
+        planes,
+        lambda state: solve(jnp.where(low_half, state[:, 3 * planes : 3 * planes + half], 0.0), 0),
+    )
     first_inverse = state[:, planes : 2 * planes]
     product_upper = jnp.where(at_col >= at_row, state[:, 2 * planes : 3 * planes], 0.0)
-    product_inverse = jnp.where(at_col <= at_row, state[:, 3 * planes :], 0.0)
+    solve(jnp.where(at_col <= at_row, state[:, 3 * planes :], 0.0)[half:], half)
     factor[...] = jnp.where(at_col >= at_row, gram_of(product_upper, first_inverse), 0.0)
-    high, middle, low = split(product_inverse)
-    left_side = jnp.concatenate([high, high, middle, high, low, middle], axis=1)
-
-    def solved(high, middle, low):
-        right_side = jnp.concatenate([high, middle, high, low, high, middle], axis=0)
-        return jnp.dot(left_side, right_side, preferred_element_type=jnp.float32)
-
-    lane = lax.broadcasted_iota(jnp.int32, (1, LANES), 1)
-    outer = solved(*split(edges[...]))
-    for row in range(rows):
-        if 2 <= row < rows - 2:
-            held, spot = inner_second, row - 2
-        else:
-            held, spot = outer_second, row if row < 2 else row - rows + 4
-        value = solved(*(held[spot, at * planes : (at + 1) * planes] for at in range(3)))
-        place = PITCH * (row + 2)
-        low_end = pltpu.roll(outer[:, :LANES], LANES - (place + 2), 1)
-        high_end = pltpu.roll(outer[:, LANES:], (LANES - 2 - (place + PITCH - 4)) % LANES, 1)
-        basis[:, row, :LANES] = jnp.where(lane < 2, low_end, value[:, :LANES])
-        basis[:, row, LANES : width - LANES] = value[:, LANES : width - LANES]
-        basis[:, row, width - LANES :] = jnp.where(lane >= LANES - 2, high_end, value[:, width - LANES :])
+    copies.append(pltpu.make_async_copy(factor, factor_out, written.at[2]))
+    copies[-1].start()
+    for copy in copies:
+        copy.wait()
 
 
 def tree_sum(parts):
@@ -439,19 +478,15 @@
     planes, rows, width = sketch.shape
     group = lax.axis_size("row") * lax.axis_size("col")
     side = f32(planes + 8, LANES)
-    by_row, weights_by_row, left, right, *messages = call(
+    tile, weight_tile, left, right, *messages = call(
         pack_rows_kernel,
-        [f32(rows, planes, width), f32(rows, 8, width), side, side]
+        [f32(*sketch.shape), f32(*weights.shape), side, side]
         + [f32(2 * planes + 8, width), f32(2 * planes + 16, width)]
         + [f32(16, LANES)] * 2,
         pltpu.with_memory_space_constraint(sketch, pltpu.HBM),
         pltpu.with_memory_space_constraint(weights, pltpu.HBM),
         memory=pltpu.HBM,
-        scratch=[
-            pltpu.VMEM(sketch.shape, jnp.float32),
-            pltpu.VMEM(weights.shape, jnp.float32),
-            pltpu.SemaphoreType.DMA((2,)),
-        ],
+        scratch=[pltpu.SemaphoreType.DMA((2,))],
     )
     from_rows = [swap(messages[at], row_pairing=at) for at in range(2)]
     from_diagonals = [swap(messages[2 + at], row_pairing=0, col_pairing=at) for at in range(2)]
@@ -461,11 +496,12 @@
     from_cols = [swap(messages[at], col_pairing=at) for at in range(2)]
     parts_of = functools.partial(jax.ShapeDtypeStruct, dtype=jnp.bfloat16)
     products = f32(3 * planes, 3 * planes)
-    middle, inner_second, *inner_products = call(
+    by_row, weights_by_row, middle, inner_second, *inner_products = call(
         inner_rows_kernel,
-        [f32(rows - 2, planes, width), parts_of((rows - 4, 3 * planes, width)), products, products],
-        by_row,
-        weights_by_row,
+        [f32(rows, planes, width), f32(rows, 8, width), f32(rows - 2, planes, width)]
+        + [parts_of((rows - 4, 3 * planes, width)), products, products],
+        tile,
+        weight_tile,
     )
     outer_second, early_grams, *halos = call(
         outer_rows_kernel,
@@ -495,6 +531,12 @@
         outer_second,
         edges,
         parts,
+        out_memory=pl.ANY,
+        scratch=[
+            pltpu.VMEM(sketch.shape, jnp.float32),
+            pltpu.VMEM((planes, planes), jnp.float32),
+            pltpu.SemaphoreType.DMA((3,)),
+        ],
     )
 
 

time: 25.8 us -> 25.8 us (level)
  no operation moved by 1% of the time
where the time goes in v2:
time: 25.8 us; the launch traced here: 25.6 us
  blocking collectives  9.78 us (38%)
  starting transfers between devices  8.35 us (32%)
  Pallas kernels  6.47 us (25%)
  between operations  0.68 us (3%)
  waiting for transfers between devices  0.3 us (1%)
    all_to_all x1, blocking collectives, on_device(): parts = lax.all_to_all(grams, ('row', 'col'), 0, 0, tiled=True)  9.78 us
    ppermute x6, starting transfers between devices, swap(): return lax.ppermute(value, names, pairs)  8.35 us
    pallas_call x6, Pallas kernels, call(): pl.pallas_call(kernel, out_shape=out_shapes, in_specs=[pl.BlockSpec(memor...  6.47 us
  transfers between devices with their start and end apart: 6, of which 1 were waited for; matrix products, arithmetic and copies ran while one was open for 0% of the time, Pallas kernels for 8%

profile of v2, /device:TPU:0, one launch (start us, length us, event | category | flops | bytes accessed | tf_op | source)
XLA Modules:
  0.0 25.6 jit_solution(3923967450921222522)
XLA Ops:
  0.6 1.4 %shard_map.41 = (f32[32,8,512]{2,1,0:T(8,128)S(1)}, f32[8,8,512]{2,1,0:T(8,128)S(1)}, f32[40,128]{1,0:T(8,128)S(1)}, f32[40,128]{1,0:T(8,128)S(1)}, f32[72,512]{...) custom-call(f32[32,8,512]{2,1,0:T(8,128)} %sketch.1, f32[8,8,512]{2,1,0:T(8,128)} %weights.1), custom_call_target="tpu_custom_call" | custom-call | tf_op jit(solution)/shard_map/pallas_call | solution.py:18
  2.1 0.5 %collective-permute-start.1 = (f32[80,512]{1,0:T(8,128)S(1)}, f32[80,512]{1,0:T(8,128)S(1)}, u32[]{:S(2)}, u32[]{:S(2)}) collective-permute-start(f32[80,512]{1,0:T(8,128)S(1)} %get-tuple-element.32), channel_id=1, source_target_pairs={{0,4},{1,5},{2,6},{3,7},{4,0},{5,1},{6,2},{7,3},{8,12},{9,13},{10,... | collective-permute-start | bytes 491528 | tf_op jit(solution)/shard_map/ppermute | solution.py:474
  2.6 2.6 %collective-permute-start = (f32[72,512]{1,0:T(8,128)S(1)}, f32[72,512]{1,0:T(8,128)S(1)}, u32[]{:S(2)}, u32[]{:S(2)}) collective-permute-start(f32[72,512]{1,0:T(8,128)S(1)} %get-tuple-element.31), channel_id=1, source_target_pairs={{0,16},{1,17},{2,18},{3,19},{4,8},{5,9},{6,10},{7,11},{8,4},{9,5},... | collective-permute-start | bytes 442376 | tf_op jit(solution)/shard_map/ppermute | solution.py:474
  5.2 0.1 collective-permute-start.2
  5.2 1.5 %collective-permute-start.3 = (f32[16,128]{1,0:T(8,128)S(1)}, f32[16,128]{1,0:T(8,128)S(1)}, u32[]{:S(2)}, u32[]{:S(2)}) collective-permute-start(f32[16,128]{1,0:T(8,128)S(1)} %get-tuple-element.44), channel_id=1, source_target_pairs={{0,16},{1,17},{2,18},{3,19},{4,9},{5,8},{6,11},{7,10},{8,5},{9,4},... | collective-permute-start | bytes 24584 | tf_op jit(solution)/shard_map/ppermute | solution.py:474
  6.8 0.0 collective-permute-done.1.second_message.bulk_message
  6.8 0.1 shard_map.44
  6.9 2.3 %collective-permute-start.4 = (f32[16,128]{1,0:T(8,128)S(1)}, f32[16,128]{1,0:T(8,128)S(1)}, u32[]{:S(2)}, u32[]{:S(2)}) collective-permute-start(f32[16,128]{1,0:T(8,128)S(1)} %get-tuple-element.45), channel_id=1, source_target_pairs={{0,4},{1,2},{2,1},{3,7},{4,0},{5,6},{6,5},{7,3},{8,12},{9,10},{10,... | collective-permute-start | bytes 24584 | tf_op jit(solution)/shard_map/ppermute | solution.py:474
  9.2 1.3 %collective-permute-start.5 = (f32[16,128]{1,0:T(8,128)S(1)}, f32[16,128]{1,0:T(8,128)S(1)}, u32[]{:S(2)}, u32[]{:S(2)}) collective-permute-start(f32[16,128]{1,0:T(8,128)S(1)} %get-tuple-element.46), channel_id=1, source_target_pairs={{0,1},{1,0},{2,3},{3,2},{4,5},{5,4},{6,7},{7,6},{8,9},{9,8},{10,11... | collective-permute-start | bytes 24584 | tf_op jit(solution)/shard_map/ppermute | solution.py:474
  10.6 1.1 %shard_map.42 = (f32[8,32,512]{2,1,0:T(8,128)S(1)}, f32[8,8,512]{2,1,0:T(8,128)S(1)}, f32[6,32,512]{2,1,0:T(8,128)S(1)}, bf16[4,96,512]{2,1,0:T(8,128)(2,1)S(1)}...) custom-call(f32[32,8,512]{2,1,0:T(8,128)S(1)} %get-tuple-element.26.tile, f32[8,8,512]{2,1,0:T(8,128)S(1)} %get-tuple-element.27.weight_tile), custom_call_target="tpu_custom_call" | custom-call | tf_op jit(solution)/shard_map/pallas_call | solution.py:18
  11.6 0.0 collective-permute-done.first_message
  11.6 0.9 %shard_map.43 = (bf16[4,96,512]{2,1,0:T(8,128)(2,1)S(1)}, f32[32,64]{1,0:T(8,128)S(1)}, f32[40,128]{1,0:T(8,128)S(1)}, f32[40,128]{1,0:T(8,128)S(1)}) custom-call(f32[8,32,512]{2,1,0:T(8,128)S(1)} %get-tuple-element.29.by_row, f32[8,8,512]{2,1,0:T(8,128)S(1)} %get-tuple-element.30.weights_by_row, f32[72,512]{1,0:T(8,128)S(1)} %collective-permute-done.first_message, ...), custom_call_target="tpu_custom_call" | custom-call | tf_op jit(solution)/shard_map/pallas_call | solution.py:18
  12.6 0.0 collective-permute-done.2.rest_0_
  12.6 0.0 collective-permute-done.3.rest_1_
  12.6 0.0 collective-permute-done.4.rest_2_
  12.6 0.3 %collective-permute-done.5.rest_3_ = f32[16,128]{1,0:T(8,128)S(1)} collective-permute-done((f32[16,128]{1,0:T(8,128)S(1)}, f32[16,128]{1,0:T(8,128)S(1)}, u32[]{:S(2)}, u32[]{:S(2)}) %collective-permute-start.5) | collective-permute-done | bytes 8224 | tf_op jit(solution)/shard_map/ppermute | solution.py:474
  12.9 0.9 %shard_map.45 = (f32[16,1,1152]{2,1,0:T(1,128)S(1)}, f32[32,256]{1,0:T(8,128)S(1)}) custom-call(f32[40,128]{1,0:T(8,128)S(1)} %get-tuple-element.39.left, f32[40,128]{1,0:T(8,128)S(1)} %get-tuple-element.40.right, f32[40,128]{1,0:T(8,128)S(1)} %get-tuple-element.41.left_halo, f32[40,128]{1,0:T(8,128)S(1)} %get-tuple-element.42.right_halo, ...), custom_call_target="tpu_custom_call" | custom-call | tf_op jit(solution)/shard_map/pallas_call | solution.py:18
  13.8 9.8 %all_to_all.5.parts = f32[16,1,1152]{2,1,0:T(1,128)S(1)} all-to-all(f32[16,1,1152]{2,1,0:T(1,128)S(1)} %get-tuple-element.49), channel_id=1, replica_groups=mesh['sec'=2,'row'=4,'col'=4] {'row','col'}, dimensions={0} | all-to-all | bytes 147456 | tf_op jit(solution)/shard_map/all_to_all | solution.py:526
  23.6 2.0 %shard_map.46 = (f32[32,8,512]{2,1,0:T(8,128)}, f32[32,32]{1,0:T(8,128)}) custom-call(bf16[4,96,512]{2,1,0:T(8,128)(2,1)S(1)} %get-tuple-element.28.inner_second, bf16[4,96,512]{2,1,0:T(8,128)(2,1)S(1)} %get-tuple-element.36.outer_second, f32[32,256]{1,0:T(8,128)S(1)} %get-tuple-element.48.edges, f32[16,1,1152]{2,1,0:T(1,128)S(1)} %all_to_all.5.parts), custom_call_target="tpu_custom_call" | custom-call | tf_op jit(solution)/shard_map/pallas_call | solution.py:18
Async XLA Ops:
  2.1 4.7 %collective-permute-start.1 = (f32[80,512]{1,0:T(8,128)S(1)}, f32[80,512]{1,0:T(8,128)S(1)}, u32[]{:S(2)}, u32[]{:S(2)}) collective-permute-start(f32[80,512]{1,0:T(8,128)S(1)} %get-tuple-element.32), channel_id=1, source_target_pairs={{0,4},{1,5},{2,6},{3,7},{4,0},{5,1},{6,2},{7,3},{8,12},{9,13},{10,... | collective-permute-start | bytes 491528 | tf_op jit(solution)/shard_map/ppermute | solution.py:474
  2.6 9.1 %collective-permute-start = (f32[72,512]{1,0:T(8,128)S(1)}, f32[72,512]{1,0:T(8,128)S(1)}, u32[]{:S(2)}, u32[]{:S(2)}) collective-permute-start(f32[72,512]{1,0:T(8,128)S(1)} %get-tuple-element.31), channel_id=1, source_target_pairs={{0,16},{1,17},{2,18},{3,19},{4,8},{5,9},{6,10},{7,11},{8,4},{9,5},... | collective-permute-start | bytes 442376 | tf_op jit(solution)/shard_map/ppermute | solution.py:474
  5.2 7.4 %collective-permute-start.2 = (f32[16,128]{1,0:T(8,128)S(1)}, f32[16,128]{1,0:T(8,128)S(1)}, u32[]{:S(2)}, u32[]{:S(2)}) collective-permute-start(f32[16,128]{1,0:T(8,128)S(1)} %get-tuple-element.43), channel_id=1, source_target_pairs={{0,4},{1,17},{2,18},{3,7},{4,0},{5,10},{6,9},{7,3},{8,12},{9,6},{1... | collective-permute-start | bytes 24584 | tf_op jit(solution)/shard_map/ppermute | solution.py:474
  5.2 7.3 %collective-permute-start.3 = (f32[16,128]{1,0:T(8,128)S(1)}, f32[16,128]{1,0:T(8,128)S(1)}, u32[]{:S(2)}, u32[]{:S(2)}) collective-permute-start(f32[16,128]{1,0:T(8,128)S(1)} %get-tuple-element.44), channel_id=1, source_target_pairs={{0,16},{1,17},{2,18},{3,19},{4,9},{5,8},{6,11},{7,10},{8,5},{9,4},... | collective-permute-start | bytes 24584 | tf_op jit(solution)/shard_map/ppermute | solution.py:474
  6.9 5.7 %collective-permute-start.4 = (f32[16,128]{1,0:T(8,128)S(1)}, f32[16,128]{1,0:T(8,128)S(1)}, u32[]{:S(2)}, u32[]{:S(2)}) collective-permute-start(f32[16,128]{1,0:T(8,128)S(1)} %get-tuple-element.45), channel_id=1, source_target_pairs={{0,4},{1,2},{2,1},{3,7},{4,0},{5,6},{6,5},{7,3},{8,12},{9,10},{10,... | collective-permute-start | bytes 24584 | tf_op jit(solution)/shard_map/ppermute | solution.py:474
  9.2 3.7 %collective-permute-start.5 = (f32[16,128]{1,0:T(8,128)S(1)}, f32[16,128]{1,0:T(8,128)S(1)}, u32[]{:S(2)}, u32[]{:S(2)}) collective-permute-start(f32[16,128]{1,0:T(8,128)S(1)} %get-tuple-element.46), channel_id=1, source_target_pairs={{0,1},{1,0},{2,3},{3,2},{4,5},{5,4},{6,7},{7,6},{8,9},{9,8},{10,11... | collective-permute-start | bytes 24584 | tf_op jit(solution)/shard_map/ppermute | solution.py:474

commit v3 on v2

--- a/solution.py
+++ b/solution.py
@@ -43,8 +43,9 @@
     return left, right
 
 
-def pack_rows_kernel(sketch, weights, tile, weight_tile, left, right, *rest):
-    bulk_messages, diagonal_messages, arrived = rest[:2], rest[2:4], rest[4]
+def pack_rows_kernel(sketch, weights, by_row, weights_by_row, left, right, *rest):
+    bulk_messages, diagonal_messages = rest[:2], rest[2:4]
+    tile, weight_tile, arrived = rest[4:]
     copies = [
         pltpu.make_async_copy(sketch, tile, arrived.at[0]),
         pltpu.make_async_copy(weights, weight_tile, arrived.at[1]),
@@ -53,21 +54,22 @@
         copy.start()
     for copy in copies:
         copy.wait()
-    planes, rows, width = tile.shape
+    rows, planes, width = by_row.shape
     odd_row, _, _ = sides_of("row")
     odd_col, _, _ = sides_of("col")
     lane = lax.broadcasted_iota(jnp.int32, (1, LANES), 1)
-    for slot in range(2):
-        low, high = tile[:, slot, :], tile[:, rows - 2 + slot, :]
-        for message, up in zip(bulk_messages, (odd_row, jnp.logical_not(odd_row))):
-            message[slot * planes : (slot + 1) * planes] = jnp.where(up, high, low)
-    low, high = weight_tile[:, 0, :], weight_tile[:, rows - 1, :]
+    for row in range(rows):
+        weights_by_row[row] = weight_tile[:, row, :]
+        by_row[row] = tile[:, row, :]
     for message, up in zip(bulk_messages, (odd_row, jnp.logical_not(odd_row))):
-        message[2 * planes : 2 * planes + 8] = jnp.where(up, high, low)
+        start = jnp.where(up, rows - 2, 0)
+        for slot in range(2):
+            message[slot * planes : (slot + 1) * planes] = by_row[start + slot]
+        message[2 * planes : 2 * planes + 8] = weights_by_row[jnp.where(up, rows - 1, 0)]
     strips = [None, None]
     for row in range(rows):
-        first = jnp.concatenate([tile[:, row, :LANES], weight_tile[:, row, :LANES]], axis=0)
-        last = jnp.concatenate([tile[:, row, width - LANES :], weight_tile[:, row, width - LANES :]], axis=0)
+        first = jnp.concatenate([by_row[row, :, :LANES], weights_by_row[row, :, :LANES]], axis=0)
+        last = jnp.concatenate([by_row[row, :, width - LANES :], weights_by_row[row, :, width - LANES :]], axis=0)
         parts = edge_columns(first, last, PITCH * (row + 2))
         strips = [part if strip is None else strip + part for strip, part in zip(strips, parts)]
     left[...], right[...] = strips
@@ -182,12 +184,6 @@
     return lax.dot_general(parts, parts, (((1,), (1,)), ((), ())), preferred_element_type=jnp.float32)
 
 
-def sum_of(products):
-    planes = products.shape[0] // 3
-    some = products[:planes] + products[planes : 2 * planes] + products[2 * planes :]
-    return some[:, :planes] + some[:, planes : 2 * planes] + some[:, 2 * planes :]
-
-
 def images_of(middle, weights, wanted, second, products):
     for at, row in enumerate(wanted):
         parts = inner_parts(apply_operator([middle(row - 1), middle(row), middle(row + 1)], weights(row)))
@@ -196,13 +192,8 @@
     return products
 
 
-def inner_rows_kernel(
-    tile, weight_tile, by_row, weights_by_row, middle, second, first_products, second_products
-):
+def inner_rows_kernel(by_row, weights_by_row, middle, second, first_products, second_products):
     rows = by_row.shape[0]
-    for row in range(rows):
-        weights_by_row[row] = weight_tile[:, row, :]
-        by_row[row] = tile[:, row, :]
     products = jnp.zeros(first_products.shape, jnp.float32)
     for row in range(1, rows - 1):
         image = apply_operator([by_row[row - 1], by_row[row], by_row[row + 1]], weights_by_row[row])
@@ -280,20 +271,16 @@
         )
     )
     for at, products in enumerate(both):
-        grams[:, at * planes : (at + 1) * planes] = sum_of(products)
+        some = products[:planes] + products[planes : 2 * planes] + products[2 * planes :]
+        total = some[:, :planes] + some[:, planes : 2 * planes] + some[:, 2 * planes :]
+        grams[:, at * planes : (at + 1) * planes] = total
 
 
 def apply_on_strip(values, weights):
-    near = {up: rolled(values, -PITCH * up) for up in (-1, 0, 1)}
     total = jnp.sum(weights, axis=0, keepdims=True) * values
-    for across in (0, -1, 1):
-        moved = rolled(weights, across)
-        terms = [
-            moved[position : position + 1] * near[up]
-            for position, (up, side) in enumerate(NEIGHBOURS)
-            if side == across
-        ]
-        total = total + rolled(functools.reduce(jnp.add, terms), -across)
+    for position, (up, across) in enumerate(NEIGHBOURS):
+        moved = pltpu.roll(values, (-PITCH * up - across) % LANES, 1)
+        total = total + weights[position : position + 1] * moved
     return total
 
 
@@ -325,8 +312,7 @@
         values = [apply_on_strip(value, strip[planes:]) for value, strip in zip(values, strips)]
         kept = jnp.concatenate([jnp.where(mask, value, 0.0) for mask, value in zip(masks, values)], axis=1)
         both = jnp.concatenate(values, axis=1)
-        products = products_of(jnp.concatenate(split(kept), axis=0))
-        gram.append(early_grams[:, at * planes : (at + 1) * planes] + sum_of(products))
+        gram.append(early_grams[:, at * planes : (at + 1) * planes] + gram_of(kept, both))
     edges[...] = both
     at_row = lax.broadcasted_iota(jnp.int32, (planes, planes), 0)
     at_col = lax.broadcasted_iota(jnp.int32, (planes, planes), 1)
@@ -478,15 +464,19 @@
     planes, rows, width = sketch.shape
     group = lax.axis_size("row") * lax.axis_size("col")
     side = f32(planes + 8, LANES)
-    tile, weight_tile, left, right, *messages = call(
+    by_row, weights_by_row, left, right, *messages = call(
         pack_rows_kernel,
-        [f32(*sketch.shape), f32(*weights.shape), side, side]
+        [f32(rows, planes, width), f32(rows, 8, width), side, side]
         + [f32(2 * planes + 8, width), f32(2 * planes + 16, width)]
         + [f32(16, LANES)] * 2,
         pltpu.with_memory_space_constraint(sketch, pltpu.HBM),
         pltpu.with_memory_space_constraint(weights, pltpu.HBM),
         memory=pltpu.HBM,
-        scratch=[pltpu.SemaphoreType.DMA((2,))],
+        scratch=[
+            pltpu.VMEM(sketch.shape, jnp.float32),
+            pltpu.VMEM(weights.shape, jnp.float32),
+            pltpu.SemaphoreType.DMA((2,)),
+        ],
     )
     from_rows = [swap(messages[at], row_pairing=at) for at in range(2)]
     from_diagonals = [swap(messages[2 + at], row_pairing=0, col_pairing=at) for at in range(2)]
@@ -496,12 +486,11 @@
     from_cols = [swap(messages[at], col_pairing=at) for at in range(2)]
     parts_of = functools.partial(jax.ShapeDtypeStruct, dtype=jnp.bfloat16)
     products = f32(3 * planes, 3 * planes)
-    by_row, weights_by_row, middle, inner_second, *inner_products = call(
+    middle, inner_second, *inner_products = call(
         inner_rows_kernel,
-        [f32(rows, planes, width), f32(rows, 8, width), f32(rows - 2, planes, width)]
-        + [parts_of((rows - 4, 3 * planes, width)), products, products],
-        tile,
-        weight_tile,
+        [f32(rows - 2, planes, width), parts_of((rows - 4, 3 * planes, width)), products, products],
+        by_row,
+        weights_by_row,
     )
     outer_second, early_grams, *halos = call(
         outer_rows_kernel,

time: 25.8 us -> 25.6 us (level)
  no operation moved by 1% of the time
where the time goes in v3:
time: 25.6 us; the launch traced here: 25.4 us
  blocking collectives  9.78 us (38%)
  starting transfers between devices  8.35 us (33%)
  Pallas kernels  6.27 us (24%)
  between operations  0.68 us (3%)
  waiting for transfers between devices  0.33 us (1%)
    all_to_all x1, blocking collectives, on_device(): parts = lax.all_to_all(grams, ('row', 'col'), 0, 0, tiled=True)  9.78 us
    ppermute x6, starting transfers between devices, swap(): return lax.ppermute(value, names, pairs)  8.35 us
    pallas_call x6, Pallas kernels, call(): pl.pallas_call(kernel, out_shape=out_shapes, in_specs=[pl.BlockSpec(memor...  6.27 us
  transfers between devices with their start and end apart: 6, of which 1 were waited for; matrix products, arithmetic and copies ran while one was open for 0% of the time, Pallas kernels for 8%

profile of v3, /device:TPU:0, one launch (start us, length us, event | category | flops | bytes accessed | tf_op | source)
XLA Modules:
  0.0 25.4 jit_solution(13777221664219391437)
XLA Ops:
  0.6 1.4 %shard_map.41 = (f32[8,32,512]{2,1,0:T(8,128)S(1)}, f32[8,8,512]{2,1,0:T(8,128)S(1)}, f32[40,128]{1,0:T(8,128)S(1)}, f32[40,128]{1,0:T(8,128)S(1)}, f32[72,512]{...) custom-call(f32[32,8,512]{2,1,0:T(8,128)} %sketch.1, f32[8,8,512]{2,1,0:T(8,128)} %weights.1), custom_call_target="tpu_custom_call" | custom-call | tf_op jit(solution)/shard_map/pallas_call | solution.py:18
  2.0 0.5 %collective-permute-start.1 = (f32[80,512]{1,0:T(8,128)S(1)}, f32[80,512]{1,0:T(8,128)S(1)}, u32[]{:S(2)}, u32[]{:S(2)}) collective-permute-start(f32[80,512]{1,0:T(8,128)S(1)} %get-tuple-element.28), channel_id=1, source_target_pairs={{0,4},{1,5},{2,6},{3,7},{4,0},{5,1},{6,2},{7,3},{8,12},{9,13},{10,... | collective-permute-start | bytes 491528 | tf_op jit(solution)/shard_map/ppermute | solution.py:460
  2.6 2.6 %collective-permute-start = (f32[72,512]{1,0:T(8,128)S(1)}, f32[72,512]{1,0:T(8,128)S(1)}, u32[]{:S(2)}, u32[]{:S(2)}) collective-permute-start(f32[72,512]{1,0:T(8,128)S(1)} %get-tuple-element.27), channel_id=1, source_target_pairs={{0,16},{1,17},{2,18},{3,19},{4,8},{5,9},{6,10},{7,11},{8,4},{9,5},... | collective-permute-start | bytes 442376 | tf_op jit(solution)/shard_map/ppermute | solution.py:460
  5.2 0.1 collective-permute-start.2
  5.2 1.5 %collective-permute-start.3 = (f32[16,128]{1,0:T(8,128)S(1)}, f32[16,128]{1,0:T(8,128)S(1)}, u32[]{:S(2)}, u32[]{:S(2)}) collective-permute-start(f32[16,128]{1,0:T(8,128)S(1)} %get-tuple-element.40), channel_id=1, source_target_pairs={{0,16},{1,17},{2,18},{3,19},{4,9},{5,8},{6,11},{7,10},{8,5},{9,4},... | collective-permute-start | bytes 24584 | tf_op jit(solution)/shard_map/ppermute | solution.py:460
  6.8 0.0 collective-permute-done.1.second_message.bulk_message
  6.8 0.1 shard_map.44
  6.9 2.3 %collective-permute-start.4 = (f32[16,128]{1,0:T(8,128)S(1)}, f32[16,128]{1,0:T(8,128)S(1)}, u32[]{:S(2)}, u32[]{:S(2)}) collective-permute-start(f32[16,128]{1,0:T(8,128)S(1)} %get-tuple-element.41), channel_id=1, source_target_pairs={{0,4},{1,2},{2,1},{3,7},{4,0},{5,6},{6,5},{7,3},{8,12},{9,10},{10,... | collective-permute-start | bytes 24584 | tf_op jit(solution)/shard_map/ppermute | solution.py:460
  9.2 1.3 %collective-permute-start.5 = (f32[16,128]{1,0:T(8,128)S(1)}, f32[16,128]{1,0:T(8,128)S(1)}, u32[]{:S(2)}, u32[]{:S(2)}) collective-permute-start(f32[16,128]{1,0:T(8,128)S(1)} %get-tuple-element.42), channel_id=1, source_target_pairs={{0,1},{1,0},{2,3},{3,2},{4,5},{5,4},{6,7},{7,6},{8,9},{9,8},{10,11... | collective-permute-start | bytes 24584 | tf_op jit(solution)/shard_map/ppermute | solution.py:460
  10.6 1.0 %shard_map.42 = (f32[6,32,512]{2,1,0:T(8,128)S(1)}, bf16[4,96,512]{2,1,0:T(8,128)(2,1)S(1)}, f32[96,96]{1,0:T(8,128)S(1)}, f32[96,96]{1,0:T(8,128)S(1)}) custom-call(f32[8,32,512]{2,1,0:T(8,128)S(1)} %get-tuple-element.24.by_row, f32[8,8,512]{2,1,0:T(8,128)S(1)} %get-tuple-element.25.weights_by_row), custom_call_target="tpu_custom_call" | custom-call | tf_op jit(solution)/shard_map/pallas_call | solution.py:18
  11.6 0.0 collective-permute-done.first_message
  11.6 1.0 %shard_map.43 = (bf16[4,96,512]{2,1,0:T(8,128)(2,1)S(1)}, f32[32,64]{1,0:T(8,128)S(1)}, f32[40,128]{1,0:T(8,128)S(1)}, f32[40,128]{1,0:T(8,128)S(1)}) custom-call(f32[8,32,512]{2,1,0:T(8,128)S(1)} %get-tuple-element.24.by_row, f32[8,8,512]{2,1,0:T(8,128)S(1)} %get-tuple-element.25.weights_by_row, f32[72,512]{1,0:T(8,128)S(1)} %collective-permute-done.first_message, ...), custom_call_target="tpu_custom_call" | custom-call | tf_op jit(solution)/shard_map/pallas_call | solution.py:18
  12.6 0.0 collective-permute-done.2.rest_0_
  12.6 0.0 collective-permute-done.3.rest_1_
  12.6 0.0 collective-permute-done.4.rest_2_
  12.6 0.3 %collective-permute-done.5.rest_3_ = f32[16,128]{1,0:T(8,128)S(1)} collective-permute-done((f32[16,128]{1,0:T(8,128)S(1)}, f32[16,128]{1,0:T(8,128)S(1)}, u32[]{:S(2)}, u32[]{:S(2)}) %collective-permute-start.5) | collective-permute-done | bytes 8224 | tf_op jit(solution)/shard_map/ppermute | solution.py:460
  12.9 0.7 %shard_map.45 = (f32[16,1,1152]{2,1,0:T(1,128)S(1)}, f32[32,256]{1,0:T(8,128)S(1)}) custom-call(f32[40,128]{1,0:T(8,128)S(1)} %get-tuple-element.35.left, f32[40,128]{1,0:T(8,128)S(1)} %get-tuple-element.36.right, f32[40,128]{1,0:T(8,128)S(1)} %get-tuple-element.37.left_halo, f32[40,128]{1,0:T(8,128)S(1)} %get-tuple-element.38.right_halo, ...), custom_call_target="tpu_custom_call" | custom-call | tf_op jit(solution)/shard_map/pallas_call | solution.py:18
  13.6 9.8 %all_to_all.5.parts = f32[16,1,1152]{2,1,0:T(1,128)S(1)} all-to-all(f32[16,1,1152]{2,1,0:T(1,128)S(1)} %get-tuple-element.45), channel_id=1, replica_groups=mesh['sec'=2,'row'=4,'col'=4] {'row','col'}, dimensions={0} | all-to-all | bytes 147456 | tf_op jit(solution)/shard_map/all_to_all | solution.py:515
  23.4 2.0 %shard_map.46 = (f32[32,8,512]{2,1,0:T(8,128)}, f32[32,32]{1,0:T(8,128)}) custom-call(bf16[4,96,512]{2,1,0:T(8,128)(2,1)S(1)} %get-tuple-element.26.inner_second, bf16[4,96,512]{2,1,0:T(8,128)(2,1)S(1)} %get-tuple-element.32.outer_second, f32[32,256]{1,0:T(8,128)S(1)} %get-tuple-element.44.edges, f32[16,1,1152]{2,1,0:T(1,128)S(1)} %all_to_all.5.parts), custom_call_target="tpu_custom_call" | custom-call | tf_op jit(solution)/shard_map/pallas_call | solution.py:18
Async XLA Ops:
  2.0 4.7 %collective-permute-start.1 = (f32[80,512]{1,0:T(8,128)S(1)}, f32[80,512]{1,0:T(8,128)S(1)}, u32[]{:S(2)}, u32[]{:S(2)}) collective-permute-start(f32[80,512]{1,0:T(8,128)S(1)} %get-tuple-element.28), channel_id=1, source_target_pairs={{0,4},{1,5},{2,6},{3,7},{4,0},{5,1},{6,2},{7,3},{8,12},{9,13},{10,... | collective-permute-start | bytes 491528 | tf_op jit(solution)/shard_map/ppermute | solution.py:460
  2.6 9.0 %collective-permute-start = (f32[72,512]{1,0:T(8,128)S(1)}, f32[72,512]{1,0:T(8,128)S(1)}, u32[]{:S(2)}, u32[]{:S(2)}) collective-permute-start(f32[72,512]{1,0:T(8,128)S(1)} %get-tuple-element.27), channel_id=1, source_target_pairs={{0,16},{1,17},{2,18},{3,19},{4,8},{5,9},{6,10},{7,11},{8,4},{9,5},... | collective-permute-start | bytes 442376 | tf_op jit(solution)/shard_map/ppermute | solution.py:460
  5.2 7.4 %collective-permute-start.2 = (f32[16,128]{1,0:T(8,128)S(1)}, f32[16,128]{1,0:T(8,128)S(1)}, u32[]{:S(2)}, u32[]{:S(2)}) collective-permute-start(f32[16,128]{1,0:T(8,128)S(1)} %get-tuple-element.39), channel_id=1, source_target_pairs={{0,4},{1,17},{2,18},{3,7},{4,0},{5,10},{6,9},{7,3},{8,12},{9,6},{1... | collective-permute-start | bytes 24584 | tf_op jit(solution)/shard_map/ppermute | solution.py:460
  5.2 7.3 %collective-permute-start.3 = (f32[16,128]{1,0:T(8,128)S(1)}, f32[16,128]{1,0:T(8,128)S(1)}, u32[]{:S(2)}, u32[]{:S(2)}) collective-permute-start(f32[16,128]{1,0:T(8,128)S(1)} %get-tuple-element.40), channel_id=1, source_target_pairs={{0,16},{1,17},{2,18},{3,19},{4,9},{5,8},{6,11},{7,10},{8,5},{9,4},... | collective-permute-start | bytes 24584 | tf_op jit(solution)/shard_map/ppermute | solution.py:460
  6.9 5.6 %collective-permute-start.4 = (f32[16,128]{1,0:T(8,128)S(1)}, f32[16,128]{1,0:T(8,128)S(1)}, u32[]{:S(2)}, u32[]{:S(2)}) collective-permute-start(f32[16,128]{1,0:T(8,128)S(1)} %get-tuple-element.41), channel_id=1, source_target_pairs={{0,4},{1,2},{2,1},{3,7},{4,0},{5,6},{6,5},{7,3},{8,12},{9,10},{10,... | collective-permute-start | bytes 24584 | tf_op jit(solution)/shard_map/ppermute | solution.py:460
  9.2 3.7 %collective-permute-start.5 = (f32[16,128]{1,0:T(8,128)S(1)}, f32[16,128]{1,0:T(8,128)S(1)}, u32[]{:S(2)}, u32[]{:S(2)}) collective-permute-start(f32[16,128]{1,0:T(8,128)S(1)} %get-tuple-element.42), channel_id=1, source_target_pairs={{0,1},{1,0},{2,3},{3,2},{4,5},{5,4},{6,7},{7,6},{8,9},{9,8},{10,11... | collective-permute-start | bytes 24584 | tf_op jit(solution)/shard_map/ppermute | solution.py:460

commit v4 on v3

--- a/solution.py
+++ b/solution.py
@@ -38,8 +38,8 @@
 def edge_columns(first, last, place):
     lane = lax.broadcasted_iota(jnp.int32, (1, LANES), 1)
     own = PITCH - 2
-    left = jnp.where((lane >= place + 2) & (lane < place + PITCH), rolled(first, place + 2), 0.0)
-    right = jnp.where((lane >= place) & (lane < place + own), rolled(last, place - (LANES - own)), 0.0)
+    left = jnp.where((lane >= place + 2) & (lane < place + PITCH), pltpu.roll(first, place + 2, 1), 0.0)
+    right = jnp.where((lane >= place) & (lane < place + own), pltpu.roll(last, place + own, 1), 0.0)
     return left, right
 
 
@@ -73,22 +73,8 @@
         parts = edge_columns(first, last, PITCH * (row + 2))
         strips = [part if strip is None else strip + part for strip, part in zip(strips, parts)]
     left[...], right[...] = strips
+    bulk_messages[0][2 * planes + 8 :] = jnp.zeros((8, width), jnp.float32)
     pair = 2 * PITCH
-    up = jnp.logical_not(odd_row)
-    pieces = []
-    for group in range(planes // 8 + 1):
-        piece = None
-        for side, strip in enumerate(strips):
-            target = (2 * group + side) * pair if group < planes // 8 else side * pair
-            value = strip[8 * group : 8 * (group + 1)]
-            moved = jnp.where(up, rolled(value, target - PITCH * rows), rolled(value, target - 2 * PITCH))
-            moved = jnp.where(lane // pair == target // pair, moved, 0.0)
-            piece = moved if piece is None else piece + moved
-        pieces.append(piece)
-    extra = bulk_messages[1].at[2 * planes + 8 :]
-    extra[:, :LANES] = functools.reduce(jnp.add, pieces[:-1])
-    extra[:, LANES : 2 * LANES] = pieces[-1]
-    extra[:, 2 * LANES :] = jnp.zeros((8, width - 2 * LANES), jnp.float32)
     to_left, to_right = folded(strips[0], 2), folded(strips[1], PITCH - 4)
     for message, up in zip(diagonal_messages, (odd_col, jnp.logical_not(odd_col))):
         edge = jnp.where(up, to_right, to_left)
@@ -102,18 +88,17 @@
     planes = own_left.shape[0] - 8
     odd_row, has_below, has_above = sides_of("row")
     odd_col, _, _ = sides_of("col")
-    extra = bulk_message[2 * planes + 8 :, : 2 * LANES]
-    lane = lax.broadcasted_iota(jnp.int32, (1, LANES), 1)
-    pair = 2 * PITCH
-    halos = ((odd_row & has_below, 0), (jnp.logical_not(odd_row) & has_above, PITCH * (rows + 2)))
-    for side, (strip, target) in enumerate(((own_left, left), (own_right, right))):
-        total = strip[...]
-        for present, place in halos:
-            pieces = [rolled(extra[:, :LANES], place - (2 * group + side) * pair) for group in range(planes // 8)]
-            pieces.append(rolled(extra[:, LANES:], place - side * pair))
-            halo = jnp.where(lane // pair == place // pair, jnp.concatenate(pieces, axis=0), 0.0)
-            total = total + jnp.where(present, halo, 0.0)
-        target[...] = total
+    width = bulk_message.shape[1]
+    totals = [own_left[...], own_right[...]]
+    present = jnp.where(odd_row, has_below, has_above)
+    for slot in range(2):
+        place = PITCH * (slot + jnp.where(odd_row, 0, rows + 2))
+        halo = [bulk_message[slot * planes : (slot + 1) * planes], bulk_message[2 * planes :]]
+        first = jnp.concatenate([part[:, :LANES] for part in halo], axis=0)
+        last = jnp.concatenate([part[:, width - LANES :] for part in halo], axis=0)
+        parts = edge_columns(first, last, place)
+        totals = [total + jnp.where(present, part, 0.0) for total, part in zip(totals, parts)]
+    left[...], right[...] = totals
     to_left, to_right = folded(left[...], 2), folded(right[...], PITCH - 4)
     for message, up in zip(col_messages, (odd_col, jnp.logical_not(odd_col))):
         message[...] = jnp.where(up, to_right, to_left)
@@ -225,7 +210,7 @@
 ):
     rows, planes, width = by_row.shape
     odd_row, has_below, has_above = sides_of("row")
-    one, other = first_message[...], second_message[: 2 * planes + 8]
+    one, other = first_message[: 2 * planes + 8], second_message[...]
     below = jnp.where(has_below, jnp.where(odd_row, other, one), 0.0)
     above = jnp.where(has_above, jnp.where(odd_row, one, other), 0.0)
     halos = [None, None]
@@ -467,7 +452,7 @@
     by_row, weights_by_row, left, right, *messages = call(
         pack_rows_kernel,
         [f32(rows, planes, width), f32(rows, 8, width), side, side]
-        + [f32(2 * planes + 8, width), f32(2 * planes + 16, width)]
+        + [f32(2 * planes + 16, width), f32(2 * planes + 8, width)]
         + [f32(16, LANES)] * 2,
         pltpu.with_memory_space_constraint(sketch, pltpu.HBM),
         pltpu.with_memory_space_constraint(weights, pltpu.HBM),

time: 25.6 us -> 25.6 us (level)
  waiting for transfers between devices: 0.33 us -> 0.67 us
  blocking collectives: 9.78 us -> 9.45 us
    ppermute x6, waiting for transfers between devices: 0.33 us -> 0.67 us  [swap(): return lax.ppermute(value, names, pairs)]
    all_to_all x1, blocking collectives: 9.78 us -> 9.45 us  [on_device(): parts = lax.all_to_all(grams, ('row', 'col'), 0, 0, tiled=True)]
where the time goes in v4:
time: 25.6 us; the launch traced here: 25.4 us
  blocking collectives  9.45 us (37%)
  starting transfers between devices  8.31 us (32%)
  Pallas kernels  6.29 us (25%)
  between operations  0.68 us (3%)
  waiting for transfers between devices  0.67 us (3%)
    all_to_all x1, blocking collectives, on_device(): parts = lax.all_to_all(grams, ('row', 'col'), 0, 0, tiled=True)  9.45 us
    ppermute x6, starting transfers between devices, swap(): return lax.ppermute(value, names, pairs)  8.31 us
    pallas_call x6, Pallas kernels, call(): pl.pallas_call(kernel, out_shape=out_shapes, in_specs=[pl.BlockSpec(memor...  6.29 us
    ppermute x6, waiting for transfers between devices, swap(): return lax.ppermute(value, names, pairs)  0.67 us
  transfers between devices with their start and end apart: 6, of which 1 were waited for; matrix products, arithmetic and copies ran while one was open for 0% of the time, Pallas kernels for 8%

profile of v4, /device:TPU:0, one launch (start us, length us, event | category | flops | bytes accessed | tf_op | source)
XLA Modules:
  0.0 25.4 jit_solution(2274386399445547328)
XLA Ops:
  0.6 1.4 %shard_map.41 = (f32[8,32,512]{2,1,0:T(8,128)S(1)}, f32[8,8,512]{2,1,0:T(8,128)S(1)}, f32[40,128]{1,0:T(8,128)S(1)}, f32[40,128]{1,0:T(8,128)S(1)}, f32[80,512]{...) custom-call(f32[32,8,512]{2,1,0:T(8,128)} %sketch.1, f32[8,8,512]{2,1,0:T(8,128)} %weights.1), custom_call_target="tpu_custom_call" | custom-call | tf_op jit(solution)/shard_map/pallas_call | solution.py:18
  2.0 3.0 %collective-permute-start = (f32[80,512]{1,0:T(8,128)S(1)}, f32[80,512]{1,0:T(8,128)S(1)}, u32[]{:S(2)}, u32[]{:S(2)}) collective-permute-start(f32[80,512]{1,0:T(8,128)S(1)} %get-tuple-element.27), channel_id=1, source_target_pairs={{0,16},{1,17},{2,18},{3,19},{4,8},{5,9},{6,10},{7,11},{8,4},{9,5},... | collective-permute-start | bytes 491528 | tf_op jit(solution)/shard_map/ppermute | solution.py:445
  5.1 0.1 collective-permute-start.1
  5.2 0.4 %collective-permute-start.2 = (f32[16,128]{1,0:T(8,128)S(1)}, f32[16,128]{1,0:T(8,128)S(1)}, u32[]{:S(2)}, u32[]{:S(2)}) collective-permute-start(f32[16,128]{1,0:T(8,128)S(1)} %get-tuple-element.39), channel_id=1, source_target_pairs={{0,4},{1,17},{2,18},{3,7},{4,0},{5,10},{6,9},{7,3},{8,12},{9,6},{1... | collective-permute-start | bytes 24584 | tf_op jit(solution)/shard_map/ppermute | solution.py:445
  5.6 1.1 %collective-permute-start.3 = (f32[16,128]{1,0:T(8,128)S(1)}, f32[16,128]{1,0:T(8,128)S(1)}, u32[]{:S(2)}, u32[]{:S(2)}) collective-permute-start(f32[16,128]{1,0:T(8,128)S(1)} %get-tuple-element.40), channel_id=1, source_target_pairs={{0,16},{1,17},{2,18},{3,19},{4,9},{5,8},{6,11},{7,10},{8,5},{9,4},... | collective-permute-start | bytes 24584 | tf_op jit(solution)/shard_map/ppermute | solution.py:445
  6.7 0.0 collective-permute-done.1.second_message.bulk_message
  6.7 0.2 shard_map.44
  6.9 2.7 %collective-permute-start.4 = (f32[16,128]{1,0:T(8,128)S(1)}, f32[16,128]{1,0:T(8,128)S(1)}, u32[]{:S(2)}, u32[]{:S(2)}) collective-permute-start(f32[16,128]{1,0:T(8,128)S(1)} %get-tuple-element.41), channel_id=1, source_target_pairs={{0,4},{1,2},{2,1},{3,7},{4,0},{5,6},{6,5},{7,3},{8,12},{9,10},{10,... | collective-permute-start | bytes 24584 | tf_op jit(solution)/shard_map/ppermute | solution.py:445
  9.5 1.0 %collective-permute-start.5 = (f32[16,128]{1,0:T(8,128)S(1)}, f32[16,128]{1,0:T(8,128)S(1)}, u32[]{:S(2)}, u32[]{:S(2)}) collective-permute-start(f32[16,128]{1,0:T(8,128)S(1)} %get-tuple-element.42), channel_id=1, source_target_pairs={{0,1},{1,0},{2,3},{3,2},{4,5},{5,4},{6,7},{7,6},{8,9},{9,8},{10,11... | collective-permute-start | bytes 24584 | tf_op jit(solution)/shard_map/ppermute | solution.py:445
  10.5 1.0 %shard_map.42 = (f32[6,32,512]{2,1,0:T(8,128)S(1)}, bf16[4,96,512]{2,1,0:T(8,128)(2,1)S(1)}, f32[96,96]{1,0:T(8,128)S(1)}, f32[96,96]{1,0:T(8,128)S(1)}) custom-call(f32[8,32,512]{2,1,0:T(8,128)S(1)} %get-tuple-element.24.by_row, f32[8,8,512]{2,1,0:T(8,128)S(1)} %get-tuple-element.25.weights_by_row), custom_call_target="tpu_custom_call" | custom-call | tf_op jit(solution)/shard_map/pallas_call | solution.py:18
  11.6 0.0 collective-permute-done.first_message
  11.6 1.0 %shard_map.43 = (bf16[4,96,512]{2,1,0:T(8,128)(2,1)S(1)}, f32[32,64]{1,0:T(8,128)S(1)}, f32[40,128]{1,0:T(8,128)S(1)}, f32[40,128]{1,0:T(8,128)S(1)}) custom-call(f32[8,32,512]{2,1,0:T(8,128)S(1)} %get-tuple-element.24.by_row, f32[8,8,512]{2,1,0:T(8,128)S(1)} %get-tuple-element.25.weights_by_row, f32[80,512]{1,0:T(8,128)S(1)} %collective-permute-done.first_message, ...), custom_call_target="tpu_custom_call" | custom-call | tf_op jit(solution)/shard_map/pallas_call | solution.py:18
  12.5 0.0 collective-permute-done.2.rest_0_
  12.5 0.0 collective-permute-done.3.rest_1_
  12.5 0.0 collective-permute-done.4.rest_2_
  12.5 0.7 %collective-permute-done.5.rest_3_ = f32[16,128]{1,0:T(8,128)S(1)} collective-permute-done((f32[16,128]{1,0:T(8,128)S(1)}, f32[16,128]{1,0:T(8,128)S(1)}, u32[]{:S(2)}, u32[]{:S(2)}) %collective-permute-start.5) | collective-permute-done | bytes 8224 | tf_op jit(solution)/shard_map/ppermute | solution.py:445
  13.2 0.7 %shard_map.45 = (f32[16,1,1152]{2,1,0:T(1,128)S(1)}, f32[32,256]{1,0:T(8,128)S(1)}) custom-call(f32[40,128]{1,0:T(8,128)S(1)} %get-tuple-element.35.left, f32[40,128]{1,0:T(8,128)S(1)} %get-tuple-element.36.right, f32[40,128]{1,0:T(8,128)S(1)} %get-tuple-element.37.left_halo, f32[40,128]{1,0:T(8,128)S(1)} %get-tuple-element.38.right_halo, ...), custom_call_target="tpu_custom_call" | custom-call | tf_op jit(solution)/shard_map/pallas_call | solution.py:18
  13.9 9.4 %all_to_all.5.parts = f32[16,1,1152]{2,1,0:T(1,128)S(1)} all-to-all(f32[16,1,1152]{2,1,0:T(1,128)S(1)} %get-tuple-element.45), channel_id=1, replica_groups=mesh['sec'=2,'row'=4,'col'=4] {'row','col'}, dimensions={0} | all-to-all | bytes 147456 | tf_op jit(solution)/shard_map/all_to_all | solution.py:500
  23.4 2.0 %shard_map.46 = (f32[32,8,512]{2,1,0:T(8,128)}, f32[32,32]{1,0:T(8,128)}) custom-call(bf16[4,96,512]{2,1,0:T(8,128)(2,1)S(1)} %get-tuple-element.26.inner_second, bf16[4,96,512]{2,1,0:T(8,128)(2,1)S(1)} %get-tuple-element.32.outer_second, f32[32,256]{1,0:T(8,128)S(1)} %get-tuple-element.44.edges, f32[16,1,1152]{2,1,0:T(1,128)S(1)} %all_to_all.5.parts), custom_call_target="tpu_custom_call" | custom-call | tf_op jit(solution)/shard_map/pallas_call | solution.py:18
Async XLA Ops:
  2.0 9.5 %collective-permute-start = (f32[80,512]{1,0:T(8,128)S(1)}, f32[80,512]{1,0:T(8,128)S(1)}, u32[]{:S(2)}, u32[]{:S(2)}) collective-permute-start(f32[80,512]{1,0:T(8,128)S(1)} %get-tuple-element.27), channel_id=1, source_target_pairs={{0,16},{1,17},{2,18},{3,19},{4,8},{5,9},{6,10},{7,11},{8,4},{9,5},... | collective-permute-start | bytes 491528 | tf_op jit(solution)/shard_map/ppermute | solution.py:445
  5.1 1.6 %collective-permute-start.1 = (f32[72,512]{1,0:T(8,128)S(1)}, f32[72,512]{1,0:T(8,128)S(1)}, u32[]{:S(2)}, u32[]{:S(2)}) collective-permute-start(f32[72,512]{1,0:T(8,128)S(1)} %get-tuple-element.28), channel_id=1, source_target_pairs={{0,4},{1,5},{2,6},{3,7},{4,0},{5,1},{6,2},{7,3},{8,12},{9,13},{10,... | collective-permute-start | bytes 442376 | tf_op jit(solution)/shard_map/ppermute | solution.py:445
  5.2 7.4 %collective-permute-start.2 = (f32[16,128]{1,0:T(8,128)S(1)}, f32[16,128]{1,0:T(8,128)S(1)}, u32[]{:S(2)}, u32[]{:S(2)}) collective-permute-start(f32[16,128]{1,0:T(8,128)S(1)} %get-tuple-element.39), channel_id=1, source_target_pairs={{0,4},{1,17},{2,18},{3,7},{4,0},{5,10},{6,9},{7,3},{8,12},{9,6},{1... | collective-permute-start | bytes 24584 | tf_op jit(solution)/shard_map/ppermute | solution.py:445
  5.6 6.9 %collective-permute-start.3 = (f32[16,128]{1,0:T(8,128)S(1)}, f32[16,128]{1,0:T(8,128)S(1)}, u32[]{:S(2)}, u32[]{:S(2)}) collective-permute-start(f32[16,128]{1,0:T(8,128)S(1)} %get-tuple-element.40), channel_id=1, source_target_pairs={{0,16},{1,17},{2,18},{3,19},{4,9},{5,8},{6,11},{7,10},{8,5},{9,4},... | collective-permute-start | bytes 24584 | tf_op jit(solution)/shard_map/ppermute | solution.py:445
  6.9 5.7 %collective-permute-start.4 = (f32[16,128]{1,0:T(8,128)S(1)}, f32[16,128]{1,0:T(8,128)S(1)}, u32[]{:S(2)}, u32[]{:S(2)}) collective-permute-start(f32[16,128]{1,0:T(8,128)S(1)} %get-tuple-element.41), channel_id=1, source_target_pairs={{0,4},{1,2},{2,1},{3,7},{4,0},{5,6},{6,5},{7,3},{8,12},{9,10},{10,... | collective-permute-start | bytes 24584 | tf_op jit(solution)/shard_map/ppermute | solution.py:445
  9.5 3.7 %collective-permute-start.5 = (f32[16,128]{1,0:T(8,128)S(1)}, f32[16,128]{1,0:T(8,128)S(1)}, u32[]{:S(2)}, u32[]{:S(2)}) collective-permute-start(f32[16,128]{1,0:T(8,128)S(1)} %get-tuple-element.42), channel_id=1, source_target_pairs={{0,1},{1,0},{2,3},{3,2},{4,5},{5,4},{6,7},{7,6},{8,9},{9,8},{10,11... | collective-permute-start | bytes 24584 | tf_op jit(solution)/shard_map/ppermute | solution.py:445

commit v5 on v4

--- a/solution.py
+++ b/solution.py
@@ -497,7 +497,9 @@
         *from_cols,
         early_grams,
     )
-    parts = lax.all_to_all(grams, ("row", "col"), 0, 0, tiled=True)
+    first = lax.axis_size("col") + lax.axis_size("col") // 2
+    order = [first] + [place for place in range(group) if place != first]
+    parts = lax.all_to_all(grams, ("row", "col"), 0, 0, axis_index_groups=[order], tiled=True)
     return call(
         functools.partial(finish_kernel, float(rows * width * group)),
         [f32(planes, rows, width), f32(planes, planes)],

time: 25.6 us -> 24.2 us (0.945)
  blocking collectives: 9.45 us -> 8.09 us
    all_to_all x1, blocking collectives: 9.45 us -> 8.09 us  [on_device(): lax.all_to_all(grams, ('row', 'col'), 0, 0, axis_index_groups=[order], ti...]
  transfers between devices with their start and end apart: 6 -> 6, of which waited for: 1 -> 1; matrix products, arithmetic and copies ran while one was open for 0% -> 0% of each run, Pallas kernels for 8% -> 9%
where the time goes in v5:
time: 24.2 us; the launch traced here: 24 us
  starting transfers between devices  8.31 us (34%)
  blocking collectives  8.09 us (33%)
  Pallas kernels  6.29 us (26%)
  between operations  0.68 us (3%)
  waiting for transfers between devices  0.67 us (3%)
    ppermute x6, starting transfers between devices, swap(): return lax.ppermute(value, names, pairs)  8.31 us
    all_to_all x1, blocking collectives, on_device(): lax.all_to_all(grams, ('row', 'col'), 0, 0, axis_index_groups=[order], ti...  8.09 us
    pallas_call x6, Pallas kernels, call(): pl.pallas_call(kernel, out_shape=out_shapes, in_specs=[pl.BlockSpec(memor...  6.29 us
    ppermute x6, waiting for transfers between devices, swap(): return lax.ppermute(value, names, pairs)  0.67 us
  transfers between devices with their start and end apart: 6, of which 1 were waited for; matrix products, arithmetic and copies ran while one was open for 0% of the time, Pallas kernels for 9%

profile of v5, /device:TPU:0, one launch (start us, length us, event | category | flops | bytes accessed | tf_op | source)
XLA Modules:
  0.0 24.0 jit_solution(14784298241140373602)
XLA Ops:
  0.6 1.4 %shard_map.41 = (f32[8,32,512]{2,1,0:T(8,128)S(1)}, f32[8,8,512]{2,1,0:T(8,128)S(1)}, f32[40,128]{1,0:T(8,128)S(1)}, f32[40,128]{1,0:T(8,128)S(1)}, f32[80,512]{...) custom-call(f32[32,8,512]{2,1,0:T(8,128)} %sketch.1, f32[8,8,512]{2,1,0:T(8,128)} %weights.1), custom_call_target="tpu_custom_call" | custom-call | tf_op jit(solution)/shard_map/pallas_call | solution.py:18
  2.0 3.0 %collective-permute-start = (f32[80,512]{1,0:T(8,128)S(1)}, f32[80,512]{1,0:T(8,128)S(1)}, u32[]{:S(2)}, u32[]{:S(2)}) collective-permute-start(f32[80,512]{1,0:T(8,128)S(1)} %get-tuple-element.27), channel_id=1, source_target_pairs={{0,16},{1,17},{2,18},{3,19},{4,8},{5,9},{6,10},{7,11},{8,4},{9,5},... | collective-permute-start | bytes 491528 | tf_op jit(solution)/shard_map/ppermute | solution.py:445
  5.1 0.1 collective-permute-start.1
  5.2 0.4 %collective-permute-start.2 = (f32[16,128]{1,0:T(8,128)S(1)}, f32[16,128]{1,0:T(8,128)S(1)}, u32[]{:S(2)}, u32[]{:S(2)}) collective-permute-start(f32[16,128]{1,0:T(8,128)S(1)} %get-tuple-element.39), channel_id=1, source_target_pairs={{0,4},{1,17},{2,18},{3,7},{4,0},{5,10},{6,9},{7,3},{8,12},{9,6},{1... | collective-permute-start | bytes 24584 | tf_op jit(solution)/shard_map/ppermute | solution.py:445
  5.6 1.1 %collective-permute-start.3 = (f32[16,128]{1,0:T(8,128)S(1)}, f32[16,128]{1,0:T(8,128)S(1)}, u32[]{:S(2)}, u32[]{:S(2)}) collective-permute-start(f32[16,128]{1,0:T(8,128)S(1)} %get-tuple-element.40), channel_id=1, source_target_pairs={{0,16},{1,17},{2,18},{3,19},{4,9},{5,8},{6,11},{7,10},{8,5},{9,4},... | collective-permute-start | bytes 24584 | tf_op jit(solution)/shard_map/ppermute | solution.py:445
  6.7 0.0 collective-permute-done.1.second_message.bulk_message
  6.7 0.2 shard_map.44
  6.9 2.7 %collective-permute-start.4 = (f32[16,128]{1,0:T(8,128)S(1)}, f32[16,128]{1,0:T(8,128)S(1)}, u32[]{:S(2)}, u32[]{:S(2)}) collective-permute-start(f32[16,128]{1,0:T(8,128)S(1)} %get-tuple-element.41), channel_id=1, source_target_pairs={{0,4},{1,2},{2,1},{3,7},{4,0},{5,6},{6,5},{7,3},{8,12},{9,10},{10,... | collective-permute-start | bytes 24584 | tf_op jit(solution)/shard_map/ppermute | solution.py:445
  9.5 1.0 %collective-permute-start.5 = (f32[16,128]{1,0:T(8,128)S(1)}, f32[16,128]{1,0:T(8,128)S(1)}, u32[]{:S(2)}, u32[]{:S(2)}) collective-permute-start(f32[16,128]{1,0:T(8,128)S(1)} %get-tuple-element.42), channel_id=1, source_target_pairs={{0,1},{1,0},{2,3},{3,2},{4,5},{5,4},{6,7},{7,6},{8,9},{9,8},{10,11... | collective-permute-start | bytes 24584 | tf_op jit(solution)/shard_map/ppermute | solution.py:445
  10.5 1.0 %shard_map.42 = (f32[6,32,512]{2,1,0:T(8,128)S(1)}, bf16[4,96,512]{2,1,0:T(8,128)(2,1)S(1)}, f32[96,96]{1,0:T(8,128)S(1)}, f32[96,96]{1,0:T(8,128)S(1)}) custom-call(f32[8,32,512]{2,1,0:T(8,128)S(1)} %get-tuple-element.24.by_row, f32[8,8,512]{2,1,0:T(8,128)S(1)} %get-tuple-element.25.weights_by_row), custom_call_target="tpu_custom_call" | custom-call | tf_op jit(solution)/shard_map/pallas_call | solution.py:18
  11.6 0.0 collective-permute-done.first_message
  11.6 1.0 %shard_map.43 = (bf16[4,96,512]{2,1,0:T(8,128)(2,1)S(1)}, f32[32,64]{1,0:T(8,128)S(1)}, f32[40,128]{1,0:T(8,128)S(1)}, f32[40,128]{1,0:T(8,128)S(1)}) custom-call(f32[8,32,512]{2,1,0:T(8,128)S(1)} %get-tuple-element.24.by_row, f32[8,8,512]{2,1,0:T(8,128)S(1)} %get-tuple-element.25.weights_by_row, f32[80,512]{1,0:T(8,128)S(1)} %collective-permute-done.first_message, ...), custom_call_target="tpu_custom_call" | custom-call | tf_op jit(solution)/shard_map/pallas_call | solution.py:18
  12.5 0.0 collective-permute-done.2.rest_0_
  12.5 0.0 collective-permute-done.3.rest_1_
  12.5 0.0 collective-permute-done.4.rest_2_
  12.5 0.7 %collective-permute-done.5.rest_3_ = f32[16,128]{1,0:T(8,128)S(1)} collective-permute-done((f32[16,128]{1,0:T(8,128)S(1)}, f32[16,128]{1,0:T(8,128)S(1)}, u32[]{:S(2)}, u32[]{:S(2)}) %collective-permute-start.5) | collective-permute-done | bytes 8224 | tf_op jit(solution)/shard_map/ppermute | solution.py:445
  13.2 0.7 %shard_map.45 = (f32[16,1,1152]{2,1,0:T(1,128)S(1)}, f32[32,256]{1,0:T(8,128)S(1)}) custom-call(f32[40,128]{1,0:T(8,128)S(1)} %get-tuple-element.35.left, f32[40,128]{1,0:T(8,128)S(1)} %get-tuple-element.36.right, f32[40,128]{1,0:T(8,128)S(1)} %get-tuple-element.37.left_halo, f32[40,128]{1,0:T(8,128)S(1)} %get-tuple-element.38.right_halo, ...), custom_call_target="tpu_custom_call" | custom-call | tf_op jit(solution)/shard_map/pallas_call | solution.py:18
  13.9 8.1 %all_to_all.5.parts = f32[16,1,1152]{2,1,0:T(1,128)S(1)} all-to-all(f32[16,1,1152]{2,1,0:T(1,128)S(1)} %get-tuple-element.45), channel_id=1, replica_groups={{6,0,1,2,3,4,5,7,8,9,10,11,12,13,14,15},{22,16,17,18,19,20,21,23,24,25,..., dimensions={0} | all-to-all | bytes 147456 | tf_op jit(solution)/shard_map/all_to_all | solution.py:502
  22.0 2.0 %shard_map.46 = (f32[32,8,512]{2,1,0:T(8,128)}, f32[32,32]{1,0:T(8,128)}) custom-call(bf16[4,96,512]{2,1,0:T(8,128)(2,1)S(1)} %get-tuple-element.26.inner_second, bf16[4,96,512]{2,1,0:T(8,128)(2,1)S(1)} %get-tuple-element.32.outer_second, f32[32,256]{1,0:T(8,128)S(1)} %get-tuple-element.44.edges, f32[16,1,1152]{2,1,0:T(1,128)S(1)} %all_to_all.5.parts), custom_call_target="tpu_custom_call" | custom-call | tf_op jit(solution)/shard_map/pallas_call | solution.py:18
Async XLA Ops:
  2.0 9.5 %collective-permute-start = (f32[80,512]{1,0:T(8,128)S(1)}, f32[80,512]{1,0:T(8,128)S(1)}, u32[]{:S(2)}, u32[]{:S(2)}) collective-permute-start(f32[80,512]{1,0:T(8,128)S(1)} %get-tuple-element.27), channel_id=1, source_target_pairs={{0,16},{1,17},{2,18},{3,19},{4,8},{5,9},{6,10},{7,11},{8,4},{9,5},... | collective-permute-start | bytes 491528 | tf_op jit(solution)/shard_map/ppermute | solution.py:445
  5.1 1.6 %collective-permute-start.1 = (f32[72,512]{1,0:T(8,128)S(1)}, f32[72,512]{1,0:T(8,128)S(1)}, u32[]{:S(2)}, u32[]{:S(2)}) collective-permute-start(f32[72,512]{1,0:T(8,128)S(1)} %get-tuple-element.28), channel_id=1, source_target_pairs={{0,4},{1,5},{2,6},{3,7},{4,0},{5,1},{6,2},{7,3},{8,12},{9,13},{10,... | collective-permute-start | bytes 442376 | tf_op jit(solution)/shard_map/ppermute | solution.py:445
  5.2 7.4 %collective-permute-start.2 = (f32[16,128]{1,0:T(8,128)S(1)}, f32[16,128]{1,0:T(8,128)S(1)}, u32[]{:S(2)}, u32[]{:S(2)}) collective-permute-start(f32[16,128]{1,0:T(8,128)S(1)} %get-tuple-element.39), channel_id=1, source_target_pairs={{0,4},{1,17},{2,18},{3,7},{4,0},{5,10},{6,9},{7,3},{8,12},{9,6},{1... | collective-permute-start | bytes 24584 | tf_op jit(solution)/shard_map/ppermute | solution.py:445
  5.6 6.9 %collective-permute-start.3 = (f32[16,128]{1,0:T(8,128)S(1)}, f32[16,128]{1,0:T(8,128)S(1)}, u32[]{:S(2)}, u32[]{:S(2)}) collective-permute-start(f32[16,128]{1,0:T(8,128)S(1)} %get-tuple-element.40), channel_id=1, source_target_pairs={{0,16},{1,17},{2,18},{3,19},{4,9},{5,8},{6,11},{7,10},{8,5},{9,4},... | collective-permute-start | bytes 24584 | tf_op jit(solution)/shard_map/ppermute | solution.py:445
  6.9 5.7 %collective-permute-start.4 = (f32[16,128]{1,0:T(8,128)S(1)}, f32[16,128]{1,0:T(8,128)S(1)}, u32[]{:S(2)}, u32[]{:S(2)}) collective-permute-start(f32[16,128]{1,0:T(8,128)S(1)} %get-tuple-element.41), channel_id=1, source_target_pairs={{0,4},{1,2},{2,1},{3,7},{4,0},{5,6},{6,5},{7,3},{8,12},{9,10},{10,... | collective-permute-start | bytes 24584 | tf_op jit(solution)/shard_map/ppermute | solution.py:445
  9.5 3.7 %collective-permute-start.5 = (f32[16,128]{1,0:T(8,128)S(1)}, f32[16,128]{1,0:T(8,128)S(1)}, u32[]{:S(2)}, u32[]{:S(2)}) collective-permute-start(f32[16,128]{1,0:T(8,128)S(1)} %get-tuple-element.42), channel_id=1, source_target_pairs={{0,1},{1,0},{2,3},{3,2},{4,5},{5,4},{6,7},{7,6},{8,9},{9,8},{10,11... | collective-permute-start | bytes 24584 | tf_op jit(solution)/shard_map/ppermute | solution.py:445

commit v6 on v5

--- a/solution.py
+++ b/solution.py
@@ -497,8 +497,10 @@
         *from_cols,
         early_grams,
     )
-    first = lax.axis_size("col") + lax.axis_size("col") // 2
-    order = [first] + [place for place in range(group) if place != first]
+    rows_of, cols_of = lax.axis_size("row"), lax.axis_size("col")
+    first = 2 * cols_of - 1
+    order = [first] + [row * cols_of + col for col in range(cols_of) for row in range(rows_of)]
+    order = list(dict.fromkeys(order))
     parts = lax.all_to_all(grams, ("row", "col"), 0, 0, axis_index_groups=[order], tiled=True)
     return call(
         functools.partial(finish_kernel, float(rows * width * group)),

time: 24.2 us -> 24.4 us (level)
  no operation moved by 1% of the time
where the time goes in v6:
time: 24.4 us; the launch traced here: 24.3 us
  blocking collectives  8.32 us (34%)
  starting transfers between devices  8.31 us (34%)
  Pallas kernels  6.29 us (26%)
  between operations  0.68 us (3%)
  waiting for transfers between devices  0.67 us (3%)
    all_to_all x1, blocking collectives, on_device(): lax.all_to_all(grams, ('row', 'col'), 0, 0, axis_index_groups=[order], ti...  8.32 us
    ppermute x6, starting transfers between devices, swap(): return lax.ppermute(value, names, pairs)  8.31 us
    pallas_call x6, Pallas kernels, call(): pl.pallas_call(kernel, out_shape=out_shapes, in_specs=[pl.BlockSpec(memor...  6.29 us
    ppermute x6, waiting for transfers between devices, swap(): return lax.ppermute(value, names, pairs)  0.67 us
  transfers between devices with their start and end apart: 6, of which 1 were waited for; matrix products, arithmetic and copies ran while one was open for 0% of the time, Pallas kernels for 9%

profile of v6, /device:TPU:0, one launch (start us, length us, event | category | flops | bytes accessed | tf_op | source)
XLA Modules:
  0.0 24.3 jit_solution(11280100474710315793)
XLA Ops:
  0.6 1.4 %shard_map.41 = (f32[8,32,512]{2,1,0:T(8,128)S(1)}, f32[8,8,512]{2,1,0:T(8,128)S(1)}, f32[40,128]{1,0:T(8,128)S(1)}, f32[40,128]{1,0:T(8,128)S(1)}, f32[80,512]{...) custom-call(f32[32,8,512]{2,1,0:T(8,128)} %sketch.1, f32[8,8,512]{2,1,0:T(8,128)} %weights.1), custom_call_target="tpu_custom_call" | custom-call | tf_op jit(solution)/shard_map/pallas_call | solution.py:18
  2.0 3.0 %collective-permute-start = (f32[80,512]{1,0:T(8,128)S(1)}, f32[80,512]{1,0:T(8,128)S(1)}, u32[]{:S(2)}, u32[]{:S(2)}) collective-permute-start(f32[80,512]{1,0:T(8,128)S(1)} %get-tuple-element.27), channel_id=1, source_target_pairs={{0,16},{1,17},{2,18},{3,19},{4,8},{5,9},{6,10},{7,11},{8,4},{9,5},... | collective-permute-start | bytes 491528 | tf_op jit(solution)/shard_map/ppermute | solution.py:445
  5.1 0.1 collective-permute-start.1
  5.2 0.4 %collective-permute-start.2 = (f32[16,128]{1,0:T(8,128)S(1)}, f32[16,128]{1,0:T(8,128)S(1)}, u32[]{:S(2)}, u32[]{:S(2)}) collective-permute-start(f32[16,128]{1,0:T(8,128)S(1)} %get-tuple-element.39), channel_id=1, source_target_pairs={{0,4},{1,17},{2,18},{3,7},{4,0},{5,10},{6,9},{7,3},{8,12},{9,6},{1... | collective-permute-start | bytes 24584 | tf_op jit(solution)/shard_map/ppermute | solution.py:445
  5.6 1.1 %collective-permute-start.3 = (f32[16,128]{1,0:T(8,128)S(1)}, f32[16,128]{1,0:T(8,128)S(1)}, u32[]{:S(2)}, u32[]{:S(2)}) collective-permute-start(f32[16,128]{1,0:T(8,128)S(1)} %get-tuple-element.40), channel_id=1, source_target_pairs={{0,16},{1,17},{2,18},{3,19},{4,9},{5,8},{6,11},{7,10},{8,5},{9,4},... | collective-permute-start | bytes 24584 | tf_op jit(solution)/shard_map/ppermute | solution.py:445
  6.7 0.0 collective-permute-done.1.second_message.bulk_message
  6.7 0.2 shard_map.44
  6.9 2.7 %collective-permute-start.4 = (f32[16,128]{1,0:T(8,128)S(1)}, f32[16,128]{1,0:T(8,128)S(1)}, u32[]{:S(2)}, u32[]{:S(2)}) collective-permute-start(f32[16,128]{1,0:T(8,128)S(1)} %get-tuple-element.41), channel_id=1, source_target_pairs={{0,4},{1,2},{2,1},{3,7},{4,0},{5,6},{6,5},{7,3},{8,12},{9,10},{10,... | collective-permute-start | bytes 24584 | tf_op jit(solution)/shard_map/ppermute | solution.py:445
  9.5 1.0 %collective-permute-start.5 = (f32[16,128]{1,0:T(8,128)S(1)}, f32[16,128]{1,0:T(8,128)S(1)}, u32[]{:S(2)}, u32[]{:S(2)}) collective-permute-start(f32[16,128]{1,0:T(8,128)S(1)} %get-tuple-element.42), channel_id=1, source_target_pairs={{0,1},{1,0},{2,3},{3,2},{4,5},{5,4},{6,7},{7,6},{8,9},{9,8},{10,11... | collective-permute-start | bytes 24584 | tf_op jit(solution)/shard_map/ppermute | solution.py:445
  10.5 1.0 %shard_map.42 = (f32[6,32,512]{2,1,0:T(8,128)S(1)}, bf16[4,96,512]{2,1,0:T(8,128)(2,1)S(1)}, f32[96,96]{1,0:T(8,128)S(1)}, f32[96,96]{1,0:T(8,128)S(1)}) custom-call(f32[8,32,512]{2,1,0:T(8,128)S(1)} %get-tuple-element.24.by_row, f32[8,8,512]{2,1,0:T(8,128)S(1)} %get-tuple-element.25.weights_by_row), custom_call_target="tpu_custom_call" | custom-call | tf_op jit(solution)/shard_map/pallas_call | solution.py:18
  11.6 0.0 collective-permute-done.first_message
  11.6 1.0 %shard_map.43 = (bf16[4,96,512]{2,1,0:T(8,128)(2,1)S(1)}, f32[32,64]{1,0:T(8,128)S(1)}, f32[40,128]{1,0:T(8,128)S(1)}, f32[40,128]{1,0:T(8,128)S(1)}) custom-call(f32[8,32,512]{2,1,0:T(8,128)S(1)} %get-tuple-element.24.by_row, f32[8,8,512]{2,1,0:T(8,128)S(1)} %get-tuple-element.25.weights_by_row, f32[80,512]{1,0:T(8,128)S(1)} %collective-permute-done.first_message, ...), custom_call_target="tpu_custom_call" | custom-call | tf_op jit(solution)/shard_map/pallas_call | solution.py:18
  12.5 0.0 collective-permute-done.2.rest_0_
  12.5 0.0 collective-permute-done.3.rest_1_
  12.5 0.0 collective-permute-done.4.rest_2_
  12.5 0.7 %collective-permute-done.5.rest_3_ = f32[16,128]{1,0:T(8,128)S(1)} collective-permute-done((f32[16,128]{1,0:T(8,128)S(1)}, f32[16,128]{1,0:T(8,128)S(1)}, u32[]{:S(2)}, u32[]{:S(2)}) %collective-permute-start.5) | collective-permute-done | bytes 8224 | tf_op jit(solution)/shard_map/ppermute | solution.py:445
  13.2 0.7 %shard_map.45 = (f32[16,1,1152]{2,1,0:T(1,128)S(1)}, f32[32,256]{1,0:T(8,128)S(1)}) custom-call(f32[40,128]{1,0:T(8,128)S(1)} %get-tuple-element.35.left, f32[40,128]{1,0:T(8,128)S(1)} %get-tuple-element.36.right, f32[40,128]{1,0:T(8,128)S(1)} %get-tuple-element.37.left_halo, f32[40,128]{1,0:T(8,128)S(1)} %get-tuple-element.38.right_halo, ...), custom_call_target="tpu_custom_call" | custom-call | tf_op jit(solution)/shard_map/pallas_call | solution.py:18
  13.9 8.3 %all_to_all.5.parts = f32[16,1,1152]{2,1,0:T(1,128)S(1)} all-to-all(f32[16,1,1152]{2,1,0:T(1,128)S(1)} %get-tuple-element.45), channel_id=1, replica_groups={{7,0,4,8,12,1,5,9,13,2,6,10,14,3,11,15},{23,16,20,24,28,17,21,25,29,18,..., dimensions={0} | all-to-all | bytes 147456 | tf_op jit(solution)/shard_map/all_to_all | solution.py:504
  22.2 2.0 %shard_map.46 = (f32[32,8,512]{2,1,0:T(8,128)}, f32[32,32]{1,0:T(8,128)}) custom-call(bf16[4,96,512]{2,1,0:T(8,128)(2,1)S(1)} %get-tuple-element.26.inner_second, bf16[4,96,512]{2,1,0:T(8,128)(2,1)S(1)} %get-tuple-element.32.outer_second, f32[32,256]{1,0:T(8,128)S(1)} %get-tuple-element.44.edges, f32[16,1,1152]{2,1,0:T(1,128)S(1)} %all_to_all.5.parts), custom_call_target="tpu_custom_call" | custom-call | tf_op jit(solution)/shard_map/pallas_call | solution.py:18
Async XLA Ops:
  2.0 9.5 %collective-permute-start = (f32[80,512]{1,0:T(8,128)S(1)}, f32[80,512]{1,0:T(8,128)S(1)}, u32[]{:S(2)}, u32[]{:S(2)}) collective-permute-start(f32[80,512]{1,0:T(8,128)S(1)} %get-tuple-element.27), channel_id=1, source_target_pairs={{0,16},{1,17},{2,18},{3,19},{4,8},{5,9},{6,10},{7,11},{8,4},{9,5},... | collective-permute-start | bytes 491528 | tf_op jit(solution)/shard_map/ppermute | solution.py:445
  5.1 1.6 %collective-permute-start.1 = (f32[72,512]{1,0:T(8,128)S(1)}, f32[72,512]{1,0:T(8,128)S(1)}, u32[]{:S(2)}, u32[]{:S(2)}) collective-permute-start(f32[72,512]{1,0:T(8,128)S(1)} %get-tuple-element.28), channel_id=1, source_target_pairs={{0,4},{1,5},{2,6},{3,7},{4,0},{5,1},{6,2},{7,3},{8,12},{9,13},{10,... | collective-permute-start | bytes 442376 | tf_op jit(solution)/shard_map/ppermute | solution.py:445
  5.2 7.4 %collective-permute-start.2 = (f32[16,128]{1,0:T(8,128)S(1)}, f32[16,128]{1,0:T(8,128)S(1)}, u32[]{:S(2)}, u32[]{:S(2)}) collective-permute-start(f32[16,128]{1,0:T(8,128)S(1)} %get-tuple-element.39), channel_id=1, source_target_pairs={{0,4},{1,17},{2,18},{3,7},{4,0},{5,10},{6,9},{7,3},{8,12},{9,6},{1... | collective-permute-start | bytes 24584 | tf_op jit(solution)/shard_map/ppermute | solution.py:445
  5.6 6.9 %collective-permute-start.3 = (f32[16,128]{1,0:T(8,128)S(1)}, f32[16,128]{1,0:T(8,128)S(1)}, u32[]{:S(2)}, u32[]{:S(2)}) collective-permute-start(f32[16,128]{1,0:T(8,128)S(1)} %get-tuple-element.40), channel_id=1, source_target_pairs={{0,16},{1,17},{2,18},{3,19},{4,9},{5,8},{6,11},{7,10},{8,5},{9,4},... | collective-permute-start | bytes 24584 | tf_op jit(solution)/shard_map/ppermute | solution.py:445
  6.9 5.7 %collective-permute-start.4 = (f32[16,128]{1,0:T(8,128)S(1)}, f32[16,128]{1,0:T(8,128)S(1)}, u32[]{:S(2)}, u32[]{:S(2)}) collective-permute-start(f32[16,128]{1,0:T(8,128)S(1)} %get-tuple-element.41), channel_id=1, source_target_pairs={{0,4},{1,2},{2,1},{3,7},{4,0},{5,6},{6,5},{7,3},{8,12},{9,10},{10,... | collective-permute-start | bytes 24584 | tf_op jit(solution)/shard_map/ppermute | solution.py:445
  9.5 3.7 %collective-permute-start.5 = (f32[16,128]{1,0:T(8,128)S(1)}, f32[16,128]{1,0:T(8,128)S(1)}, u32[]{:S(2)}, u32[]{:S(2)}) collective-permute-start(f32[16,128]{1,0:T(8,128)S(1)} %get-tuple-element.42), channel_id=1, source_target_pairs={{0,1},{1,0},{2,3},{3,2},{4,5},{5,4},{6,7},{7,6},{8,9},{9,8},{10,11... | collective-permute-start | bytes 24584 | tf_op jit(solution)/shard_map/ppermute | solution.py:445

commit v7 on v6

--- a/solution.py
+++ b/solution.py
@@ -498,7 +498,7 @@
         early_grams,
     )
     rows_of, cols_of = lax.axis_size("row"), lax.axis_size("col")
-    first = 2 * cols_of - 1
+    first = cols_of + cols_of // 2
     order = [first] + [row * cols_of + col for col in range(cols_of) for row in range(rows_of)]
     order = list(dict.fromkeys(order))
     parts = lax.all_to_all(grams, ("row", "col"), 0, 0, axis_index_groups=[order], tiled=True)

time: 24.4 us -> 24.4 us (level)
  no operation moved by 1% of the time
where the time goes in v7:
time: 24.4 us; the launch traced here: 24.2 us
  starting transfers between devices  8.31 us (34%)
  blocking collectives  8.27 us (34%)
  Pallas kernels  6.29 us (26%)
  between operations  0.68 us (3%)
  waiting for transfers between devices  0.67 us (3%)
    ppermute x6, starting transfers between devices, swap(): return lax.ppermute(value, names, pairs)  8.31 us
    all_to_all x1, blocking collectives, on_device(): lax.all_to_all(grams, ('row', 'col'), 0, 0, axis_index_groups=[order], ti...  8.27 us
    pallas_call x6, Pallas kernels, call(): pl.pallas_call(kernel, out_shape=out_shapes, in_specs=[pl.BlockSpec(memor...  6.29 us
    ppermute x6, waiting for transfers between devices, swap(): return lax.ppermute(value, names, pairs)  0.67 us
  transfers between devices with their start and end apart: 6, of which 1 were waited for; matrix products, arithmetic and copies ran while one was open for 0% of the time, Pallas kernels for 9%

profile of v7, /device:TPU:0, one launch (start us, length us, event | category | flops | bytes accessed | tf_op | source)
XLA Modules:
  0.0 24.2 jit_solution(3810898668078308245)
XLA Ops:
  0.6 1.4 %shard_map.41 = (f32[8,32,512]{2,1,0:T(8,128)S(1)}, f32[8,8,512]{2,1,0:T(8,128)S(1)}, f32[40,128]{1,0:T(8,128)S(1)}, f32[40,128]{1,0:T(8,128)S(1)}, f32[80,512]{...) custom-call(f32[32,8,512]{2,1,0:T(8,128)} %sketch.1, f32[8,8,512]{2,1,0:T(8,128)} %weights.1), custom_call_target="tpu_custom_call" | custom-call | tf_op jit(solution)/shard_map/pallas_call | solution.py:18
  2.0 3.0 %collective-permute-start = (f32[80,512]{1,0:T(8,128)S(1)}, f32[80,512]{1,0:T(8,128)S(1)}, u32[]{:S(2)}, u32[]{:S(2)}) collective-permute-start(f32[80,512]{1,0:T(8,128)S(1)} %get-tuple-element.27), channel_id=1, source_target_pairs={{0,16},{1,17},{2,18},{3,19},{4,8},{5,9},{6,10},{7,11},{8,4},{9,5},... | collective-permute-start | bytes 491528 | tf_op jit(solution)/shard_map/ppermute | solution.py:445
  5.1 0.1 collective-permute-start.1
  5.2 0.4 %collective-permute-start.2 = (f32[16,128]{1,0:T(8,128)S(1)}, f32[16,128]{1,0:T(8,128)S(1)}, u32[]{:S(2)}, u32[]{:S(2)}) collective-permute-start(f32[16,128]{1,0:T(8,128)S(1)} %get-tuple-element.39), channel_id=1, source_target_pairs={{0,4},{1,17},{2,18},{3,7},{4,0},{5,10},{6,9},{7,3},{8,12},{9,6},{1... | collective-permute-start | bytes 24584 | tf_op jit(solution)/shard_map/ppermute | solution.py:445
  5.6 1.1 %collective-permute-start.3 = (f32[16,128]{1,0:T(8,128)S(1)}, f32[16,128]{1,0:T(8,128)S(1)}, u32[]{:S(2)}, u32[]{:S(2)}) collective-permute-start(f32[16,128]{1,0:T(8,128)S(1)} %get-tuple-element.40), channel_id=1, source_target_pairs={{0,16},{1,17},{2,18},{3,19},{4,9},{5,8},{6,11},{7,10},{8,5},{9,4},... | collective-permute-start | bytes 24584 | tf_op jit(solution)/shard_map/ppermute | solution.py:445
  6.7 0.0 collective-permute-done.1.second_message.bulk_message
  6.7 0.2 shard_map.44
  6.9 2.7 %collective-permute-start.4 = (f32[16,128]{1,0:T(8,128)S(1)}, f32[16,128]{1,0:T(8,128)S(1)}, u32[]{:S(2)}, u32[]{:S(2)}) collective-permute-start(f32[16,128]{1,0:T(8,128)S(1)} %get-tuple-element.41), channel_id=1, source_target_pairs={{0,4},{1,2},{2,1},{3,7},{4,0},{5,6},{6,5},{7,3},{8,12},{9,10},{10,... | collective-permute-start | bytes 24584 | tf_op jit(solution)/shard_map/ppermute | solution.py:445
  9.5 1.0 %collective-permute-start.5 = (f32[16,128]{1,0:T(8,128)S(1)}, f32[16,128]{1,0:T(8,128)S(1)}, u32[]{:S(2)}, u32[]{:S(2)}) collective-permute-start(f32[16,128]{1,0:T(8,128)S(1)} %get-tuple-element.42), channel_id=1, source_target_pairs={{0,1},{1,0},{2,3},{3,2},{4,5},{5,4},{6,7},{7,6},{8,9},{9,8},{10,11... | collective-permute-start | bytes 24584 | tf_op jit(solution)/shard_map/ppermute | solution.py:445
  10.5 1.0 %shard_map.42 = (f32[6,32,512]{2,1,0:T(8,128)S(1)}, bf16[4,96,512]{2,1,0:T(8,128)(2,1)S(1)}, f32[96,96]{1,0:T(8,128)S(1)}, f32[96,96]{1,0:T(8,128)S(1)}) custom-call(f32[8,32,512]{2,1,0:T(8,128)S(1)} %get-tuple-element.24.by_row, f32[8,8,512]{2,1,0:T(8,128)S(1)} %get-tuple-element.25.weights_by_row), custom_call_target="tpu_custom_call" | custom-call | tf_op jit(solution)/shard_map/pallas_call | solution.py:18
  11.6 0.0 collective-permute-done.first_message
  11.6 1.0 %shard_map.43 = (bf16[4,96,512]{2,1,0:T(8,128)(2,1)S(1)}, f32[32,64]{1,0:T(8,128)S(1)}, f32[40,128]{1,0:T(8,128)S(1)}, f32[40,128]{1,0:T(8,128)S(1)}) custom-call(f32[8,32,512]{2,1,0:T(8,128)S(1)} %get-tuple-element.24.by_row, f32[8,8,512]{2,1,0:T(8,128)S(1)} %get-tuple-element.25.weights_by_row, f32[80,512]{1,0:T(8,128)S(1)} %collective-permute-done.first_message, ...), custom_call_target="tpu_custom_call" | custom-call | tf_op jit(solution)/shard_map/pallas_call | solution.py:18
  12.5 0.0 collective-permute-done.2.rest_0_
  12.5 0.0 collective-permute-done.3.rest_1_
  12.5 0.0 collective-permute-done.4.rest_2_
  12.5 0.7 %collective-permute-done.5.rest_3_ = f32[16,128]{1,0:T(8,128)S(1)} collective-permute-done((f32[16,128]{1,0:T(8,128)S(1)}, f32[16,128]{1,0:T(8,128)S(1)}, u32[]{:S(2)}, u32[]{:S(2)}) %collective-permute-start.5) | collective-permute-done | bytes 8224 | tf_op jit(solution)/shard_map/ppermute | solution.py:445
  13.2 0.7 %shard_map.45 = (f32[16,1,1152]{2,1,0:T(1,128)S(1)}, f32[32,256]{1,0:T(8,128)S(1)}) custom-call(f32[40,128]{1,0:T(8,128)S(1)} %get-tuple-element.35.left, f32[40,128]{1,0:T(8,128)S(1)} %get-tuple-element.36.right, f32[40,128]{1,0:T(8,128)S(1)} %get-tuple-element.37.left_halo, f32[40,128]{1,0:T(8,128)S(1)} %get-tuple-element.38.right_halo, ...), custom_call_target="tpu_custom_call" | custom-call | tf_op jit(solution)/shard_map/pallas_call | solution.py:18
  13.9 8.3 %all_to_all.5.parts = f32[16,1,1152]{2,1,0:T(1,128)S(1)} all-to-all(f32[16,1,1152]{2,1,0:T(1,128)S(1)} %get-tuple-element.45), channel_id=1, replica_groups={{6,0,4,8,12,1,5,9,13,2,10,14,3,7,11,15},{22,16,20,24,28,17,21,25,29,18,..., dimensions={0} | all-to-all | bytes 147456 | tf_op jit(solution)/shard_map/all_to_all | solution.py:504
  22.2 2.0 %shard_map.46 = (f32[32,8,512]{2,1,0:T(8,128)}, f32[32,32]{1,0:T(8,128)}) custom-call(bf16[4,96,512]{2,1,0:T(8,128)(2,1)S(1)} %get-tuple-element.26.inner_second, bf16[4,96,512]{2,1,0:T(8,128)(2,1)S(1)} %get-tuple-element.32.outer_second, f32[32,256]{1,0:T(8,128)S(1)} %get-tuple-element.44.edges, f32[16,1,1152]{2,1,0:T(1,128)S(1)} %all_to_all.5.parts), custom_call_target="tpu_custom_call" | custom-call | tf_op jit(solution)/shard_map/pallas_call | solution.py:18
Async XLA Ops:
  2.0 9.5 %collective-permute-start = (f32[80,512]{1,0:T(8,128)S(1)}, f32[80,512]{1,0:T(8,128)S(1)}, u32[]{:S(2)}, u32[]{:S(2)}) collective-permute-start(f32[80,512]{1,0:T(8,128)S(1)} %get-tuple-element.27), channel_id=1, source_target_pairs={{0,16},{1,17},{2,18},{3,19},{4,8},{5,9},{6,10},{7,11},{8,4},{9,5},... | collective-permute-start | bytes 491528 | tf_op jit(solution)/shard_map/ppermute | solution.py:445
  5.1 1.6 %collective-permute-start.1 = (f32[72,512]{1,0:T(8,128)S(1)}, f32[72,512]{1,0:T(8,128)S(1)}, u32[]{:S(2)}, u32[]{:S(2)}) collective-permute-start(f32[72,512]{1,0:T(8,128)S(1)} %get-tuple-element.28), channel_id=1, source_target_pairs={{0,4},{1,5},{2,6},{3,7},{4,0},{5,1},{6,2},{7,3},{8,12},{9,13},{10,... | collective-permute-start | bytes 442376 | tf_op jit(solution)/shard_map/ppermute | solution.py:445
  5.2 7.4 %collective-permute-start.2 = (f32[16,128]{1,0:T(8,128)S(1)}, f32[16,128]{1,0:T(8,128)S(1)}, u32[]{:S(2)}, u32[]{:S(2)}) collective-permute-start(f32[16,128]{1,0:T(8,128)S(1)} %get-tuple-element.39), channel_id=1, source_target_pairs={{0,4},{1,17},{2,18},{3,7},{4,0},{5,10},{6,9},{7,3},{8,12},{9,6},{1... | collective-permute-start | bytes 24584 | tf_op jit(solution)/shard_map/ppermute | solution.py:445
  5.6 6.9 %collective-permute-start.3 = (f32[16,128]{1,0:T(8,128)S(1)}, f32[16,128]{1,0:T(8,128)S(1)}, u32[]{:S(2)}, u32[]{:S(2)}) collective-permute-start(f32[16,128]{1,0:T(8,128)S(1)} %get-tuple-element.40), channel_id=1, source_target_pairs={{0,16},{1,17},{2,18},{3,19},{4,9},{5,8},{6,11},{7,10},{8,5},{9,4},... | collective-permute-start | bytes 24584 | tf_op jit(solution)/shard_map/ppermute | solution.py:445
  6.9 5.7 %collective-permute-start.4 = (f32[16,128]{1,0:T(8,128)S(1)}, f32[16,128]{1,0:T(8,128)S(1)}, u32[]{:S(2)}, u32[]{:S(2)}) collective-permute-start(f32[16,128]{1,0:T(8,128)S(1)} %get-tuple-element.41), channel_id=1, source_target_pairs={{0,4},{1,2},{2,1},{3,7},{4,0},{5,6},{6,5},{7,3},{8,12},{9,10},{10,... | collective-permute-start | bytes 24584 | tf_op jit(solution)/shard_map/ppermute | solution.py:445
  9.5 3.7 %collective-permute-start.5 = (f32[16,128]{1,0:T(8,128)S(1)}, f32[16,128]{1,0:T(8,128)S(1)}, u32[]{:S(2)}, u32[]{:S(2)}) collective-permute-start(f32[16,128]{1,0:T(8,128)S(1)} %get-tuple-element.42), channel_id=1, source_target_pairs={{0,1},{1,0},{2,3},{3,2},{4,5},{5,4},{6,7},{7,6},{8,9},{9,8},{10,11... | collective-permute-start | bytes 24584 | tf_op jit(solution)/shard_map/ppermute | solution.py:445

commit v8 on v7

--- a/solution.py
+++ b/solution.py
@@ -498,9 +498,9 @@
         early_grams,
     )
     rows_of, cols_of = lax.axis_size("row"), lax.axis_size("col")
-    first = cols_of + cols_of // 2
-    order = [first] + [row * cols_of + col for col in range(cols_of) for row in range(rows_of)]
-    order = list(dict.fromkeys(order))
+    places = [(col > 0, col > 0 and row % 2 == 0, col, row) for col in range(cols_of) for row in range(rows_of)]
+    order = [row * cols_of + col for _, _, col, row in sorted(places)]
+    order = list(dict.fromkeys([cols_of + cols_of // 2] + order))
     parts = lax.all_to_all(grams, ("row", "col"), 0, 0, axis_index_groups=[order], tiled=True)
     return call(
         functools.partial(finish_kernel, float(rows * width * group)),

time: 24.4 us -> 24.7 us (1.012)
  blocking collectives: 8.27 us -> 8.54 us
    all_to_all x1, blocking collectives: 8.27 us -> 8.54 us  [on_device(): lax.all_to_all(grams, ('row', 'col'), 0, 0, axis_index_groups=[order], ti...]
where the time goes in v8:
time: 24.7 us; the launch traced here: 24.5 us
  blocking collectives  8.54 us (35%)
  starting transfers between devices  8.31 us (34%)
  Pallas kernels  6.29 us (25%)
  between operations  0.68 us (3%)
  waiting for transfers between devices  0.67 us (3%)
    all_to_all x1, blocking collectives, on_device(): lax.all_to_all(grams, ('row', 'col'), 0, 0, axis_index_groups=[order], ti...  8.54 us
    ppermute x6, starting transfers between devices, swap(): return lax.ppermute(value, names, pairs)  8.31 us
    pallas_call x6, Pallas kernels, call(): pl.pallas_call(kernel, out_shape=out_shapes, in_specs=[pl.BlockSpec(memor...  6.29 us
    ppermute x6, waiting for transfers between devices, swap(): return lax.ppermute(value, names, pairs)  0.67 us
  transfers between devices with their start and end apart: 6, of which 1 were waited for; matrix products, arithmetic and copies ran while one was open for 0% of the time, Pallas kernels for 9%

profile of v8, /device:TPU:0, one launch (start us, length us, event | category | flops | bytes accessed | tf_op | source)
XLA Modules:
  0.0 24.5 jit_solution(17746039241236575834)
XLA Ops:
  0.6 1.4 %shard_map.41 = (f32[8,32,512]{2,1,0:T(8,128)S(1)}, f32[8,8,512]{2,1,0:T(8,128)S(1)}, f32[40,128]{1,0:T(8,128)S(1)}, f32[40,128]{1,0:T(8,128)S(1)}, f32[80,512]{...) custom-call(f32[32,8,512]{2,1,0:T(8,128)} %sketch.1, f32[8,8,512]{2,1,0:T(8,128)} %weights.1), custom_call_target="tpu_custom_call" | custom-call | tf_op jit(solution)/shard_map/pallas_call | solution.py:18
  2.0 3.0 %collective-permute-start = (f32[80,512]{1,0:T(8,128)S(1)}, f32[80,512]{1,0:T(8,128)S(1)}, u32[]{:S(2)}, u32[]{:S(2)}) collective-permute-start(f32[80,512]{1,0:T(8,128)S(1)} %get-tuple-element.27), channel_id=1, source_target_pairs={{0,16},{1,17},{2,18},{3,19},{4,8},{5,9},{6,10},{7,11},{8,4},{9,5},... | collective-permute-start | bytes 491528 | tf_op jit(solution)/shard_map/ppermute | solution.py:445
  5.1 0.1 collective-permute-start.1
  5.2 0.4 %collective-permute-start.2 = (f32[16,128]{1,0:T(8,128)S(1)}, f32[16,128]{1,0:T(8,128)S(1)}, u32[]{:S(2)}, u32[]{:S(2)}) collective-permute-start(f32[16,128]{1,0:T(8,128)S(1)} %get-tuple-element.39), channel_id=1, source_target_pairs={{0,4},{1,17},{2,18},{3,7},{4,0},{5,10},{6,9},{7,3},{8,12},{9,6},{1... | collective-permute-start | bytes 24584 | tf_op jit(solution)/shard_map/ppermute | solution.py:445
  5.6 1.1 %collective-permute-start.3 = (f32[16,128]{1,0:T(8,128)S(1)}, f32[16,128]{1,0:T(8,128)S(1)}, u32[]{:S(2)}, u32[]{:S(2)}) collective-permute-start(f32[16,128]{1,0:T(8,128)S(1)} %get-tuple-element.40), channel_id=1, source_target_pairs={{0,16},{1,17},{2,18},{3,19},{4,9},{5,8},{6,11},{7,10},{8,5},{9,4},... | collective-permute-start | bytes 24584 | tf_op jit(solution)/shard_map/ppermute | solution.py:445
  6.7 0.0 collective-permute-done.1.second_message.bulk_message
  6.7 0.2 shard_map.44
  6.9 2.7 %collective-permute-start.4 = (f32[16,128]{1,0:T(8,128)S(1)}, f32[16,128]{1,0:T(8,128)S(1)}, u32[]{:S(2)}, u32[]{:S(2)}) collective-permute-start(f32[16,128]{1,0:T(8,128)S(1)} %get-tuple-element.41), channel_id=1, source_target_pairs={{0,4},{1,2},{2,1},{3,7},{4,0},{5,6},{6,5},{7,3},{8,12},{9,10},{10,... | collective-permute-start | bytes 24584 | tf_op jit(solution)/shard_map/ppermute | solution.py:445
  9.5 1.0 %collective-permute-start.5 = (f32[16,128]{1,0:T(8,128)S(1)}, f32[16,128]{1,0:T(8,128)S(1)}, u32[]{:S(2)}, u32[]{:S(2)}) collective-permute-start(f32[16,128]{1,0:T(8,128)S(1)} %get-tuple-element.42), channel_id=1, source_target_pairs={{0,1},{1,0},{2,3},{3,2},{4,5},{5,4},{6,7},{7,6},{8,9},{9,8},{10,11... | collective-permute-start | bytes 24584 | tf_op jit(solution)/shard_map/ppermute | solution.py:445
  10.5 1.0 %shard_map.42 = (f32[6,32,512]{2,1,0:T(8,128)S(1)}, bf16[4,96,512]{2,1,0:T(8,128)(2,1)S(1)}, f32[96,96]{1,0:T(8,128)S(1)}, f32[96,96]{1,0:T(8,128)S(1)}) custom-call(f32[8,32,512]{2,1,0:T(8,128)S(1)} %get-tuple-element.24.by_row, f32[8,8,512]{2,1,0:T(8,128)S(1)} %get-tuple-element.25.weights_by_row), custom_call_target="tpu_custom_call" | custom-call | tf_op jit(solution)/shard_map/pallas_call | solution.py:18
  11.6 0.0 collective-permute-done.first_message
  11.6 1.0 %shard_map.43 = (bf16[4,96,512]{2,1,0:T(8,128)(2,1)S(1)}, f32[32,64]{1,0:T(8,128)S(1)}, f32[40,128]{1,0:T(8,128)S(1)}, f32[40,128]{1,0:T(8,128)S(1)}) custom-call(f32[8,32,512]{2,1,0:T(8,128)S(1)} %get-tuple-element.24.by_row, f32[8,8,512]{2,1,0:T(8,128)S(1)} %get-tuple-element.25.weights_by_row, f32[80,512]{1,0:T(8,128)S(1)} %collective-permute-done.first_message, ...), custom_call_target="tpu_custom_call" | custom-call | tf_op jit(solution)/shard_map/pallas_call | solution.py:18
  12.5 0.0 collective-permute-done.2.rest_0_
  12.5 0.0 collective-permute-done.3.rest_1_
  12.5 0.0 collective-permute-done.4.rest_2_
  12.5 0.7 %collective-permute-done.5.rest_3_ = f32[16,128]{1,0:T(8,128)S(1)} collective-permute-done((f32[16,128]{1,0:T(8,128)S(1)}, f32[16,128]{1,0:T(8,128)S(1)}, u32[]{:S(2)}, u32[]{:S(2)}) %collective-permute-start.5) | collective-permute-done | bytes 8224 | tf_op jit(solution)/shard_map/ppermute | solution.py:445
  13.2 0.7 %shard_map.45 = (f32[16,1,1152]{2,1,0:T(1,128)S(1)}, f32[32,256]{1,0:T(8,128)S(1)}) custom-call(f32[40,128]{1,0:T(8,128)S(1)} %get-tuple-element.35.left, f32[40,128]{1,0:T(8,128)S(1)} %get-tuple-element.36.right, f32[40,128]{1,0:T(8,128)S(1)} %get-tuple-element.37.left_halo, f32[40,128]{1,0:T(8,128)S(1)} %get-tuple-element.38.right_halo, ...), custom_call_target="tpu_custom_call" | custom-call | tf_op jit(solution)/shard_map/pallas_call | solution.py:18
  13.9 8.5 %all_to_all.5.parts = f32[16,1,1152]{2,1,0:T(1,128)S(1)} all-to-all(f32[16,1,1152]{2,1,0:T(1,128)S(1)} %get-tuple-element.45), channel_id=1, replica_groups={{6,0,4,8,12,5,13,14,7,15,1,9,2,10,3,11},{22,16,20,24,28,21,29,30,23,31,..., dimensions={0} | all-to-all | bytes 147456 | tf_op jit(solution)/shard_map/all_to_all | solution.py:504
  22.5 2.0 %shard_map.46 = (f32[32,8,512]{2,1,0:T(8,128)}, f32[32,32]{1,0:T(8,128)}) custom-call(bf16[4,96,512]{2,1,0:T(8,128)(2,1)S(1)} %get-tuple-element.26.inner_second, bf16[4,96,512]{2,1,0:T(8,128)(2,1)S(1)} %get-tuple-element.32.outer_second, f32[32,256]{1,0:T(8,128)S(1)} %get-tuple-element.44.edges, f32[16,1,1152]{2,1,0:T(1,128)S(1)} %all_to_all.5.parts), custom_call_target="tpu_custom_call" | custom-call | tf_op jit(solution)/shard_map/pallas_call | solution.py:18
Async XLA Ops:
  2.0 9.5 %collective-permute-start = (f32[80,512]{1,0:T(8,128)S(1)}, f32[80,512]{1,0:T(8,128)S(1)}, u32[]{:S(2)}, u32[]{:S(2)}) collective-permute-start(f32[80,512]{1,0:T(8,128)S(1)} %get-tuple-element.27), channel_id=1, source_target_pairs={{0,16},{1,17},{2,18},{3,19},{4,8},{5,9},{6,10},{7,11},{8,4},{9,5},... | collective-permute-start | bytes 491528 | tf_op jit(solution)/shard_map/ppermute | solution.py:445
  5.1 1.6 %collective-permute-start.1 = (f32[72,512]{1,0:T(8,128)S(1)}, f32[72,512]{1,0:T(8,128)S(1)}, u32[]{:S(2)}, u32[]{:S(2)}) collective-permute-start(f32[72,512]{1,0:T(8,128)S(1)} %get-tuple-element.28), channel_id=1, source_target_pairs={{0,4},{1,5},{2,6},{3,7},{4,0},{5,1},{6,2},{7,3},{8,12},{9,13},{10,... | collective-permute-start | bytes 442376 | tf_op jit(solution)/shard_map/ppermute | solution.py:445
  5.2 7.4 %collective-permute-start.2 = (f32[16,128]{1,0:T(8,128)S(1)}, f32[16,128]{1,0:T(8,128)S(1)}, u32[]{:S(2)}, u32[]{:S(2)}) collective-permute-start(f32[16,128]{1,0:T(8,128)S(1)} %get-tuple-element.39), channel_id=1, source_target_pairs={{0,4},{1,17},{2,18},{3,7},{4,0},{5,10},{6,9},{7,3},{8,12},{9,6},{1... | collective-permute-start | bytes 24584 | tf_op jit(solution)/shard_map/ppermute | solution.py:445
  5.6 6.9 %collective-permute-start.3 = (f32[16,128]{1,0:T(8,128)S(1)}, f32[16,128]{1,0:T(8,128)S(1)}, u32[]{:S(2)}, u32[]{:S(2)}) collective-permute-start(f32[16,128]{1,0:T(8,128)S(1)} %get-tuple-element.40), channel_id=1, source_target_pairs={{0,16},{1,17},{2,18},{3,19},{4,9},{5,8},{6,11},{7,10},{8,5},{9,4},... | collective-permute-start | bytes 24584 | tf_op jit(solution)/shard_map/ppermute | solution.py:445
  6.9 5.7 %collective-permute-start.4 = (f32[16,128]{1,0:T(8,128)S(1)}, f32[16,128]{1,0:T(8,128)S(1)}, u32[]{:S(2)}, u32[]{:S(2)}) collective-permute-start(f32[16,128]{1,0:T(8,128)S(1)} %get-tuple-element.41), channel_id=1, source_target_pairs={{0,4},{1,2},{2,1},{3,7},{4,0},{5,6},{6,5},{7,3},{8,12},{9,10},{10,... | collective-permute-start | bytes 24584 | tf_op jit(solution)/shard_map/ppermute | solution.py:445
  9.5 3.7 %collective-permute-start.5 = (f32[16,128]{1,0:T(8,128)S(1)}, f32[16,128]{1,0:T(8,128)S(1)}, u32[]{:S(2)}, u32[]{:S(2)}) collective-permute-start(f32[16,128]{1,0:T(8,128)S(1)} %get-tuple-element.42), channel_id=1, source_target_pairs={{0,1},{1,0},{2,3},{3,2},{4,5},{5,4},{6,7},{7,6},{8,9},{9,8},{10,11... | collective-permute-start | bytes 24584 | tf_op jit(solution)/shard_map/ppermute | solution.py:445

commit v9 on v7

--- a/solution.py
+++ b/solution.py
@@ -100,7 +100,7 @@
         totals = [total + jnp.where(present, part, 0.0) for total, part in zip(totals, parts)]
     left[...], right[...] = totals
     to_left, to_right = folded(left[...], 2), folded(right[...], PITCH - 4)
-    for message, up in zip(col_messages, (odd_col, jnp.logical_not(odd_col))):
+    for message, up in zip(col_messages, (jnp.logical_not(odd_col), odd_col)):
         message[...] = jnp.where(up, to_right, to_left)
 
 
@@ -270,7 +270,7 @@
 
 
 def late_kernel(rows, left, right, left_halo, right_halo, *rest):
-    diagonal_messages, col_messages, (early_grams, grams, edges) = rest[:2], rest[2:4], rest[4:]
+    diagonal_messages, col_messages, (early_grams, grams, edges) = rest[:2], rest[3:1:-1], rest[4:]
     planes = early_grams.shape[0]
     odd_row, has_below, has_above = sides_of("row")
     odd_col, has_left, has_right = sides_of("col")
@@ -468,7 +468,7 @@
     left, right, *messages = call(
         functools.partial(strips_kernel, rows), [side, side] + [f32(16, LANES)] * 2, left, right, from_rows[1]
     )
-    from_cols = [swap(messages[at], col_pairing=at) for at in range(2)]
+    from_cols = [swap(messages[1 - at], col_pairing=at) for at in (1, 0)]
     parts_of = functools.partial(jax.ShapeDtypeStruct, dtype=jnp.bfloat16)
     products = f32(3 * planes, 3 * planes)
     middle, inner_second, *inner_products = call(

time: 24.4 us -> 24.8 us (1.016)
  blocking collectives: 8.27 us -> 10.3 us
  starting transfers between devices: 8.31 us -> 7.41 us
  waiting for transfers between devices: 0.67 us -> 0.02 us
    all_to_all x1, blocking collectives: 8.27 us -> 10.3 us  [on_device(): lax.all_to_all(grams, ('row', 'col'), 0, 0, axis_index_groups=[order], ti...]
    ppermute x6, starting transfers between devices: 8.31 us -> 7.41 us  [swap(): return lax.ppermute(value, names, pairs)]
    ppermute x6, waiting for transfers between devices: 0.67 us -> 0.02 us  [swap(): return lax.ppermute(value, names, pairs)]
  transfers between devices with their start and end apart: 6 -> 6, of which waited for: 1 -> 0; matrix products, arithmetic and copies ran while one was open for 0% -> 0% of each run, Pallas kernels for 9% -> 9%
where the time goes in v9:
time: 24.8 us; the launch traced here: 24.7 us
  blocking collectives  10.3 us (42%)
  starting transfers between devices  7.41 us (30%)
  Pallas kernels  6.3 us (25%)
  between operations  0.69 us (3%)
    all_to_all x1, blocking collectives, on_device(): lax.all_to_all(grams, ('row', 'col'), 0, 0, axis_index_groups=[order], ti...  10.3 us
    ppermute x6, starting transfers between devices, swap(): return lax.ppermute(value, names, pairs)  7.41 us
    pallas_call x6, Pallas kernels, call(): pl.pallas_call(kernel, out_shape=out_shapes, in_specs=[pl.BlockSpec(memor...  6.3 us
  transfers between devices with their start and end apart: 6, of which 0 were waited for; matrix products, arithmetic and copies ran while one was open for 0% of the time, Pallas kernels for 9%

profile of v9, /device:TPU:0, one launch (start us, length us, event | category | flops | bytes accessed | tf_op | source)
XLA Modules:
  0.0 24.7 jit_solution(8427415395225256960)
XLA Ops:
  0.6 1.4 %shard_map.41 = (f32[8,32,512]{2,1,0:T(8,128)S(1)}, f32[8,8,512]{2,1,0:T(8,128)S(1)}, f32[40,128]{1,0:T(8,128)S(1)}, f32[40,128]{1,0:T(8,128)S(1)}, f32[80,512]{...) custom-call(f32[32,8,512]{2,1,0:T(8,128)} %sketch.1, f32[8,8,512]{2,1,0:T(8,128)} %weights.1), custom_call_target="tpu_custom_call" | custom-call | tf_op jit(solution)/shard_map/pallas_call | solution.py:18
  2.0 3.0 %collective-permute-start = (f32[80,512]{1,0:T(8,128)S(1)}, f32[80,512]{1,0:T(8,128)S(1)}, u32[]{:S(2)}, u32[]{:S(2)}) collective-permute-start(f32[80,512]{1,0:T(8,128)S(1)} %get-tuple-element.27), channel_id=1, source_target_pairs={{0,16},{1,17},{2,18},{3,19},{4,8},{5,9},{6,10},{7,11},{8,4},{9,5},... | collective-permute-start | bytes 491528 | tf_op jit(solution)/shard_map/ppermute | solution.py:445
  5.1 0.1 collective-permute-start.1
  5.2 0.4 %collective-permute-start.2 = (f32[16,128]{1,0:T(8,128)S(1)}, f32[16,128]{1,0:T(8,128)S(1)}, u32[]{:S(2)}, u32[]{:S(2)}) collective-permute-start(f32[16,128]{1,0:T(8,128)S(1)} %get-tuple-element.39), channel_id=1, source_target_pairs={{0,4},{1,17},{2,18},{3,7},{4,0},{5,10},{6,9},{7,3},{8,12},{9,6},{1... | collective-permute-start | bytes 24584 | tf_op jit(solution)/shard_map/ppermute | solution.py:445
  5.6 1.1 %collective-permute-start.3 = (f32[16,128]{1,0:T(8,128)S(1)}, f32[16,128]{1,0:T(8,128)S(1)}, u32[]{:S(2)}, u32[]{:S(2)}) collective-permute-start(f32[16,128]{1,0:T(8,128)S(1)} %get-tuple-element.40), channel_id=1, source_target_pairs={{0,16},{1,17},{2,18},{3,19},{4,9},{5,8},{6,11},{7,10},{8,5},{9,4},... | collective-permute-start | bytes 24584 | tf_op jit(solution)/shard_map/ppermute | solution.py:445
  6.7 0.0 collective-permute-done.1.second_message.bulk_message
  6.7 0.2 shard_map.44
  6.9 2.1 %collective-permute-start.4 = (f32[16,128]{1,0:T(8,128)S(1)}, f32[16,128]{1,0:T(8,128)S(1)}, u32[]{:S(2)}, u32[]{:S(2)}) collective-permute-start(f32[16,128]{1,0:T(8,128)S(1)} %get-tuple-element.41), channel_id=1, source_target_pairs={{0,1},{1,0},{2,3},{3,2},{4,5},{5,4},{6,7},{7,6},{8,9},{9,8},{10,11... | collective-permute-start | bytes 24584 | tf_op jit(solution)/shard_map/ppermute | solution.py:445
  9.0 0.7 %collective-permute-start.5 = (f32[16,128]{1,0:T(8,128)S(1)}, f32[16,128]{1,0:T(8,128)S(1)}, u32[]{:S(2)}, u32[]{:S(2)}) collective-permute-start(f32[16,128]{1,0:T(8,128)S(1)} %get-tuple-element.42), channel_id=1, source_target_pairs={{0,4},{1,2},{2,1},{3,7},{4,0},{5,6},{6,5},{7,3},{8,12},{9,10},{10,... | collective-permute-start | bytes 24584 | tf_op jit(solution)/shard_map/ppermute | solution.py:445
  9.6 1.0 %shard_map.42 = (f32[6,32,512]{2,1,0:T(8,128)S(1)}, bf16[4,96,512]{2,1,0:T(8,128)(2,1)S(1)}, f32[96,96]{1,0:T(8,128)S(1)}, f32[96,96]{1,0:T(8,128)S(1)}) custom-call(f32[8,32,512]{2,1,0:T(8,128)S(1)} %get-tuple-element.24.by_row, f32[8,8,512]{2,1,0:T(8,128)S(1)} %get-tuple-element.25.weights_by_row), custom_call_target="tpu_custom_call" | custom-call | tf_op jit(solution)/shard_map/pallas_call | solution.py:18
  10.7 0.0 collective-permute-done.first_message
  10.7 1.0 %shard_map.43 = (bf16[4,96,512]{2,1,0:T(8,128)(2,1)S(1)}, f32[32,64]{1,0:T(8,128)S(1)}, f32[40,128]{1,0:T(8,128)S(1)}, f32[40,128]{1,0:T(8,128)S(1)}) custom-call(f32[8,32,512]{2,1,0:T(8,128)S(1)} %get-tuple-element.24.by_row, f32[8,8,512]{2,1,0:T(8,128)S(1)} %get-tuple-element.25.weights_by_row, f32[80,512]{1,0:T(8,128)S(1)} %collective-permute-done.first_message, ...), custom_call_target="tpu_custom_call" | custom-call | tf_op jit(solution)/shard_map/pallas_call | solution.py:18
  11.6 0.0 collective-permute-done.2.rest_0_
  11.6 0.0 collective-permute-done.3.rest_1_
  11.6 0.0 collective-permute-done.4.rest_2_
  11.6 0.0 collective-permute-done.5.rest_3_
  11.6 0.7 %shard_map.45 = (f32[16,1,1152]{2,1,0:T(1,128)S(1)}, f32[32,256]{1,0:T(8,128)S(1)}) custom-call(f32[40,128]{1,0:T(8,128)S(1)} %get-tuple-element.35.left, f32[40,128]{1,0:T(8,128)S(1)} %get-tuple-element.36.right, f32[40,128]{1,0:T(8,128)S(1)} %get-tuple-element.37.left_halo, f32[40,128]{1,0:T(8,128)S(1)} %get-tuple-element.38.right_halo, ...), custom_call_target="tpu_custom_call" | custom-call | tf_op jit(solution)/shard_map/pallas_call | solution.py:18
  12.4 10.3 %all_to_all.5.parts = f32[16,1,1152]{2,1,0:T(1,128)S(1)} all-to-all(f32[16,1,1152]{2,1,0:T(1,128)S(1)} %get-tuple-element.45), channel_id=1, replica_groups={{6,0,4,8,12,1,5,9,13,2,10,14,3,7,11,15},{22,16,20,24,28,17,21,25,29,18,..., dimensions={0} | all-to-all | bytes 147456 | tf_op jit(solution)/shard_map/all_to_all | solution.py:504
  22.6 2.0 %shard_map.46 = (f32[32,8,512]{2,1,0:T(8,128)}, f32[32,32]{1,0:T(8,128)}) custom-call(bf16[4,96,512]{2,1,0:T(8,128)(2,1)S(1)} %get-tuple-element.26.inner_second, bf16[4,96,512]{2,1,0:T(8,128)(2,1)S(1)} %get-tuple-element.32.outer_second, f32[32,256]{1,0:T(8,128)S(1)} %get-tuple-element.44.edges, f32[16,1,1152]{2,1,0:T(1,128)S(1)} %all_to_all.5.parts), custom_call_target="tpu_custom_call" | custom-call | tf_op jit(solution)/shard_map/pallas_call | solution.py:18
Async XLA Ops:
  2.0 8.6 %collective-permute-start = (f32[80,512]{1,0:T(8,128)S(1)}, f32[80,512]{1,0:T(8,128)S(1)}, u32[]{:S(2)}, u32[]{:S(2)}) collective-permute-start(f32[80,512]{1,0:T(8,128)S(1)} %get-tuple-element.27), channel_id=1, source_target_pairs={{0,16},{1,17},{2,18},{3,19},{4,8},{5,9},{6,10},{7,11},{8,4},{9,5},... | collective-permute-start | bytes 491528 | tf_op jit(solution)/shard_map/ppermute | solution.py:445
  5.1 1.6 %collective-permute-start.1 = (f32[72,512]{1,0:T(8,128)S(1)}, f32[72,512]{1,0:T(8,128)S(1)}, u32[]{:S(2)}, u32[]{:S(2)}) collective-permute-start(f32[72,512]{1,0:T(8,128)S(1)} %get-tuple-element.28), channel_id=1, source_target_pairs={{0,4},{1,5},{2,6},{3,7},{4,0},{5,1},{6,2},{7,3},{8,12},{9,13},{10,... | collective-permute-start | bytes 442376 | tf_op jit(solution)/shard_map/ppermute | solution.py:445
  5.2 6.5 %collective-permute-start.2 = (f32[16,128]{1,0:T(8,128)S(1)}, f32[16,128]{1,0:T(8,128)S(1)}, u32[]{:S(2)}, u32[]{:S(2)}) collective-permute-start(f32[16,128]{1,0:T(8,128)S(1)} %get-tuple-element.39), channel_id=1, source_target_pairs={{0,4},{1,17},{2,18},{3,7},{4,0},{5,10},{6,9},{7,3},{8,12},{9,6},{1... | collective-permute-start | bytes 24584 | tf_op jit(solution)/shard_map/ppermute | solution.py:445
  5.6 6.0 %collective-permute-start.3 = (f32[16,128]{1,0:T(8,128)S(1)}, f32[16,128]{1,0:T(8,128)S(1)}, u32[]{:S(2)}, u32[]{:S(2)}) collective-permute-start(f32[16,128]{1,0:T(8,128)S(1)} %get-tuple-element.40), channel_id=1, source_target_pairs={{0,16},{1,17},{2,18},{3,19},{4,9},{5,8},{6,11},{7,10},{8,5},{9,4},... | collective-permute-start | bytes 24584 | tf_op jit(solution)/shard_map/ppermute | solution.py:445
  6.9 4.8 %collective-permute-start.4 = (f32[16,128]{1,0:T(8,128)S(1)}, f32[16,128]{1,0:T(8,128)S(1)}, u32[]{:S(2)}, u32[]{:S(2)}) collective-permute-start(f32[16,128]{1,0:T(8,128)S(1)} %get-tuple-element.41), channel_id=1, source_target_pairs={{0,1},{1,0},{2,3},{3,2},{4,5},{5,4},{6,7},{7,6},{8,9},{9,8},{10,11... | collective-permute-start | bytes 24584 | tf_op jit(solution)/shard_map/ppermute | solution.py:445
  9.0 2.7 %collective-permute-start.5 = (f32[16,128]{1,0:T(8,128)S(1)}, f32[16,128]{1,0:T(8,128)S(1)}, u32[]{:S(2)}, u32[]{:S(2)}) collective-permute-start(f32[16,128]{1,0:T(8,128)S(1)} %get-tuple-element.42), channel_id=1, source_target_pairs={{0,4},{1,2},{2,1},{3,7},{4,0},{5,6},{6,5},{7,3},{8,12},{9,10},{10,... | collective-permute-start | bytes 24584 | tf_op jit(solution)/shard_map/ppermute | solution.py:445

commit v10 on v9

--- a/solution.py
+++ b/solution.py
@@ -76,7 +76,7 @@
     bulk_messages[0][2 * planes + 8 :] = jnp.zeros((8, width), jnp.float32)
     pair = 2 * PITCH
     to_left, to_right = folded(strips[0], 2), folded(strips[1], PITCH - 4)
-    for message, up in zip(diagonal_messages, (odd_col, jnp.logical_not(odd_col))):
+    for message, up in zip(diagonal_messages, (jnp.logical_not(odd_col), odd_col)):
         edge = jnp.where(up, to_right, to_left)
         below = jnp.where(lane < pair, rolled(edge, -PITCH * rows), 0.0)
         start = PITCH * (rows + 2)
@@ -270,7 +270,7 @@
 
 
 def late_kernel(rows, left, right, left_halo, right_halo, *rest):
-    diagonal_messages, col_messages, (early_grams, grams, edges) = rest[:2], rest[3:1:-1], rest[4:]
+    diagonal_messages, col_messages, (early_grams, grams, edges) = rest[1::-1], rest[3:1:-1], rest[4:]
     planes = early_grams.shape[0]
     odd_row, has_below, has_above = sides_of("row")
     odd_col, has_left, has_right = sides_of("col")
@@ -464,7 +464,7 @@
         ],
     )
     from_rows = [swap(messages[at], row_pairing=at) for at in range(2)]
-    from_diagonals = [swap(messages[2 + at], row_pairing=0, col_pairing=at) for at in range(2)]
+    from_diagonals = [swap(messages[3 - at], row_pairing=0, col_pairing=at) for at in (1, 0)]
     left, right, *messages = call(
         functools.partial(strips_kernel, rows), [side, side] + [f32(16, LANES)] * 2, left, right, from_rows[1]
     )

time: 24.8 us -> 24.5 us (0.988)
  blocking collectives: 10.3 us -> 8.66 us
  starting transfers between devices: 7.41 us -> 8.63 us
    all_to_all x1, blocking collectives: 10.3 us -> 8.66 us  [on_device(): lax.all_to_all(grams, ('row', 'col'), 0, 0, axis_index_groups=[order], ti...]
    ppermute x6, starting transfers between devices: 7.41 us -> 8.63 us  [swap(): return lax.ppermute(value, names, pairs)]
where the time goes in v10:
time: 24.5 us; the launch traced here: 24.3 us
  blocking collectives  8.66 us (35%)
  starting transfers between devices  8.63 us (35%)
  Pallas kernels  6.3 us (26%)
  between operations  0.69 us (3%)
    all_to_all x1, blocking collectives, on_device(): lax.all_to_all(grams, ('row', 'col'), 0, 0, axis_index_groups=[order], ti...  8.66 us
    ppermute x6, starting transfers between devices, swap(): return lax.ppermute(value, names, pairs)  8.63 us
    pallas_call x6, Pallas kernels, call(): pl.pallas_call(kernel, out_shape=out_shapes, in_specs=[pl.BlockSpec(memor...  6.3 us
  transfers between devices with their start and end apart: 6, of which 0 were waited for; matrix products, arithmetic and copies ran while one was open for 0% of the time, Pallas kernels for 9%

profile of v10, /device:TPU:0, one launch (start us, length us, event | category | flops | bytes accessed | tf_op | source)
XLA Modules:
  0.0 24.3 jit_solution(7759038093281767088)
XLA Ops:
  0.6 1.4 %shard_map.41 = (f32[8,32,512]{2,1,0:T(8,128)S(1)}, f32[8,8,512]{2,1,0:T(8,128)S(1)}, f32[40,128]{1,0:T(8,128)S(1)}, f32[40,128]{1,0:T(8,128)S(1)}, f32[80,512]{...) custom-call(f32[32,8,512]{2,1,0:T(8,128)} %sketch.1, f32[8,8,512]{2,1,0:T(8,128)} %weights.1), custom_call_target="tpu_custom_call" | custom-call | tf_op jit(solution)/shard_map/pallas_call | solution.py:18
  2.0 3.0 %collective-permute-start = (f32[80,512]{1,0:T(8,128)S(1)}, f32[80,512]{1,0:T(8,128)S(1)}, u32[]{:S(2)}, u32[]{:S(2)}) collective-permute-start(f32[80,512]{1,0:T(8,128)S(1)} %get-tuple-element.27), channel_id=1, source_target_pairs={{0,16},{1,17},{2,18},{3,19},{4,8},{5,9},{6,10},{7,11},{8,4},{9,5},... | collective-permute-start | bytes 491528 | tf_op jit(solution)/shard_map/ppermute | solution.py:445
  5.1 0.1 collective-permute-start.1
  5.2 1.5 %collective-permute-start.2 = (f32[16,128]{1,0:T(8,128)S(1)}, f32[16,128]{1,0:T(8,128)S(1)}, u32[]{:S(2)}, u32[]{:S(2)}) collective-permute-start(f32[16,128]{1,0:T(8,128)S(1)} %get-tuple-element.39), channel_id=1, source_target_pairs={{0,16},{1,17},{2,18},{3,19},{4,9},{5,8},{6,11},{7,10},{8,5},{9,4},... | collective-permute-start | bytes 24584 | tf_op jit(solution)/shard_map/ppermute | solution.py:445
  6.7 0.6 %collective-permute-start.3 = (f32[16,128]{1,0:T(8,128)S(1)}, f32[16,128]{1,0:T(8,128)S(1)}, u32[]{:S(2)}, u32[]{:S(2)}) collective-permute-start(f32[16,128]{1,0:T(8,128)S(1)} %get-tuple-element.40), channel_id=1, source_target_pairs={{0,4},{1,17},{2,18},{3,7},{4,0},{5,10},{6,9},{7,3},{8,12},{9,6},{1... | collective-permute-start | bytes 24584 | tf_op jit(solution)/shard_map/ppermute | solution.py:445
  7.2 0.0 collective-permute-done.1.second_message.bulk_message
  7.3 0.2 shard_map.44
  7.4 1.5 %collective-permute-start.4 = (f32[16,128]{1,0:T(8,128)S(1)}, f32[16,128]{1,0:T(8,128)S(1)}, u32[]{:S(2)}, u32[]{:S(2)}) collective-permute-start(f32[16,128]{1,0:T(8,128)S(1)} %get-tuple-element.41), channel_id=1, source_target_pairs={{0,1},{1,0},{2,3},{3,2},{4,5},{5,4},{6,7},{7,6},{8,9},{9,8},{10,11... | collective-permute-start | bytes 24584 | tf_op jit(solution)/shard_map/ppermute | solution.py:445
  9.0 1.9 %collective-permute-start.5 = (f32[16,128]{1,0:T(8,128)S(1)}, f32[16,128]{1,0:T(8,128)S(1)}, u32[]{:S(2)}, u32[]{:S(2)}) collective-permute-start(f32[16,128]{1,0:T(8,128)S(1)} %get-tuple-element.42), channel_id=1, source_target_pairs={{0,4},{1,2},{2,1},{3,7},{4,0},{5,6},{6,5},{7,3},{8,12},{9,10},{10,... | collective-permute-start | bytes 24584 | tf_op jit(solution)/shard_map/ppermute | solution.py:445
  10.8 1.0 %shard_map.42 = (f32[6,32,512]{2,1,0:T(8,128)S(1)}, bf16[4,96,512]{2,1,0:T(8,128)(2,1)S(1)}, f32[96,96]{1,0:T(8,128)S(1)}, f32[96,96]{1,0:T(8,128)S(1)}) custom-call(f32[8,32,512]{2,1,0:T(8,128)S(1)} %get-tuple-element.24.by_row, f32[8,8,512]{2,1,0:T(8,128)S(1)} %get-tuple-element.25.weights_by_row), custom_call_target="tpu_custom_call" | custom-call | tf_op jit(solution)/shard_map/pallas_call | solution.py:18
  11.9 0.0 collective-permute-done.first_message
  11.9 1.0 %shard_map.43 = (bf16[4,96,512]{2,1,0:T(8,128)(2,1)S(1)}, f32[32,64]{1,0:T(8,128)S(1)}, f32[40,128]{1,0:T(8,128)S(1)}, f32[40,128]{1,0:T(8,128)S(1)}) custom-call(f32[8,32,512]{2,1,0:T(8,128)S(1)} %get-tuple-element.24.by_row, f32[8,8,512]{2,1,0:T(8,128)S(1)} %get-tuple-element.25.weights_by_row, f32[80,512]{1,0:T(8,128)S(1)} %collective-permute-done.first_message, ...), custom_call_target="tpu_custom_call" | custom-call | tf_op jit(solution)/shard_map/pallas_call | solution.py:18
  12.8 0.0 collective-permute-done.2.rest_0_
  12.8 0.0 collective-permute-done.3.rest_1_
  12.8 0.0 collective-permute-done.4.rest_2_
  12.9 0.0 collective-permute-done.5.rest_3_
  12.9 0.7 %shard_map.45 = (f32[16,1,1152]{2,1,0:T(1,128)S(1)}, f32[32,256]{1,0:T(8,128)S(1)}) custom-call(f32[40,128]{1,0:T(8,128)S(1)} %get-tuple-element.35.left, f32[40,128]{1,0:T(8,128)S(1)} %get-tuple-element.36.right, f32[40,128]{1,0:T(8,128)S(1)} %get-tuple-element.37.left_halo, f32[40,128]{1,0:T(8,128)S(1)} %get-tuple-element.38.right_halo, ...), custom_call_target="tpu_custom_call" | custom-call | tf_op jit(solution)/shard_map/pallas_call | solution.py:18
  13.6 8.7 %all_to_all.5.parts = f32[16,1,1152]{2,1,0:T(1,128)S(1)} all-to-all(f32[16,1,1152]{2,1,0:T(1,128)S(1)} %get-tuple-element.45), channel_id=1, replica_groups={{6,0,4,8,12,1,5,9,13,2,10,14,3,7,11,15},{22,16,20,24,28,17,21,25,29,18,..., dimensions={0} | all-to-all | bytes 147456 | tf_op jit(solution)/shard_map/all_to_all | solution.py:504
  22.3 2.0 %shard_map.46 = (f32[32,8,512]{2,1,0:T(8,128)}, f32[32,32]{1,0:T(8,128)}) custom-call(bf16[4,96,512]{2,1,0:T(8,128)(2,1)S(1)} %get-tuple-element.26.inner_second, bf16[4,96,512]{2,1,0:T(8,128)(2,1)S(1)} %get-tuple-element.32.outer_second, f32[32,256]{1,0:T(8,128)S(1)} %get-tuple-element.44.edges, f32[16,1,1152]{2,1,0:T(1,128)S(1)} %all_to_all.5.parts), custom_call_target="tpu_custom_call" | custom-call | tf_op jit(solution)/shard_map/pallas_call | solution.py:18
Async XLA Ops:
  2.0 9.8 %collective-permute-start = (f32[80,512]{1,0:T(8,128)S(1)}, f32[80,512]{1,0:T(8,128)S(1)}, u32[]{:S(2)}, u32[]{:S(2)}) collective-permute-start(f32[80,512]{1,0:T(8,128)S(1)} %get-tuple-element.27), channel_id=1, source_target_pairs={{0,16},{1,17},{2,18},{3,19},{4,8},{5,9},{6,10},{7,11},{8,4},{9,5},... | collective-permute-start | bytes 491528 | tf_op jit(solution)/shard_map/ppermute | solution.py:445
  5.1 2.2 %collective-permute-start.1 = (f32[72,512]{1,0:T(8,128)S(1)}, f32[72,512]{1,0:T(8,128)S(1)}, u32[]{:S(2)}, u32[]{:S(2)}) collective-permute-start(f32[72,512]{1,0:T(8,128)S(1)} %get-tuple-element.28), channel_id=1, source_target_pairs={{0,4},{1,5},{2,6},{3,7},{4,0},{5,1},{6,2},{7,3},{8,12},{9,13},{10,... | collective-permute-start | bytes 442376 | tf_op jit(solution)/shard_map/ppermute | solution.py:445
  5.2 7.7 %collective-permute-start.2 = (f32[16,128]{1,0:T(8,128)S(1)}, f32[16,128]{1,0:T(8,128)S(1)}, u32[]{:S(2)}, u32[]{:S(2)}) collective-permute-start(f32[16,128]{1,0:T(8,128)S(1)} %get-tuple-element.39), channel_id=1, source_target_pairs={{0,16},{1,17},{2,18},{3,19},{4,9},{5,8},{6,11},{7,10},{8,5},{9,4},... | collective-permute-start | bytes 24584 | tf_op jit(solution)/shard_map/ppermute | solution.py:445
  6.7 6.2 %collective-permute-start.3 = (f32[16,128]{1,0:T(8,128)S(1)}, f32[16,128]{1,0:T(8,128)S(1)}, u32[]{:S(2)}, u32[]{:S(2)}) collective-permute-start(f32[16,128]{1,0:T(8,128)S(1)} %get-tuple-element.40), channel_id=1, source_target_pairs={{0,4},{1,17},{2,18},{3,7},{4,0},{5,10},{6,9},{7,3},{8,12},{9,6},{1... | collective-permute-start | bytes 24584 | tf_op jit(solution)/shard_map/ppermute | solution.py:445
  7.4 5.4 %collective-permute-start.4 = (f32[16,128]{1,0:T(8,128)S(1)}, f32[16,128]{1,0:T(8,128)S(1)}, u32[]{:S(2)}, u32[]{:S(2)}) collective-permute-start(f32[16,128]{1,0:T(8,128)S(1)} %get-tuple-element.41), channel_id=1, source_target_pairs={{0,1},{1,0},{2,3},{3,2},{4,5},{5,4},{6,7},{7,6},{8,9},{9,8},{10,11... | collective-permute-start | bytes 24584 | tf_op jit(solution)/shard_map/ppermute | solution.py:445
  9.0 3.9 %collective-permute-start.5 = (f32[16,128]{1,0:T(8,128)S(1)}, f32[16,128]{1,0:T(8,128)S(1)}, u32[]{:S(2)}, u32[]{:S(2)}) collective-permute-start(f32[16,128]{1,0:T(8,128)S(1)} %get-tuple-element.42), channel_id=1, source_target_pairs={{0,4},{1,2},{2,1},{3,7},{4,0},{5,6},{6,5},{7,3},{8,12},{9,10},{10,... | collective-permute-start | bytes 24584 | tf_op jit(solution)/shard_map/ppermute | solution.py:445

commit v11 on v7

--- a/solution.py
+++ b/solution.py
@@ -498,7 +498,7 @@
         early_grams,
     )
     rows_of, cols_of = lax.axis_size("row"), lax.axis_size("col")
-    first = cols_of + cols_of // 2
+    first = cols_of + (cols_of - 1) // 2
     order = [first] + [row * cols_of + col for col in range(cols_of) for row in range(rows_of)]
     order = list(dict.fromkeys(order))
     parts = lax.all_to_all(grams, ("row", "col"), 0, 0, axis_index_groups=[order], tiled=True)

time: 24.4 us -> 24.4 us (level)
  no operation moved by 1% of the time
where the time goes in v11:
time: 24.4 us; the launch traced here: 24.2 us
  starting transfers between devices  8.31 us (34%)
  blocking collectives  8.27 us (34%)
  Pallas kernels  6.29 us (26%)
  between operations  0.68 us (3%)
  waiting for transfers between devices  0.67 us (3%)
    ppermute x6, starting transfers between devices, swap(): return lax.ppermute(value, names, pairs)  8.31 us
    all_to_all x1, blocking collectives, on_device(): lax.all_to_all(grams, ('row', 'col'), 0, 0, axis_index_groups=[order], ti...  8.27 us
    pallas_call x6, Pallas kernels, call(): pl.pallas_call(kernel, out_shape=out_shapes, in_specs=[pl.BlockSpec(memor...  6.29 us
    ppermute x6, waiting for transfers between devices, swap(): return lax.ppermute(value, names, pairs)  0.67 us
  transfers between devices with their start and end apart: 6, of which 1 were waited for; matrix products, arithmetic and copies ran while one was open for 0% of the time, Pallas kernels for 9%

profile of v11, /device:TPU:0, one launch (start us, length us, event | category | flops | bytes accessed | tf_op | source)
XLA Modules:
  0.0 24.2 jit_solution(1852969959635171044)
XLA Ops:
  0.6 1.4 %shard_map.41 = (f32[8,32,512]{2,1,0:T(8,128)S(1)}, f32[8,8,512]{2,1,0:T(8,128)S(1)}, f32[40,128]{1,0:T(8,128)S(1)}, f32[40,128]{1,0:T(8,128)S(1)}, f32[80,512]{...) custom-call(f32[32,8,512]{2,1,0:T(8,128)} %sketch.1, f32[8,8,512]{2,1,0:T(8,128)} %weights.1), custom_call_target="tpu_custom_call" | custom-call | tf_op jit(solution)/shard_map/pallas_call | solution.py:18
  2.0 3.0 %collective-permute-start = (f32[80,512]{1,0:T(8,128)S(1)}, f32[80,512]{1,0:T(8,128)S(1)}, u32[]{:S(2)}, u32[]{:S(2)}) collective-permute-start(f32[80,512]{1,0:T(8,128)S(1)} %get-tuple-element.27), channel_id=1, source_target_pairs={{0,16},{1,17},{2,18},{3,19},{4,8},{5,9},{6,10},{7,11},{8,4},{9,5},... | collective-permute-start | bytes 491528 | tf_op jit(solution)/shard_map/ppermute | solution.py:445
  5.1 0.1 collective-permute-start.1
  5.2 0.4 %collective-permute-start.2 = (f32[16,128]{1,0:T(8,128)S(1)}, f32[16,128]{1,0:T(8,128)S(1)}, u32[]{:S(2)}, u32[]{:S(2)}) collective-permute-start(f32[16,128]{1,0:T(8,128)S(1)} %get-tuple-element.39), channel_id=1, source_target_pairs={{0,4},{1,17},{2,18},{3,7},{4,0},{5,10},{6,9},{7,3},{8,12},{9,6},{1... | collective-permute-start | bytes 24584 | tf_op jit(solution)/shard_map/ppermute | solution.py:445
  5.6 1.1 %collective-permute-start.3 = (f32[16,128]{1,0:T(8,128)S(1)}, f32[16,128]{1,0:T(8,128)S(1)}, u32[]{:S(2)}, u32[]{:S(2)}) collective-permute-start(f32[16,128]{1,0:T(8,128)S(1)} %get-tuple-element.40), channel_id=1, source_target_pairs={{0,16},{1,17},{2,18},{3,19},{4,9},{5,8},{6,11},{7,10},{8,5},{9,4},... | collective-permute-start | bytes 24584 | tf_op jit(solution)/shard_map/ppermute | solution.py:445
  6.7 0.0 collective-permute-done.1.second_message.bulk_message
  6.7 0.2 shard_map.44
  6.9 2.7 %collective-permute-start.4 = (f32[16,128]{1,0:T(8,128)S(1)}, f32[16,128]{1,0:T(8,128)S(1)}, u32[]{:S(2)}, u32[]{:S(2)}) collective-permute-start(f32[16,128]{1,0:T(8,128)S(1)} %get-tuple-element.41), channel_id=1, source_target_pairs={{0,4},{1,2},{2,1},{3,7},{4,0},{5,6},{6,5},{7,3},{8,12},{9,10},{10,... | collective-permute-start | bytes 24584 | tf_op jit(solution)/shard_map/ppermute | solution.py:445
  9.5 1.0 %collective-permute-start.5 = (f32[16,128]{1,0:T(8,128)S(1)}, f32[16,128]{1,0:T(8,128)S(1)}, u32[]{:S(2)}, u32[]{:S(2)}) collective-permute-start(f32[16,128]{1,0:T(8,128)S(1)} %get-tuple-element.42), channel_id=1, source_target_pairs={{0,1},{1,0},{2,3},{3,2},{4,5},{5,4},{6,7},{7,6},{8,9},{9,8},{10,11... | collective-permute-start | bytes 24584 | tf_op jit(solution)/shard_map/ppermute | solution.py:445
  10.5 1.0 %shard_map.42 = (f32[6,32,512]{2,1,0:T(8,128)S(1)}, bf16[4,96,512]{2,1,0:T(8,128)(2,1)S(1)}, f32[96,96]{1,0:T(8,128)S(1)}, f32[96,96]{1,0:T(8,128)S(1)}) custom-call(f32[8,32,512]{2,1,0:T(8,128)S(1)} %get-tuple-element.24.by_row, f32[8,8,512]{2,1,0:T(8,128)S(1)} %get-tuple-element.25.weights_by_row), custom_call_target="tpu_custom_call" | custom-call | tf_op jit(solution)/shard_map/pallas_call | solution.py:18
  11.6 0.0 collective-permute-done.first_message
  11.6 1.0 %shard_map.43 = (bf16[4,96,512]{2,1,0:T(8,128)(2,1)S(1)}, f32[32,64]{1,0:T(8,128)S(1)}, f32[40,128]{1,0:T(8,128)S(1)}, f32[40,128]{1,0:T(8,128)S(1)}) custom-call(f32[8,32,512]{2,1,0:T(8,128)S(1)} %get-tuple-element.24.by_row, f32[8,8,512]{2,1,0:T(8,128)S(1)} %get-tuple-element.25.weights_by_row, f32[80,512]{1,0:T(8,128)S(1)} %collective-permute-done.first_message, ...), custom_call_target="tpu_custom_call" | custom-call | tf_op jit(solution)/shard_map/pallas_call | solution.py:18
  12.5 0.0 collective-permute-done.2.rest_0_
  12.5 0.0 collective-permute-done.3.rest_1_
  12.5 0.0 collective-permute-done.4.rest_2_
  12.5 0.7 %collective-permute-done.5.rest_3_ = f32[16,128]{1,0:T(8,128)S(1)} collective-permute-done((f32[16,128]{1,0:T(8,128)S(1)}, f32[16,128]{1,0:T(8,128)S(1)}, u32[]{:S(2)}, u32[]{:S(2)}) %collective-permute-start.5) | collective-permute-done | bytes 8224 | tf_op jit(solution)/shard_map/ppermute | solution.py:445
  13.2 0.7 %shard_map.45 = (f32[16,1,1152]{2,1,0:T(1,128)S(1)}, f32[32,256]{1,0:T(8,128)S(1)}) custom-call(f32[40,128]{1,0:T(8,128)S(1)} %get-tuple-element.35.left, f32[40,128]{1,0:T(8,128)S(1)} %get-tuple-element.36.right, f32[40,128]{1,0:T(8,128)S(1)} %get-tuple-element.37.left_halo, f32[40,128]{1,0:T(8,128)S(1)} %get-tuple-element.38.right_halo, ...), custom_call_target="tpu_custom_call" | custom-call | tf_op jit(solution)/shard_map/pallas_call | solution.py:18
  13.9 8.3 %all_to_all.5.parts = f32[16,1,1152]{2,1,0:T(1,128)S(1)} all-to-all(f32[16,1,1152]{2,1,0:T(1,128)S(1)} %get-tuple-element.45), channel_id=1, replica_groups={{5,0,4,8,12,1,9,13,2,6,10,14,3,7,11,15},{21,16,20,24,28,17,25,29,18,22,..., dimensions={0} | all-to-all | bytes 147456 | tf_op jit(solution)/shard_map/all_to_all | solution.py:504
  22.2 2.0 %shard_map.46 = (f32[32,8,512]{2,1,0:T(8,128)}, f32[32,32]{1,0:T(8,128)}) custom-call(bf16[4,96,512]{2,1,0:T(8,128)(2,1)S(1)} %get-tuple-element.26.inner_second, bf16[4,96,512]{2,1,0:T(8,128)(2,1)S(1)} %get-tuple-element.32.outer_second, f32[32,256]{1,0:T(8,128)S(1)} %get-tuple-element.44.edges, f32[16,1,1152]{2,1,0:T(1,128)S(1)} %all_to_all.5.parts), custom_call_target="tpu_custom_call" | custom-call | tf_op jit(solution)/shard_map/pallas_call | solution.py:18
Async XLA Ops:
  2.0 9.5 %collective-permute-start = (f32[80,512]{1,0:T(8,128)S(1)}, f32[80,512]{1,0:T(8,128)S(1)}, u32[]{:S(2)}, u32[]{:S(2)}) collective-permute-start(f32[80,512]{1,0:T(8,128)S(1)} %get-tuple-element.27), channel_id=1, source_target_pairs={{0,16},{1,17},{2,18},{3,19},{4,8},{5,9},{6,10},{7,11},{8,4},{9,5},... | collective-permute-start | bytes 491528 | tf_op jit(solution)/shard_map/ppermute | solution.py:445
  5.1 1.6 %collective-permute-start.1 = (f32[72,512]{1,0:T(8,128)S(1)}, f32[72,512]{1,0:T(8,128)S(1)}, u32[]{:S(2)}, u32[]{:S(2)}) collective-permute-start(f32[72,512]{1,0:T(8,128)S(1)} %get-tuple-element.28), channel_id=1, source_target_pairs={{0,4},{1,5},{2,6},{3,7},{4,0},{5,1},{6,2},{7,3},{8,12},{9,13},{10,... | collective-permute-start | bytes 442376 | tf_op jit(solution)/shard_map/ppermute | solution.py:445
  5.2 7.4 %collective-permute-start.2 = (f32[16,128]{1,0:T(8,128)S(1)}, f32[16,128]{1,0:T(8,128)S(1)}, u32[]{:S(2)}, u32[]{:S(2)}) collective-permute-start(f32[16,128]{1,0:T(8,128)S(1)} %get-tuple-element.39), channel_id=1, source_target_pairs={{0,4},{1,17},{2,18},{3,7},{4,0},{5,10},{6,9},{7,3},{8,12},{9,6},{1... | collective-permute-start | bytes 24584 | tf_op jit(solution)/shard_map/ppermute | solution.py:445
  5.6 6.9 %collective-permute-start.3 = (f32[16,128]{1,0:T(8,128)S(1)}, f32[16,128]{1,0:T(8,128)S(1)}, u32[]{:S(2)}, u32[]{:S(2)}) collective-permute-start(f32[16,128]{1,0:T(8,128)S(1)} %get-tuple-element.40), channel_id=1, source_target_pairs={{0,16},{1,17},{2,18},{3,19},{4,9},{5,8},{6,11},{7,10},{8,5},{9,4},... | collective-permute-start | bytes 24584 | tf_op jit(solution)/shard_map/ppermute | solution.py:445
  6.9 5.7 %collective-permute-start.4 = (f32[16,128]{1,0:T(8,128)S(1)}, f32[16,128]{1,0:T(8,128)S(1)}, u32[]{:S(2)}, u32[]{:S(2)}) collective-permute-start(f32[16,128]{1,0:T(8,128)S(1)} %get-tuple-element.41), channel_id=1, source_target_pairs={{0,4},{1,2},{2,1},{3,7},{4,0},{5,6},{6,5},{7,3},{8,12},{9,10},{10,... | collective-permute-start | bytes 24584 | tf_op jit(solution)/shard_map/ppermute | solution.py:445
  9.5 3.7 %collective-permute-start.5 = (f32[16,128]{1,0:T(8,128)S(1)}, f32[16,128]{1,0:T(8,128)S(1)}, u32[]{:S(2)}, u32[]{:S(2)}) collective-permute-start(f32[16,128]{1,0:T(8,128)S(1)} %get-tuple-element.42), channel_id=1, source_target_pairs={{0,1},{1,0},{2,3},{3,2},{4,5},{5,4},{6,7},{7,6},{8,9},{9,8},{10,11... | collective-permute-start | bytes 24584 | tf_op jit(solution)/shard_map/ppermute | solution.py:445

commit v12 on v7

--- a/solution.py
+++ b/solution.py
@@ -165,8 +165,9 @@
     return jnp.concatenate(split(jnp.concatenate(kept, axis=1)), axis=0)
 
 
-def products_of(parts):
-    return lax.dot_general(parts, parts, (((1,), (1,)), ((), ())), preferred_element_type=jnp.float32)
+def products_of(parts, others=None):
+    others = parts if others is None else others
+    return lax.dot_general(parts, others, (((1,), (1,)), ((), ())), preferred_element_type=jnp.float32)
 
 
 def images_of(middle, weights, wanted, second, products):
@@ -297,7 +298,10 @@
         values = [apply_on_strip(value, strip[planes:]) for value, strip in zip(values, strips)]
         kept = jnp.concatenate([jnp.where(mask, value, 0.0) for mask, value in zip(masks, values)], axis=1)
         both = jnp.concatenate(values, axis=1)
-        gram.append(early_grams[:, at * planes : (at + 1) * planes] + gram_of(kept, both))
+        high, middle, low = split(kept)
+        one_side = jnp.concatenate([high, high, middle, high, low, middle], axis=1)
+        other_side = jnp.concatenate([high, middle, high, low, high, middle], axis=1)
+        gram.append(early_grams[:, at * planes : (at + 1) * planes] + products_of(one_side, other_side))
     edges[...] = both
     at_row = lax.broadcasted_iota(jnp.int32, (planes, planes), 0)
     at_col = lax.broadcasted_iota(jnp.int32, (planes, planes), 1)
@@ -305,10 +309,9 @@
     diagonal = jnp.sum(jnp.where(at_row == at_col, gram[1], 0.0), axis=0, keepdims=True)
     block = jnp.concatenate([mixed[8 * g : 8 * (g + 1)] for g in range(planes // 8)], axis=1)
     last = jnp.concatenate([diagonal] * (LANES // planes), axis=1)
-    for target in range(grams.shape[0]):
-        for at in range(8):
-            grams[target, :, at * LANES : (at + 1) * LANES] = block[at : at + 1]
-        grams[target, :, 8 * LANES :] = last
+    for at in range(8):
+        grams[:, at * LANES : (at + 1) * LANES] = block[at : at + 1]
+    grams[:, 8 * LANES :] = last
 
 
 def eliminate(grams, planes, half_way):
@@ -489,7 +492,7 @@
     )
     grams, edges = call(
         functools.partial(late_kernel, rows),
-        [f32(group, 1, 9 * LANES), f32(planes, 2 * LANES)],
+        [f32(1, 9 * LANES), f32(planes, 2 * LANES)],
         left,
         right,
         *halos,
@@ -501,6 +504,7 @@
     first = cols_of + cols_of // 2
     order = [first] + [row * cols_of + col for col in range(cols_of) for row in range(rows_of)]
     order = list(dict.fromkeys(order))
+    grams = jnp.broadcast_to(grams, (group, *grams.shape))
     parts = lax.all_to_all(grams, ("row", "col"), 0, 0, axis_index_groups=[order], tiled=True)
     return call(
         functools.partial(finish_kernel, float(rows * width * group)),

time: 24.4 us -> 24.4 us (level)
  no operation moved by 1% of the time
where the time goes in v12:
time: 24.4 us; the launch traced here: 24.3 us
  starting transfers between devices  8.31 us (34%)
  blocking collectives  8.27 us (34%)
  Pallas kernels  6.26 us (26%)
  between operations  0.69 us (3%)
  waiting for transfers between devices  0.67 us (3%)
    ppermute x6, starting transfers between devices, swap(): return lax.ppermute(value, names, pairs)  8.31 us
    all_to_all x1, blocking collectives, on_device(): lax.all_to_all(grams, ('row', 'col'), 0, 0, axis_index_groups=[order], ti...  8.27 us
    pallas_call x6, Pallas kernels, call(): pl.pallas_call(kernel, out_shape=out_shapes, in_specs=[pl.BlockSpec(memor...  6.26 us
    ppermute x6, waiting for transfers between devices, swap(): return lax.ppermute(value, names, pairs)  0.67 us
  transfers between devices with their start and end apart: 6, of which 1 were waited for; matrix products, arithmetic and copies ran while one was open for 0% of the time, Pallas kernels for 9%

profile of v12, /device:TPU:0, one launch (start us, length us, event | category | flops | bytes accessed | tf_op | source)
XLA Modules:
  0.0 24.3 jit_solution(6147393205293556796)
XLA Ops:
  0.6 1.4 %shard_map.41 = (f32[8,32,512]{2,1,0:T(8,128)S(1)}, f32[8,8,512]{2,1,0:T(8,128)S(1)}, f32[40,128]{1,0:T(8,128)S(1)}, f32[40,128]{1,0:T(8,128)S(1)}, f32[80,512]{...) custom-call(f32[32,8,512]{2,1,0:T(8,128)} %sketch.1, f32[8,8,512]{2,1,0:T(8,128)} %weights.1), custom_call_target="tpu_custom_call" | custom-call | tf_op jit(solution)/shard_map/pallas_call | solution.py:18
  2.0 3.0 %collective-permute-start = (f32[80,512]{1,0:T(8,128)S(1)}, f32[80,512]{1,0:T(8,128)S(1)}, u32[]{:S(2)}, u32[]{:S(2)}) collective-permute-start(f32[80,512]{1,0:T(8,128)S(1)} %get-tuple-element.27), channel_id=1, source_target_pairs={{0,16},{1,17},{2,18},{3,19},{4,8},{5,9},{6,10},{7,11},{8,4},{9,5},... | collective-permute-start | bytes 491528 | tf_op jit(solution)/shard_map/ppermute | solution.py:448
  5.1 0.1 collective-permute-start.1
  5.2 0.4 %collective-permute-start.2 = (f32[16,128]{1,0:T(8,128)S(1)}, f32[16,128]{1,0:T(8,128)S(1)}, u32[]{:S(2)}, u32[]{:S(2)}) collective-permute-start(f32[16,128]{1,0:T(8,128)S(1)} %get-tuple-element.39), channel_id=1, source_target_pairs={{0,4},{1,17},{2,18},{3,7},{4,0},{5,10},{6,9},{7,3},{8,12},{9,6},{1... | collective-permute-start | bytes 24584 | tf_op jit(solution)/shard_map/ppermute | solution.py:448
  5.6 1.1 %collective-permute-start.3 = (f32[16,128]{1,0:T(8,128)S(1)}, f32[16,128]{1,0:T(8,128)S(1)}, u32[]{:S(2)}, u32[]{:S(2)}) collective-permute-start(f32[16,128]{1,0:T(8,128)S(1)} %get-tuple-element.40), channel_id=1, source_target_pairs={{0,16},{1,17},{2,18},{3,19},{4,9},{5,8},{6,11},{7,10},{8,5},{9,4},... | collective-permute-start | bytes 24584 | tf_op jit(solution)/shard_map/ppermute | solution.py:448
  6.7 0.0 collective-permute-done.1.second_message.bulk_message
  6.7 0.2 shard_map.44
  6.9 2.7 %collective-permute-start.4 = (f32[16,128]{1,0:T(8,128)S(1)}, f32[16,128]{1,0:T(8,128)S(1)}, u32[]{:S(2)}, u32[]{:S(2)}) collective-permute-start(f32[16,128]{1,0:T(8,128)S(1)} %get-tuple-element.41), channel_id=1, source_target_pairs={{0,4},{1,2},{2,1},{3,7},{4,0},{5,6},{6,5},{7,3},{8,12},{9,10},{10,... | collective-permute-start | bytes 24584 | tf_op jit(solution)/shard_map/ppermute | solution.py:448
  9.5 1.0 %collective-permute-start.5 = (f32[16,128]{1,0:T(8,128)S(1)}, f32[16,128]{1,0:T(8,128)S(1)}, u32[]{:S(2)}, u32[]{:S(2)}) collective-permute-start(f32[16,128]{1,0:T(8,128)S(1)} %get-tuple-element.42), channel_id=1, source_target_pairs={{0,1},{1,0},{2,3},{3,2},{4,5},{5,4},{6,7},{7,6},{8,9},{9,8},{10,11... | collective-permute-start | bytes 24584 | tf_op jit(solution)/shard_map/ppermute | solution.py:448
  10.5 1.0 %shard_map.42 = (f32[6,32,512]{2,1,0:T(8,128)S(1)}, bf16[4,96,512]{2,1,0:T(8,128)(2,1)S(1)}, f32[96,96]{1,0:T(8,128)S(1)}, f32[96,96]{1,0:T(8,128)S(1)}) custom-call(f32[8,32,512]{2,1,0:T(8,128)S(1)} %get-tuple-element.24.by_row, f32[8,8,512]{2,1,0:T(8,128)S(1)} %get-tuple-element.25.weights_by_row), custom_call_target="tpu_custom_call" | custom-call | tf_op jit(solution)/shard_map/pallas_call | solution.py:18
  11.6 0.0 collective-permute-done.first_message
  11.6 0.9 %shard_map.43 = (bf16[4,96,512]{2,1,0:T(8,128)(2,1)S(1)}, f32[32,64]{1,0:T(8,128)S(1)}, f32[40,128]{1,0:T(8,128)S(1)}, f32[40,128]{1,0:T(8,128)S(1)}) custom-call(f32[8,32,512]{2,1,0:T(8,128)S(1)} %get-tuple-element.24.by_row, f32[8,8,512]{2,1,0:T(8,128)S(1)} %get-tuple-element.25.weights_by_row, f32[80,512]{1,0:T(8,128)S(1)} %collective-permute-done.first_message, ...), custom_call_target="tpu_custom_call" | custom-call | tf_op jit(solution)/shard_map/pallas_call | solution.py:18
  12.5 0.0 collective-permute-done.2.rest_0_
  12.5 0.0 collective-permute-done.3.rest_1_
  12.5 0.0 collective-permute-done.4.rest_2_
  12.5 0.7 %collective-permute-done.5.rest_3_ = f32[16,128]{1,0:T(8,128)S(1)} collective-permute-done((f32[16,128]{1,0:T(8,128)S(1)}, f32[16,128]{1,0:T(8,128)S(1)}, u32[]{:S(2)}, u32[]{:S(2)}) %collective-permute-start.5) | collective-permute-done | bytes 8224 | tf_op jit(solution)/shard_map/ppermute | solution.py:448
  13.2 0.7 %shard_map.45 = (f32[1,1152]{1,0:T(1,128)S(1)}, f32[32,256]{1,0:T(8,128)S(1)}) custom-call(f32[40,128]{1,0:T(8,128)S(1)} %get-tuple-element.35.left, f32[40,128]{1,0:T(8,128)S(1)} %get-tuple-element.36.right, f32[40,128]{1,0:T(8,128)S(1)} %get-tuple-element.37.left_halo, f32[40,128]{1,0:T(8,128)S(1)} %get-tuple-element.38.right_halo, ...), custom_call_target="tpu_custom_call" | custom-call | tf_op jit(solution)/shard_map/pallas_call | solution.py:18
  14.0 8.3 %all_to_all.5.parts = f32[16,1,1152]{2,1,0:T(1,128)S(1)} all-to-all(f32[16,1,1152]{2,1,0:T(1,128)S(1)} %broadcast_in_dim.3), channel_id=1, replica_groups={{6,0,4,8,12,1,5,9,13,2,10,14,3,7,11,15},{22,16,20,24,28,17,21,25,29,18,..., dimensions={0} | all-to-all | bytes 147456 | tf_op jit(solution)/shard_map/all_to_all | solution.py:508
  22.2 2.0 %shard_map.46 = (f32[32,8,512]{2,1,0:T(8,128)}, f32[32,32]{1,0:T(8,128)}) custom-call(bf16[4,96,512]{2,1,0:T(8,128)(2,1)S(1)} %get-tuple-element.26.inner_second, bf16[4,96,512]{2,1,0:T(8,128)(2,1)S(1)} %get-tuple-element.32.outer_second, f32[32,256]{1,0:T(8,128)S(1)} %get-tuple-element.44.edges, f32[16,1,1152]{2,1,0:T(1,128)S(1)} %all_to_all.5.parts), custom_call_target="tpu_custom_call" | custom-call | tf_op jit(solution)/shard_map/pallas_call | solution.py:18
  (2 shorter events, 0.1 us)
Async XLA Ops:
  2.0 9.5 %collective-permute-start = (f32[80,512]{1,0:T(8,128)S(1)}, f32[80,512]{1,0:T(8,128)S(1)}, u32[]{:S(2)}, u32[]{:S(2)}) collective-permute-start(f32[80,512]{1,0:T(8,128)S(1)} %get-tuple-element.27), channel_id=1, source_target_pairs={{0,16},{1,17},{2,18},{3,19},{4,8},{5,9},{6,10},{7,11},{8,4},{9,5},... | collective-permute-start | bytes 491528 | tf_op jit(solution)/shard_map/ppermute | solution.py:448
  5.1 1.6 %collective-permute-start.1 = (f32[72,512]{1,0:T(8,128)S(1)}, f32[72,512]{1,0:T(8,128)S(1)}, u32[]{:S(2)}, u32[]{:S(2)}) collective-permute-start(f32[72,512]{1,0:T(8,128)S(1)} %get-tuple-element.28), channel_id=1, source_target_pairs={{0,4},{1,5},{2,6},{3,7},{4,0},{5,1},{6,2},{7,3},{8,12},{9,13},{10,... | collective-permute-start | bytes 442376 | tf_op jit(solution)/shard_map/ppermute | solution.py:448
  5.2 7.4 %collective-permute-start.2 = (f32[16,128]{1,0:T(8,128)S(1)}, f32[16,128]{1,0:T(8,128)S(1)}, u32[]{:S(2)}, u32[]{:S(2)}) collective-permute-start(f32[16,128]{1,0:T(8,128)S(1)} %get-tuple-element.39), channel_id=1, source_target_pairs={{0,4},{1,17},{2,18},{3,7},{4,0},{5,10},{6,9},{7,3},{8,12},{9,6},{1... | collective-permute-start | bytes 24584 | tf_op jit(solution)/shard_map/ppermute | solution.py:448
  5.6 6.9 %collective-permute-start.3 = (f32[16,128]{1,0:T(8,128)S(1)}, f32[16,128]{1,0:T(8,128)S(1)}, u32[]{:S(2)}, u32[]{:S(2)}) collective-permute-start(f32[16,128]{1,0:T(8,128)S(1)} %get-tuple-element.40), channel_id=1, source_target_pairs={{0,16},{1,17},{2,18},{3,19},{4,9},{5,8},{6,11},{7,10},{8,5},{9,4},... | collective-permute-start | bytes 24584 | tf_op jit(solution)/shard_map/ppermute | solution.py:448
  6.9 5.7 %collective-permute-start.4 = (f32[16,128]{1,0:T(8,128)S(1)}, f32[16,128]{1,0:T(8,128)S(1)}, u32[]{:S(2)}, u32[]{:S(2)}) collective-permute-start(f32[16,128]{1,0:T(8,128)S(1)} %get-tuple-element.41), channel_id=1, source_target_pairs={{0,4},{1,2},{2,1},{3,7},{4,0},{5,6},{6,5},{7,3},{8,12},{9,10},{10,... | collective-permute-start | bytes 24584 | tf_op jit(solution)/shard_map/ppermute | solution.py:448
  9.5 3.7 %collective-permute-start.5 = (f32[16,128]{1,0:T(8,128)S(1)}, f32[16,128]{1,0:T(8,128)S(1)}, u32[]{:S(2)}, u32[]{:S(2)}) collective-permute-start(f32[16,128]{1,0:T(8,128)S(1)} %get-tuple-element.42), channel_id=1, source_target_pairs={{0,1},{1,0},{2,3},{3,2},{4,5},{5,4},{6,7},{7,6},{8,9},{9,8},{10,11... | collective-permute-start | bytes 24584 | tf_op jit(solution)/shard_map/ppermute | solution.py:448

commit v13 on v7

--- a/solution.py
+++ b/solution.py
@@ -338,8 +338,8 @@
     for step in range(planes):
         own, at = step // 8, step % 8
         column = columns[step]
-        root = lax.rsqrt(jnp.broadcast_to(column[own][at : at + 1], (8, LANES)))
-        inverse = root * root
+        pivot = jnp.broadcast_to(column[own][at : at + 1], (8, LANES))
+        inverse, root = pl.reciprocal(pivot, approx=False), lax.rsqrt(pivot)
         scale[own] = jnp.where(sub == at, root, scale[own])
         left = {g: jnp.where(sub > at, value, 0.0) if g == own else value for g, value in column.items()}
         factors = {g: value * inverse for g, value in left.items()}

time: 24.4 us -> 24.4 us (level)
  no operation moved by 1% of the time
where the time goes in v13:
time: 24.4 us; the launch traced here: 24.2 us
  starting transfers between devices  8.31 us (34%)
  blocking collectives  8.27 us (34%)
  Pallas kernels  6.26 us (26%)
  between operations  0.68 us (3%)
  waiting for transfers between devices  0.67 us (3%)
    ppermute x6, starting transfers between devices, swap(): return lax.ppermute(value, names, pairs)  8.31 us
    all_to_all x1, blocking collectives, on_device(): lax.all_to_all(grams, ('row', 'col'), 0, 0, axis_index_groups=[order], ti...  8.27 us
    pallas_call x6, Pallas kernels, call(): pl.pallas_call(kernel, out_shape=out_shapes, in_specs=[pl.BlockSpec(memor...  6.26 us
    ppermute x6, waiting for transfers between devices, swap(): return lax.ppermute(value, names, pairs)  0.67 us
  transfers between devices with their start and end apart: 6, of which 1 were waited for; matrix products, arithmetic and copies ran while one was open for 0% of the time, Pallas kernels for 9%

profile of v13, /device:TPU:0, one launch (start us, length us, event | category | flops | bytes accessed | tf_op | source)
XLA Modules:
  0.0 24.2 jit_solution(4117176761658194592)
XLA Ops:
  0.6 1.4 %shard_map.41 = (f32[8,32,512]{2,1,0:T(8,128)S(1)}, f32[8,8,512]{2,1,0:T(8,128)S(1)}, f32[40,128]{1,0:T(8,128)S(1)}, f32[40,128]{1,0:T(8,128)S(1)}, f32[80,512]{...) custom-call(f32[32,8,512]{2,1,0:T(8,128)} %sketch.1, f32[8,8,512]{2,1,0:T(8,128)} %weights.1), custom_call_target="tpu_custom_call" | custom-call | tf_op jit(solution)/shard_map/pallas_call | solution.py:18
  2.0 3.0 %collective-permute-start = (f32[80,512]{1,0:T(8,128)S(1)}, f32[80,512]{1,0:T(8,128)S(1)}, u32[]{:S(2)}, u32[]{:S(2)}) collective-permute-start(f32[80,512]{1,0:T(8,128)S(1)} %get-tuple-element.27), channel_id=1, source_target_pairs={{0,16},{1,17},{2,18},{3,19},{4,8},{5,9},{6,10},{7,11},{8,4},{9,5},... | collective-permute-start | bytes 491528 | tf_op jit(solution)/shard_map/ppermute | solution.py:445
  5.1 0.1 collective-permute-start.1
  5.2 0.4 %collective-permute-start.2 = (f32[16,128]{1,0:T(8,128)S(1)}, f32[16,128]{1,0:T(8,128)S(1)}, u32[]{:S(2)}, u32[]{:S(2)}) collective-permute-start(f32[16,128]{1,0:T(8,128)S(1)} %get-tuple-element.39), channel_id=1, source_target_pairs={{0,4},{1,17},{2,18},{3,7},{4,0},{5,10},{6,9},{7,3},{8,12},{9,6},{1... | collective-permute-start | bytes 24584 | tf_op jit(solution)/shard_map/ppermute | solution.py:445
  5.6 1.1 %collective-permute-start.3 = (f32[16,128]{1,0:T(8,128)S(1)}, f32[16,128]{1,0:T(8,128)S(1)}, u32[]{:S(2)}, u32[]{:S(2)}) collective-permute-start(f32[16,128]{1,0:T(8,128)S(1)} %get-tuple-element.40), channel_id=1, source_target_pairs={{0,16},{1,17},{2,18},{3,19},{4,9},{5,8},{6,11},{7,10},{8,5},{9,4},... | collective-permute-start | bytes 24584 | tf_op jit(solution)/shard_map/ppermute | solution.py:445
  6.7 0.0 collective-permute-done.1.second_message.bulk_message
  6.7 0.2 shard_map.44
  6.9 2.7 %collective-permute-start.4 = (f32[16,128]{1,0:T(8,128)S(1)}, f32[16,128]{1,0:T(8,128)S(1)}, u32[]{:S(2)}, u32[]{:S(2)}) collective-permute-start(f32[16,128]{1,0:T(8,128)S(1)} %get-tuple-element.41), channel_id=1, source_target_pairs={{0,4},{1,2},{2,1},{3,7},{4,0},{5,6},{6,5},{7,3},{8,12},{9,10},{10,... | collective-permute-start | bytes 24584 | tf_op jit(solution)/shard_map/ppermute | solution.py:445
  9.5 1.0 %collective-permute-start.5 = (f32[16,128]{1,0:T(8,128)S(1)}, f32[16,128]{1,0:T(8,128)S(1)}, u32[]{:S(2)}, u32[]{:S(2)}) collective-permute-start(f32[16,128]{1,0:T(8,128)S(1)} %get-tuple-element.42), channel_id=1, source_target_pairs={{0,1},{1,0},{2,3},{3,2},{4,5},{5,4},{6,7},{7,6},{8,9},{9,8},{10,11... | collective-permute-start | bytes 24584 | tf_op jit(solution)/shard_map/ppermute | solution.py:445
  10.5 1.0 %shard_map.42 = (f32[6,32,512]{2,1,0:T(8,128)S(1)}, bf16[4,96,512]{2,1,0:T(8,128)(2,1)S(1)}, f32[96,96]{1,0:T(8,128)S(1)}, f32[96,96]{1,0:T(8,128)S(1)}) custom-call(f32[8,32,512]{2,1,0:T(8,128)S(1)} %get-tuple-element.24.by_row, f32[8,8,512]{2,1,0:T(8,128)S(1)} %get-tuple-element.25.weights_by_row), custom_call_target="tpu_custom_call" | custom-call | tf_op jit(solution)/shard_map/pallas_call | solution.py:18
  11.6 0.0 collective-permute-done.first_message
  11.6 1.0 %shard_map.43 = (bf16[4,96,512]{2,1,0:T(8,128)(2,1)S(1)}, f32[32,64]{1,0:T(8,128)S(1)}, f32[40,128]{1,0:T(8,128)S(1)}, f32[40,128]{1,0:T(8,128)S(1)}) custom-call(f32[8,32,512]{2,1,0:T(8,128)S(1)} %get-tuple-element.24.by_row, f32[8,8,512]{2,1,0:T(8,128)S(1)} %get-tuple-element.25.weights_by_row, f32[80,512]{1,0:T(8,128)S(1)} %collective-permute-done.first_message, ...), custom_call_target="tpu_custom_call" | custom-call | tf_op jit(solution)/shard_map/pallas_call | solution.py:18
  12.5 0.0 collective-permute-done.2.rest_0_
  12.5 0.0 collective-permute-done.3.rest_1_
  12.5 0.0 collective-permute-done.4.rest_2_
  12.5 0.7 %collective-permute-done.5.rest_3_ = f32[16,128]{1,0:T(8,128)S(1)} collective-permute-done((f32[16,128]{1,0:T(8,128)S(1)}, f32[16,128]{1,0:T(8,128)S(1)}, u32[]{:S(2)}, u32[]{:S(2)}) %collective-permute-start.5) | collective-permute-done | bytes 8224 | tf_op jit(solution)/shard_map/ppermute | solution.py:445
  13.2 0.7 %shard_map.45 = (f32[16,1,1152]{2,1,0:T(1,128)S(1)}, f32[32,256]{1,0:T(8,128)S(1)}) custom-call(f32[40,128]{1,0:T(8,128)S(1)} %get-tuple-element.35.left, f32[40,128]{1,0:T(8,128)S(1)} %get-tuple-element.36.right, f32[40,128]{1,0:T(8,128)S(1)} %get-tuple-element.37.left_halo, f32[40,128]{1,0:T(8,128)S(1)} %get-tuple-element.38.right_halo, ...), custom_call_target="tpu_custom_call" | custom-call | tf_op jit(solution)/shard_map/pallas_call | solution.py:18
  13.9 8.3 %all_to_all.5.parts = f32[16,1,1152]{2,1,0:T(1,128)S(1)} all-to-all(f32[16,1,1152]{2,1,0:T(1,128)S(1)} %get-tuple-element.45), channel_id=1, replica_groups={{6,0,4,8,12,1,5,9,13,2,10,14,3,7,11,15},{22,16,20,24,28,17,21,25,29,18,..., dimensions={0} | all-to-all | bytes 147456 | tf_op jit(solution)/shard_map/all_to_all | solution.py:504
  22.2 2.0 %shard_map.46 = (f32[32,8,512]{2,1,0:T(8,128)}, f32[32,32]{1,0:T(8,128)}) custom-call(bf16[4,96,512]{2,1,0:T(8,128)(2,1)S(1)} %get-tuple-element.26.inner_second, bf16[4,96,512]{2,1,0:T(8,128)(2,1)S(1)} %get-tuple-element.32.outer_second, f32[32,256]{1,0:T(8,128)S(1)} %get-tuple-element.44.edges, f32[16,1,1152]{2,1,0:T(1,128)S(1)} %all_to_all.5.parts), custom_call_target="tpu_custom_call" | custom-call | tf_op jit(solution)/shard_map/pallas_call | solution.py:18
Async XLA Ops:
  2.0 9.5 %collective-permute-start = (f32[80,512]{1,0:T(8,128)S(1)}, f32[80,512]{1,0:T(8,128)S(1)}, u32[]{:S(2)}, u32[]{:S(2)}) collective-permute-start(f32[80,512]{1,0:T(8,128)S(1)} %get-tuple-element.27), channel_id=1, source_target_pairs={{0,16},{1,17},{2,18},{3,19},{4,8},{5,9},{6,10},{7,11},{8,4},{9,5},... | collective-permute-start | bytes 491528 | tf_op jit(solution)/shard_map/ppermute | solution.py:445
  5.1 1.6 %collective-permute-start.1 = (f32[72,512]{1,0:T(8,128)S(1)}, f32[72,512]{1,0:T(8,128)S(1)}, u32[]{:S(2)}, u32[]{:S(2)}) collective-permute-start(f32[72,512]{1,0:T(8,128)S(1)} %get-tuple-element.28), channel_id=1, source_target_pairs={{0,4},{1,5},{2,6},{3,7},{4,0},{5,1},{6,2},{7,3},{8,12},{9,13},{10,... | collective-permute-start | bytes 442376 | tf_op jit(solution)/shard_map/ppermute | solution.py:445
  5.2 7.4 %collective-permute-start.2 = (f32[16,128]{1,0:T(8,128)S(1)}, f32[16,128]{1,0:T(8,128)S(1)}, u32[]{:S(2)}, u32[]{:S(2)}) collective-permute-start(f32[16,128]{1,0:T(8,128)S(1)} %get-tuple-element.39), channel_id=1, source_target_pairs={{0,4},{1,17},{2,18},{3,7},{4,0},{5,10},{6,9},{7,3},{8,12},{9,6},{1... | collective-permute-start | bytes 24584 | tf_op jit(solution)/shard_map/ppermute | solution.py:445
  5.6 6.9 %collective-permute-start.3 = (f32[16,128]{1,0:T(8,128)S(1)}, f32[16,128]{1,0:T(8,128)S(1)}, u32[]{:S(2)}, u32[]{:S(2)}) collective-permute-start(f32[16,128]{1,0:T(8,128)S(1)} %get-tuple-element.40), channel_id=1, source_target_pairs={{0,16},{1,17},{2,18},{3,19},{4,9},{5,8},{6,11},{7,10},{8,5},{9,4},... | collective-permute-start | bytes 24584 | tf_op jit(solution)/shard_map/ppermute | solution.py:445
  6.9 5.7 %collective-permute-start.4 = (f32[16,128]{1,0:T(8,128)S(1)}, f32[16,128]{1,0:T(8,128)S(1)}, u32[]{:S(2)}, u32[]{:S(2)}) collective-permute-start(f32[16,128]{1,0:T(8,128)S(1)} %get-tuple-element.41), channel_id=1, source_target_pairs={{0,4},{1,2},{2,1},{3,7},{4,0},{5,6},{6,5},{7,3},{8,12},{9,10},{10,... | collective-permute-start | bytes 24584 | tf_op jit(solution)/shard_map/ppermute | solution.py:445
  9.5 3.7 %collective-permute-start.5 = (f32[16,128]{1,0:T(8,128)S(1)}, f32[16,128]{1,0:T(8,128)S(1)}, u32[]{:S(2)}, u32[]{:S(2)}) collective-permute-start(f32[16,128]{1,0:T(8,128)S(1)} %get-tuple-element.42), channel_id=1, source_target_pairs={{0,1},{1,0},{2,3},{3,2},{4,5},{5,4},{6,7},{7,6},{8,9},{9,8},{10,11... | collective-permute-start | bytes 24584 | tf_op jit(solution)/shard_map/ppermute | solution.py:445

commit v14 on v13

--- a/solution.py
+++ b/solution.py
@@ -177,8 +177,12 @@
     return products
 
 
-def inner_rows_kernel(by_row, weights_by_row, middle, second, first_products, second_products):
+def inner_rows_kernel(
+    by_row, weights_by_row, diagonal_message, middle, second, first_products, second_products, diagonal
+):
     rows = by_row.shape[0]
+    odd_row, has_below, has_above = sides_of("row")
+    diagonal[...] = jnp.where(jnp.where(odd_row, has_above, has_below), diagonal_message[...], 0.0)
     products = jnp.zeros(first_products.shape, jnp.float32)
     for row in range(1, rows - 1):
         image = apply_operator([by_row[row - 1], by_row[row], by_row[row + 1]], weights_by_row[row])
@@ -471,11 +475,14 @@
     from_cols = [swap(messages[at], col_pairing=at) for at in range(2)]
     parts_of = functools.partial(jax.ShapeDtypeStruct, dtype=jnp.bfloat16)
     products = f32(3 * planes, 3 * planes)
-    middle, inner_second, *inner_products = call(
+    middle, inner_second, *inner_products, from_diagonals[0] = call(
         inner_rows_kernel,
-        [f32(rows - 2, planes, width), parts_of((rows - 4, 3 * planes, width)), products, products],
+        [f32(rows - 2, planes, width), parts_of((rows - 4, 3 * planes, width)), products, products]
+        + [f32(16, LANES)],
         by_row,
         weights_by_row,
+        from_diagonals[0],
+        cost=pl.CostEstimate(flops=2000000000, bytes_accessed=4000000, transcendentals=0),
     )
     outer_second, early_grams, *halos = call(
         outer_rows_kernel,

time: 24.4 us -> 24.4 us (level)
  blocking collectives: 8.27 us -> 8.61 us
  waiting for transfers between devices: 0.67 us -> 0.34 us
    all_to_all x1, blocking collectives: 8.27 us -> 8.61 us  [on_device(): lax.all_to_all(grams, ('row', 'col'), 0, 0, axis_index_groups=[order], ti...]
    ppermute x6, waiting for transfers between devices: 0.67 us -> 0.34 us  [swap(): return lax.ppermute(value, names, pairs)]
where the time goes in v14:
time: 24.4 us; the launch traced here: 24.2 us
  blocking collectives  8.61 us (35%)
  starting transfers between devices  8.31 us (34%)
  Pallas kernels  6.26 us (26%)
  between operations  0.67 us (3%)
  waiting for transfers between devices  0.34 us (1%)
    all_to_all x1, blocking collectives, on_device(): lax.all_to_all(grams, ('row', 'col'), 0, 0, axis_index_groups=[order], ti...  8.61 us
    ppermute x6, starting transfers between devices, swap(): return lax.ppermute(value, names, pairs)  8.31 us
    pallas_call x6, Pallas kernels, call(): pl.pallas_call(kernel, out_shape=out_shapes, in_specs=[pl.BlockSpec(memor...  6.26 us
  transfers between devices with their start and end apart: 6, of which 1 were waited for; matrix products, arithmetic and copies ran while one was open for 0% of the time, Pallas kernels for 9%

profile of v14, /device:TPU:0, one launch (start us, length us, event | category | flops | bytes accessed | tf_op | source)
XLA Modules:
  0.0 24.2 jit_solution(3419796611741376024)
XLA Ops:
  0.6 1.4 %shard_map.41 = (f32[8,32,512]{2,1,0:T(8,128)S(1)}, f32[8,8,512]{2,1,0:T(8,128)S(1)}, f32[40,128]{1,0:T(8,128)S(1)}, f32[40,128]{1,0:T(8,128)S(1)}, f32[80,512]{...) custom-call(f32[32,8,512]{2,1,0:T(8,128)} %sketch.1, f32[8,8,512]{2,1,0:T(8,128)} %weights.1), custom_call_target="tpu_custom_call" | custom-call | tf_op jit(solution)/shard_map/pallas_call | solution.py:18
  2.0 0.5 %collective-permute-start.2 = (f32[72,512]{1,0:T(8,128)S(1)}, f32[72,512]{1,0:T(8,128)S(1)}, u32[]{:S(2)}, u32[]{:S(2)}) collective-permute-start(f32[72,512]{1,0:T(8,128)S(1)} %get-tuple-element.30), channel_id=1, source_target_pairs={{0,4},{1,5},{2,6},{3,7},{4,0},{5,1},{6,2},{7,3},{8,12},{9,13},{10,... | collective-permute-start | bytes 442376 | tf_op jit(solution)/shard_map/ppermute | solution.py:449
  2.6 0.1 collective-permute-start
  2.6 2.9 %collective-permute-start.1 = (f32[80,512]{1,0:T(8,128)S(1)}, f32[80,512]{1,0:T(8,128)S(1)}, u32[]{:S(2)}, u32[]{:S(2)}) collective-permute-start(f32[80,512]{1,0:T(8,128)S(1)} %get-tuple-element.29), channel_id=1, source_target_pairs={{0,16},{1,17},{2,18},{3,19},{4,8},{5,9},{6,10},{7,11},{8,4},{9,5},... | collective-permute-start | bytes 491528 | tf_op jit(solution)/shard_map/ppermute | solution.py:449
  5.6 0.0 collective-permute-start.3
  5.6 0.0 collective-permute-done.2.second_message.bulk_message
  5.6 0.2 shard_map.44
  5.8 3.4 %collective-permute-start.4 = (f32[16,128]{1,0:T(8,128)S(1)}, f32[16,128]{1,0:T(8,128)S(1)}, u32[]{:S(2)}, u32[]{:S(2)}) collective-permute-start(f32[16,128]{1,0:T(8,128)S(1)} %get-tuple-element.43), channel_id=1, source_target_pairs={{0,4},{1,2},{2,1},{3,7},{4,0},{5,6},{6,5},{7,3},{8,12},{9,10},{10,... | collective-permute-start | bytes 24584 | tf_op jit(solution)/shard_map/ppermute | solution.py:449
  9.2 1.3 %collective-permute-start.5 = (f32[16,128]{1,0:T(8,128)S(1)}, f32[16,128]{1,0:T(8,128)S(1)}, u32[]{:S(2)}, u32[]{:S(2)}) collective-permute-start(f32[16,128]{1,0:T(8,128)S(1)} %get-tuple-element.44), channel_id=1, source_target_pairs={{0,1},{1,0},{2,3},{3,2},{4,5},{5,4},{6,7},{7,6},{8,9},{9,8},{10,11... | collective-permute-start | bytes 24584 | tf_op jit(solution)/shard_map/ppermute | solution.py:449
  10.5 0.0 collective-permute-done.diagonal_message
  10.5 1.0 %shard_map.42 = (f32[6,32,512]{2,1,0:T(8,128)S(1)}, bf16[4,96,512]{2,1,0:T(8,128)(2,1)S(1)}, f32[96,96]{1,0:T(8,128)S(1)}, f32[96,96]{1,0:T(8,128)S(1)}, f32[16,128]{1,0:T(8,128)S(1)}) custom-call(f32[8,32,512]{2,1,0:T(8,128)S(1)} %get-tuple-element.25.by_row, f32[8,8,512]{2,1,0:T(8,128)S(1)} %get-tuple-element.26.weights_by_row, ...), custom_call_target="tpu_custom_call" | custom-call | flops 2000000000 | bytes 4000000 | tf_op jit(solution)/shard_map/pallas_call | solution.py:18
  11.6 0.0 collective-permute-done.1.first_message
  11.6 1.0 %shard_map.43 = (bf16[4,96,512]{2,1,0:T(8,128)(2,1)S(1)}, f32[32,64]{1,0:T(8,128)S(1)}, f32[40,128]{1,0:T(8,128)S(1)}, f32[40,128]{1,0:T(8,128)S(1)}) custom-call(f32[8,32,512]{2,1,0:T(8,128)S(1)} %get-tuple-element.25.by_row, f32[8,8,512]{2,1,0:T(8,128)S(1)} %get-tuple-element.26.weights_by_row, f32[80,512]{1,0:T(8,128)S(1)} %collective-permute-done.1.first_message, ...), custom_call_target="tpu_custom_call" | custom-call | tf_op jit(solution)/shard_map/pallas_call | solution.py:18
  12.5 0.0 collective-permute-done.3.rest_1_
  12.5 0.0 collective-permute-done.4.rest_2_
  12.5 0.3 %collective-permute-done.5.rest_3_ = f32[16,128]{1,0:T(8,128)S(1)} collective-permute-done((f32[16,128]{1,0:T(8,128)S(1)}, f32[16,128]{1,0:T(8,128)S(1)}, u32[]{:S(2)}, u32[]{:S(2)}) %collective-permute-start.5) | collective-permute-done | bytes 8224 | tf_op jit(solution)/shard_map/ppermute | solution.py:449
  12.8 0.7 %shard_map.45 = (f32[16,1,1152]{2,1,0:T(1,128)S(1)}, f32[32,256]{1,0:T(8,128)S(1)}) custom-call(f32[40,128]{1,0:T(8,128)S(1)} %get-tuple-element.37.left, f32[40,128]{1,0:T(8,128)S(1)} %get-tuple-element.38.right, f32[40,128]{1,0:T(8,128)S(1)} %get-tuple-element.39.left_halo, f32[40,128]{1,0:T(8,128)S(1)} %get-tuple-element.40.right_halo, ...), custom_call_target="tpu_custom_call" | custom-call | tf_op jit(solution)/shard_map/pallas_call | solution.py:18
  13.6 8.6 %all_to_all.5.parts = f32[16,1,1152]{2,1,0:T(1,128)S(1)} all-to-all(f32[16,1,1152]{2,1,0:T(1,128)S(1)} %get-tuple-element.47), channel_id=1, replica_groups={{6,0,4,8,12,1,5,9,13,2,10,14,3,7,11,15},{22,16,20,24,28,17,21,25,29,18,..., dimensions={0} | all-to-all | bytes 147456 | tf_op jit(solution)/shard_map/all_to_all | solution.py:511
  22.2 2.0 %shard_map.46 = (f32[32,8,512]{2,1,0:T(8,128)}, f32[32,32]{1,0:T(8,128)}) custom-call(bf16[4,96,512]{2,1,0:T(8,128)(2,1)S(1)} %get-tuple-element.28.inner_second, bf16[4,96,512]{2,1,0:T(8,128)(2,1)S(1)} %get-tuple-element.34.outer_second, f32[32,256]{1,0:T(8,128)S(1)} %get-tuple-element.46.edges, f32[16,1,1152]{2,1,0:T(1,128)S(1)} %all_to_all.5.parts), custom_call_target="tpu_custom_call" | custom-call | tf_op jit(solution)/shard_map/pallas_call | solution.py:18
Async XLA Ops:
  2.0 3.6 %collective-permute-start.2 = (f32[72,512]{1,0:T(8,128)S(1)}, f32[72,512]{1,0:T(8,128)S(1)}, u32[]{:S(2)}, u32[]{:S(2)}) collective-permute-start(f32[72,512]{1,0:T(8,128)S(1)} %get-tuple-element.30), channel_id=1, source_target_pairs={{0,4},{1,5},{2,6},{3,7},{4,0},{5,1},{6,2},{7,3},{8,12},{9,13},{10,... | collective-permute-start | bytes 442376 | tf_op jit(solution)/shard_map/ppermute | solution.py:449
  2.6 8.0 %collective-permute-start = (f32[16,128]{1,0:T(8,128)S(1)}, f32[16,128]{1,0:T(8,128)S(1)}, u32[]{:S(2)}, u32[]{:S(2)}) collective-permute-start(f32[16,128]{1,0:T(8,128)S(1)} %get-tuple-element.27), channel_id=1, source_target_pairs={{0,4},{1,17},{2,18},{3,7},{4,0},{5,10},{6,9},{7,3},{8,12},{9,6},{1... | collective-permute-start | bytes 24584 | tf_op jit(solution)/shard_map/ppermute | solution.py:449
  2.6 8.9 %collective-permute-start.1 = (f32[80,512]{1,0:T(8,128)S(1)}, f32[80,512]{1,0:T(8,128)S(1)}, u32[]{:S(2)}, u32[]{:S(2)}) collective-permute-start(f32[80,512]{1,0:T(8,128)S(1)} %get-tuple-element.29), channel_id=1, source_target_pairs={{0,16},{1,17},{2,18},{3,19},{4,8},{5,9},{6,10},{7,11},{8,4},{9,5},... | collective-permute-start | bytes 491528 | tf_op jit(solution)/shard_map/ppermute | solution.py:449
  5.6 6.9 %collective-permute-start.3 = (f32[16,128]{1,0:T(8,128)S(1)}, f32[16,128]{1,0:T(8,128)S(1)}, u32[]{:S(2)}, u32[]{:S(2)}) collective-permute-start(f32[16,128]{1,0:T(8,128)S(1)} %get-tuple-element.42), channel_id=1, source_target_pairs={{0,16},{1,17},{2,18},{3,19},{4,9},{5,8},{6,11},{7,10},{8,5},{9,4},... | collective-permute-start | bytes 24584 | tf_op jit(solution)/shard_map/ppermute | solution.py:449
  5.8 6.7 %collective-permute-start.4 = (f32[16,128]{1,0:T(8,128)S(1)}, f32[16,128]{1,0:T(8,128)S(1)}, u32[]{:S(2)}, u32[]{:S(2)}) collective-permute-start(f32[16,128]{1,0:T(8,128)S(1)} %get-tuple-element.43), channel_id=1, source_target_pairs={{0,4},{1,2},{2,1},{3,7},{4,0},{5,6},{6,5},{7,3},{8,12},{9,10},{10,... | collective-permute-start | bytes 24584 | tf_op jit(solution)/shard_map/ppermute | solution.py:449
  9.2 3.7 %collective-permute-start.5 = (f32[16,128]{1,0:T(8,128)S(1)}, f32[16,128]{1,0:T(8,128)S(1)}, u32[]{:S(2)}, u32[]{:S(2)}) collective-permute-start(f32[16,128]{1,0:T(8,128)S(1)} %get-tuple-element.44), channel_id=1, source_target_pairs={{0,1},{1,0},{2,3},{3,2},{4,5},{5,4},{6,7},{7,6},{8,9},{9,8},{10,11... | collective-permute-start | bytes 24584 | tf_op jit(solution)/shard_map/ppermute | solution.py:449

commit v15 on v14

--- a/solution.py
+++ b/solution.py
@@ -100,7 +100,7 @@
         totals = [total + jnp.where(present, part, 0.0) for total, part in zip(totals, parts)]
     left[...], right[...] = totals
     to_left, to_right = folded(left[...], 2), folded(right[...], PITCH - 4)
-    for message, up in zip(col_messages, (odd_col, jnp.logical_not(odd_col))):
+    for message, up in zip(col_messages, (jnp.logical_not(odd_col), odd_col)):
         message[...] = jnp.where(up, to_right, to_left)
 
 
@@ -274,7 +274,7 @@
 
 
 def late_kernel(rows, left, right, left_halo, right_halo, *rest):
-    diagonal_messages, col_messages, (early_grams, grams, edges) = rest[:2], rest[2:4], rest[4:]
+    diagonal_messages, col_messages, (early_grams, grams, edges) = rest[:2], rest[3:1:-1], rest[4:]
     planes = early_grams.shape[0]
     odd_row, has_below, has_above = sides_of("row")
     odd_col, has_left, has_right = sides_of("col")
@@ -472,16 +472,16 @@
     left, right, *messages = call(
         functools.partial(strips_kernel, rows), [side, side] + [f32(16, LANES)] * 2, left, right, from_rows[1]
     )
-    from_cols = [swap(messages[at], col_pairing=at) for at in range(2)]
+    from_cols = [swap(messages[1 - at], col_pairing=at) for at in (1, 0)]
     parts_of = functools.partial(jax.ShapeDtypeStruct, dtype=jnp.bfloat16)
     products = f32(3 * planes, 3 * planes)
-    middle, inner_second, *inner_products, from_diagonals[0] = call(
+    middle, inner_second, *inner_products, from_diagonals[1] = call(
         inner_rows_kernel,
         [f32(rows - 2, planes, width), parts_of((rows - 4, 3 * planes, width)), products, products]
         + [f32(16, LANES)],
         by_row,
         weights_by_row,
-        from_diagonals[0],
+        from_diagonals[1],
         cost=pl.CostEstimate(flops=2000000000, bytes_accessed=4000000, transcendentals=0),
     )
     outer_second, early_grams, *halos = call(

time: 24.4 us -> 24.2 us (level)
  waiting for transfers between devices: 0.34 us -> 0.02 us
    ppermute x6, waiting for transfers between devices: 0.34 us -> 0.02 us  [swap(): return lax.ppermute(value, names, pairs)]
  transfers between devices with their start and end apart: 6 -> 6, of which waited for: 1 -> 0; matrix products, arithmetic and copies ran while one was open for 0% -> 0% of each run, Pallas kernels for 9% -> 9%
where the time goes in v15:
time: 24.2 us; the launch traced here: 24.1 us
  blocking collectives  8.82 us (36%)
  starting transfers between devices  8.28 us (34%)
  Pallas kernels  6.27 us (26%)
  between operations  0.68 us (3%)
    all_to_all x1, blocking collectives, on_device(): lax.all_to_all(grams, ('row', 'col'), 0, 0, axis_index_groups=[order], ti...  8.82 us
    ppermute x6, starting transfers between devices, swap(): return lax.ppermute(value, names, pairs)  8.28 us
    pallas_call x6, Pallas kernels, call(): pl.pallas_call(kernel, out_shape=out_shapes, in_specs=[pl.BlockSpec(memor...  6.27 us
  transfers between devices with their start and end apart: 6, of which 0 were waited for; matrix products, arithmetic and copies ran while one was open for 0% of the time, Pallas kernels for 9%

profile of v15, /device:TPU:0, one launch (start us, length us, event | category | flops | bytes accessed | tf_op | source)
XLA Modules:
  0.0 24.1 jit_solution(9074651203620955158)
XLA Ops:
  0.6 1.4 %shard_map.41 = (f32[8,32,512]{2,1,0:T(8,128)S(1)}, f32[8,8,512]{2,1,0:T(8,128)S(1)}, f32[40,128]{1,0:T(8,128)S(1)}, f32[40,128]{1,0:T(8,128)S(1)}, f32[80,512]{...) custom-call(f32[32,8,512]{2,1,0:T(8,128)} %sketch.1, f32[8,8,512]{2,1,0:T(8,128)} %weights.1), custom_call_target="tpu_custom_call" | custom-call | tf_op jit(solution)/shard_map/pallas_call | solution.py:18
  2.0 0.5 %collective-permute-start.2 = (f32[72,512]{1,0:T(8,128)S(1)}, f32[72,512]{1,0:T(8,128)S(1)}, u32[]{:S(2)}, u32[]{:S(2)}) collective-permute-start(f32[72,512]{1,0:T(8,128)S(1)} %get-tuple-element.30), channel_id=1, source_target_pairs={{0,4},{1,5},{2,6},{3,7},{4,0},{5,1},{6,2},{7,3},{8,12},{9,13},{10,... | collective-permute-start | bytes 442376 | tf_op jit(solution)/shard_map/ppermute | solution.py:449
  2.6 2.6 %collective-permute-start = (f32[16,128]{1,0:T(8,128)S(1)}, f32[16,128]{1,0:T(8,128)S(1)}, u32[]{:S(2)}, u32[]{:S(2)}) collective-permute-start(f32[16,128]{1,0:T(8,128)S(1)} %get-tuple-element.27), channel_id=1, source_target_pairs={{0,16},{1,17},{2,18},{3,19},{4,9},{5,8},{6,11},{7,10},{8,5},{9,4},... | collective-permute-start | bytes 24584 | tf_op jit(solution)/shard_map/ppermute | solution.py:449
  5.2 0.1 collective-permute-start.1
  5.2 1.6 %collective-permute-start.3 = (f32[16,128]{1,0:T(8,128)S(1)}, f32[16,128]{1,0:T(8,128)S(1)}, u32[]{:S(2)}, u32[]{:S(2)}) collective-permute-start(f32[16,128]{1,0:T(8,128)S(1)} %get-tuple-element.41), channel_id=1, source_target_pairs={{0,4},{1,17},{2,18},{3,7},{4,0},{5,10},{6,9},{7,3},{8,12},{9,6},{1... | collective-permute-start | bytes 24584 | tf_op jit(solution)/shard_map/ppermute | solution.py:449
  6.8 0.0 collective-permute-done.2.second_message.bulk_message
  6.8 0.2 shard_map.44
  7.0 1.9 %collective-permute-start.4 = (f32[16,128]{1,0:T(8,128)S(1)}, f32[16,128]{1,0:T(8,128)S(1)}, u32[]{:S(2)}, u32[]{:S(2)}) collective-permute-start(f32[16,128]{1,0:T(8,128)S(1)} %get-tuple-element.43), channel_id=1, source_target_pairs={{0,1},{1,0},{2,3},{3,2},{4,5},{5,4},{6,7},{7,6},{8,9},{9,8},{10,11... | collective-permute-start | bytes 24584 | tf_op jit(solution)/shard_map/ppermute | solution.py:449
  8.9 1.6 %collective-permute-start.5 = (f32[16,128]{1,0:T(8,128)S(1)}, f32[16,128]{1,0:T(8,128)S(1)}, u32[]{:S(2)}, u32[]{:S(2)}) collective-permute-start(f32[16,128]{1,0:T(8,128)S(1)} %get-tuple-element.44), channel_id=1, source_target_pairs={{0,4},{1,2},{2,1},{3,7},{4,0},{5,6},{6,5},{7,3},{8,12},{9,10},{10,... | collective-permute-start | bytes 24584 | tf_op jit(solution)/shard_map/ppermute | solution.py:449
  10.5 0.0 collective-permute-done.diagonal_message
  10.5 1.0 %shard_map.42 = (f32[6,32,512]{2,1,0:T(8,128)S(1)}, bf16[4,96,512]{2,1,0:T(8,128)(2,1)S(1)}, f32[96,96]{1,0:T(8,128)S(1)}, f32[96,96]{1,0:T(8,128)S(1)}, f32[16,128]{1,0:T(8,128)S(1)}) custom-call(f32[8,32,512]{2,1,0:T(8,128)S(1)} %get-tuple-element.25.by_row, f32[8,8,512]{2,1,0:T(8,128)S(1)} %get-tuple-element.26.weights_by_row, ...), custom_call_target="tpu_custom_call" | custom-call | flops 2000000000 | bytes 4000000 | tf_op jit(solution)/shard_map/pallas_call | solution.py:18
  11.5 0.0 collective-permute-done.1.first_message
  11.5 1.0 %shard_map.43 = (bf16[4,96,512]{2,1,0:T(8,128)(2,1)S(1)}, f32[32,64]{1,0:T(8,128)S(1)}, f32[40,128]{1,0:T(8,128)S(1)}, f32[40,128]{1,0:T(8,128)S(1)}) custom-call(f32[8,32,512]{2,1,0:T(8,128)S(1)} %get-tuple-element.25.by_row, f32[8,8,512]{2,1,0:T(8,128)S(1)} %get-tuple-element.26.weights_by_row, f32[80,512]{1,0:T(8,128)S(1)} %collective-permute-done.1.first_message, ...), custom_call_target="tpu_custom_call" | custom-call | tf_op jit(solution)/shard_map/pallas_call | solution.py:18
  12.5 0.0 collective-permute-done.3.rest_0_
  12.5 0.0 collective-permute-done.4.rest_2_
  12.5 0.0 collective-permute-done.5.rest_3_
  12.5 0.7 %shard_map.45 = (f32[16,1,1152]{2,1,0:T(1,128)S(1)}, f32[32,256]{1,0:T(8,128)S(1)}) custom-call(f32[40,128]{1,0:T(8,128)S(1)} %get-tuple-element.37.left, f32[40,128]{1,0:T(8,128)S(1)} %get-tuple-element.38.right, f32[40,128]{1,0:T(8,128)S(1)} %get-tuple-element.39.left_halo, f32[40,128]{1,0:T(8,128)S(1)} %get-tuple-element.40.right_halo, ...), custom_call_target="tpu_custom_call" | custom-call | tf_op jit(solution)/shard_map/pallas_call | solution.py:18
  13.2 8.8 %all_to_all.5.parts = f32[16,1,1152]{2,1,0:T(1,128)S(1)} all-to-all(f32[16,1,1152]{2,1,0:T(1,128)S(1)} %get-tuple-element.47), channel_id=1, replica_groups={{6,0,4,8,12,1,5,9,13,2,10,14,3,7,11,15},{22,16,20,24,28,17,21,25,29,18,..., dimensions={0} | all-to-all | bytes 147456 | tf_op jit(solution)/shard_map/all_to_all | solution.py:511
  22.1 2.0 %shard_map.46 = (f32[32,8,512]{2,1,0:T(8,128)}, f32[32,32]{1,0:T(8,128)}) custom-call(bf16[4,96,512]{2,1,0:T(8,128)(2,1)S(1)} %get-tuple-element.28.inner_second, bf16[4,96,512]{2,1,0:T(8,128)(2,1)S(1)} %get-tuple-element.34.outer_second, f32[32,256]{1,0:T(8,128)S(1)} %get-tuple-element.46.edges, f32[16,1,1152]{2,1,0:T(1,128)S(1)} %all_to_all.5.parts), custom_call_target="tpu_custom_call" | custom-call | tf_op jit(solution)/shard_map/pallas_call | solution.py:18
Async XLA Ops:
  2.0 4.8 %collective-permute-start.2 = (f32[72,512]{1,0:T(8,128)S(1)}, f32[72,512]{1,0:T(8,128)S(1)}, u32[]{:S(2)}, u32[]{:S(2)}) collective-permute-start(f32[72,512]{1,0:T(8,128)S(1)} %get-tuple-element.30), channel_id=1, source_target_pairs={{0,4},{1,5},{2,6},{3,7},{4,0},{5,1},{6,2},{7,3},{8,12},{9,13},{10,... | collective-permute-start | bytes 442376 | tf_op jit(solution)/shard_map/ppermute | solution.py:449
  2.6 7.9 %collective-permute-start = (f32[16,128]{1,0:T(8,128)S(1)}, f32[16,128]{1,0:T(8,128)S(1)}, u32[]{:S(2)}, u32[]{:S(2)}) collective-permute-start(f32[16,128]{1,0:T(8,128)S(1)} %get-tuple-element.27), channel_id=1, source_target_pairs={{0,16},{1,17},{2,18},{3,19},{4,9},{5,8},{6,11},{7,10},{8,5},{9,4},... | collective-permute-start | bytes 24584 | tf_op jit(solution)/shard_map/ppermute | solution.py:449
  5.2 6.4 %collective-permute-start.1 = (f32[80,512]{1,0:T(8,128)S(1)}, f32[80,512]{1,0:T(8,128)S(1)}, u32[]{:S(2)}, u32[]{:S(2)}) collective-permute-start(f32[80,512]{1,0:T(8,128)S(1)} %get-tuple-element.29), channel_id=1, source_target_pairs={{0,16},{1,17},{2,18},{3,19},{4,8},{5,9},{6,10},{7,11},{8,4},{9,5},... | collective-permute-start | bytes 491528 | tf_op jit(solution)/shard_map/ppermute | solution.py:449
  5.2 7.3 %collective-permute-start.3 = (f32[16,128]{1,0:T(8,128)S(1)}, f32[16,128]{1,0:T(8,128)S(1)}, u32[]{:S(2)}, u32[]{:S(2)}) collective-permute-start(f32[16,128]{1,0:T(8,128)S(1)} %get-tuple-element.41), channel_id=1, source_target_pairs={{0,4},{1,17},{2,18},{3,7},{4,0},{5,10},{6,9},{7,3},{8,12},{9,6},{1... | collective-permute-start | bytes 24584 | tf_op jit(solution)/shard_map/ppermute | solution.py:449
  7.0 5.5 %collective-permute-start.4 = (f32[16,128]{1,0:T(8,128)S(1)}, f32[16,128]{1,0:T(8,128)S(1)}, u32[]{:S(2)}, u32[]{:S(2)}) collective-permute-start(f32[16,128]{1,0:T(8,128)S(1)} %get-tuple-element.43), channel_id=1, source_target_pairs={{0,1},{1,0},{2,3},{3,2},{4,5},{5,4},{6,7},{7,6},{8,9},{9,8},{10,11... | collective-permute-start | bytes 24584 | tf_op jit(solution)/shard_map/ppermute | solution.py:449
  8.9 3.6 %collective-permute-start.5 = (f32[16,128]{1,0:T(8,128)S(1)}, f32[16,128]{1,0:T(8,128)S(1)}, u32[]{:S(2)}, u32[]{:S(2)}) collective-permute-start(f32[16,128]{1,0:T(8,128)S(1)} %get-tuple-element.44), channel_id=1, source_target_pairs={{0,4},{1,2},{2,1},{3,7},{4,0},{5,6},{6,5},{7,3},{8,12},{9,10},{10,... | collective-permute-start | bytes 24584 | tf_op jit(solution)/shard_map/ppermute | solution.py:449

commit v16 on v15

--- a/solution.py
+++ b/solution.py
@@ -177,90 +177,86 @@
     return products
 
 
+def side_rows(above, present, message, by_row, weights_by_row, middle, products):
+    rows, planes, _ = by_row.shape
+
+    def pick(high, low):
+        return jnp.where(above, high, low)
+
+    halo = jnp.where(present, message[: 2 * planes + 8], 0.0)
+    one, other, halo_weights = halo[:planes], halo[planes : 2 * planes], halo[2 * planes :]
+    near, far = pick(one, other), pick(other, one)
+    edge, inside = pick(by_row[rows - 1], by_row[0]), pick(by_row[rows - 2], by_row[1])
+    edge_weights = pick(weights_by_row[rows - 1], weights_by_row[0])
+    inside_weights = pick(weights_by_row[rows - 2], weights_by_row[1])
+    first_near = apply_operator([pick(edge, far), near, pick(far, edge)], halo_weights)
+    first_edge = apply_operator([pick(inside, near), edge, pick(near, inside)], edge_weights)
+    last = middle.shape[0] - 1
+    first_inside, first_next = pick(middle[last], middle[0]), pick(middle[last - 1], middle[1])
+    rows3 = [pick(first_inside, first_near), first_edge, pick(first_near, first_inside)]
+    second_edge = inner_parts(apply_operator(rows3, edge_weights))
+    rows3 = [pick(first_next, first_edge), first_inside, pick(first_edge, first_next)]
+    second_inside = inner_parts(apply_operator(rows3, inside_weights))
+    first, second = products
+    first = first + products_of(inner_parts(first_edge))
+    second = second + products_of(second_edge) + products_of(second_inside)
+    return (second_edge, second_inside), (first, second)
+
+
 def inner_rows_kernel(
-    by_row, weights_by_row, diagonal_message, middle, second, first_products, second_products, diagonal
+    by_row, weights_by_row, diagonal_message, message, middle, second, side, first_products, second_products, diagonal
 ):
     rows = by_row.shape[0]
     odd_row, has_below, has_above = sides_of("row")
     diagonal[...] = jnp.where(jnp.where(odd_row, has_above, has_below), diagonal_message[...], 0.0)
-    products = jnp.zeros(first_products.shape, jnp.float32)
+    first = jnp.zeros(first_products.shape, jnp.float32)
     for row in range(1, rows - 1):
         image = apply_operator([by_row[row - 1], by_row[row], by_row[row + 1]], weights_by_row[row])
         middle[row - 1] = image
-        products = products + products_of(inner_parts(image))
-    first_products[...] = products
-    second_products[...] = images_of(
+        first = first + products_of(inner_parts(image))
+    products = first, images_of(
         lambda row: middle[row - 1],
         lambda row: weights_by_row[row],
         range(2, rows - 2),
         second,
         jnp.zeros(second_products.shape, jnp.float32),
     )
+    above, present = jnp.logical_not(odd_row), jnp.where(odd_row, has_below, has_above)
+    parts, products = side_rows(above, present, message, by_row, weights_by_row, middle, products)
+    side[0], side[1] = parts
+    first_products[...], second_products[...] = products
 
 
 def outer_rows_kernel(
     by_row,
     weights_by_row,
-    first_message,
-    second_message,
+    message,
     middle,
+    side,
     first_products,
     second_products,
     second,
     grams,
     left_halo,
     right_halo,
-    outer,
 ):
     rows, planes, width = by_row.shape
     odd_row, has_below, has_above = sides_of("row")
-    one, other = first_message[: 2 * planes + 8], second_message[...]
-    below = jnp.where(has_below, jnp.where(odd_row, other, one), 0.0)
-    above = jnp.where(has_above, jnp.where(odd_row, one, other), 0.0)
-    halos = [None, None]
-    for side, (halo, present) in enumerate(
-        ((below, jnp.logical_not(odd_row)), (above, odd_row))
-    ):
-        for slot in range(2):
-            index = slot if side == 0 else rows + 2 + slot
-            blank = jnp.zeros((8, width), jnp.float32)
-            weight = halo[2 * planes :] if slot != side else blank
-            row_values = jnp.concatenate([halo[slot * planes : (slot + 1) * planes], weight], axis=0)
-            parts = edge_columns(row_values[:, :LANES], row_values[:, width - LANES :], PITCH * index)
-            parts = [jnp.where(present, part, 0.0) for part in parts]
-            halos = [part if total is None else total + part for total, part in zip(halos, parts)]
+    present = jnp.where(odd_row, has_above, has_below)
+    halo = jnp.where(present, message[: 2 * planes + 8], 0.0)
+    halos = [jnp.zeros(left_halo.shape, jnp.float32)] * 2
+    for slot in range(2):
+        place = PITCH * (slot + jnp.where(odd_row, rows + 2, 0))
+        first = jnp.concatenate([halo[slot * planes : (slot + 1) * planes], halo[2 * planes :]], axis=0)
+        parts = edge_columns(first[:, :LANES], first[:, width - LANES :], place)
+        halos = [total + part for total, part in zip(halos, parts)]
     left_halo[...], right_halo[...] = halos
-
-    def field(row):
-        if 0 <= row < rows:
-            return by_row[row]
-        at = (row + 2 if row < 0 else row - rows) * planes
-        return (below if row < 0 else above)[at : at + planes]
-
-    def weights(row):
-        if 0 <= row < rows:
-            return weights_by_row[row]
-        return (below if row < 0 else above)[2 * planes :]
-
-    products = first_products[...]
-    places = (-1, 0, rows - 1, rows)
-    for at, row in enumerate(places):
-        image = apply_operator([field(row - 1), field(row), field(row + 1)], weights(row))
-        outer[at] = image
-        if 0 <= row < rows:
-            products = products + products_of(inner_parts(image))
-    both = [products]
-    both.append(
-        images_of(
-            lambda row: outer[places.index(row)] if row in places else middle[row - 1],
-            weights,
-            (0, 1, rows - 2, rows - 1),
-            second,
-            second_products[...],
-        )
-    )
-    for at, products in enumerate(both):
-        some = products[:planes] + products[planes : 2 * planes] + products[2 * planes :]
+    products = first_products[...], second_products[...]
+    parts, products = side_rows(odd_row, present, message, by_row, weights_by_row, middle, products)
+    second[jnp.where(odd_row, 3, 0)], second[jnp.where(odd_row, 2, 1)] = parts
+    second[jnp.where(odd_row, 0, 3)], second[jnp.where(odd_row, 1, 2)] = side[0], side[1]
+    for at, both in enumerate(products):
+        some = both[:planes] + both[planes : 2 * planes] + both[2 * planes :]
         total = some[:, :planes] + some[:, planes : 2 * planes] + some[:, 2 * planes :]
         grams[:, at * planes : (at + 1) * planes] = total
 
@@ -475,24 +471,25 @@
     from_cols = [swap(messages[1 - at], col_pairing=at) for at in (1, 0)]
     parts_of = functools.partial(jax.ShapeDtypeStruct, dtype=jnp.bfloat16)
     products = f32(3 * planes, 3 * planes)
-    middle, inner_second, *inner_products, from_diagonals[1] = call(
+    middle, inner_second, side_second, *inner_products, from_diagonals[1] = call(
         inner_rows_kernel,
-        [f32(rows - 2, planes, width), parts_of((rows - 4, 3 * planes, width)), products, products]
-        + [f32(16, LANES)],
+        [f32(rows - 2, planes, width), parts_of((rows - 4, 3 * planes, width)), parts_of((2, 3 * planes, width))]
+        + [products, products, f32(16, LANES)],
         by_row,
         weights_by_row,
         from_diagonals[1],
-        cost=pl.CostEstimate(flops=2000000000, bytes_accessed=4000000, transcendentals=0),
+        from_rows[1],
+        cost=pl.CostEstimate(flops=400000000, bytes_accessed=800000, transcendentals=0),
     )
     outer_second, early_grams, *halos = call(
         outer_rows_kernel,
         [parts_of((4, 3 * planes, width)), f32(planes, 2 * planes), side, side],
         by_row,
         weights_by_row,
-        *from_rows,
+        from_rows[0],
         middle,
+        side_second,
         *inner_products,
-        scratch=[pltpu.VMEM((4, planes, width), jnp.float32)],
     )
     grams, edges = call(
         functools.partial(late_kernel, rows),

time: 24.2 us -> 24 us (level)
  blocking collectives: 8.82 us -> 8.5 us
    all_to_all x1, blocking collectives: 8.82 us -> 8.5 us  [on_device(): lax.all_to_all(grams, ('row', 'col'), 0, 0, axis_index_groups=[order], ti...]
where the time goes in v16:
time: 24 us; the launch traced here: 23.8 us
  blocking collectives  8.5 us (35%)
  starting transfers between devices  8.28 us (34%)
  Pallas kernels  6.36 us (26%)
  between operations  0.68 us (3%)
    all_to_all x1, blocking collectives, on_device(): lax.all_to_all(grams, ('row', 'col'), 0, 0, axis_index_groups=[order], ti...  8.5 us
    ppermute x6, starting transfers between devices, swap(): return lax.ppermute(value, names, pairs)  8.28 us
    pallas_call x6, Pallas kernels, call(): pl.pallas_call(kernel, out_shape=out_shapes, in_specs=[pl.BlockSpec(memor...  6.36 us
  transfers between devices with their start and end apart: 6, of which 0 were waited for; matrix products, arithmetic and copies ran while one was open for 0% of the time, Pallas kernels for 9%

profile of v16, /device:TPU:0, one launch (start us, length us, event | category | flops | bytes accessed | tf_op | source)
XLA Modules:
  0.0 23.8 jit_solution(4074381995446097792)
XLA Ops:
  0.6 1.4 %shard_map.41 = (f32[8,32,512]{2,1,0:T(8,128)S(1)}, f32[8,8,512]{2,1,0:T(8,128)S(1)}, f32[40,128]{1,0:T(8,128)S(1)}, f32[40,128]{1,0:T(8,128)S(1)}, f32[80,512]{...) custom-call(f32[32,8,512]{2,1,0:T(8,128)} %sketch.1, f32[8,8,512]{2,1,0:T(8,128)} %weights.1), custom_call_target="tpu_custom_call" | custom-call | tf_op jit(solution)/shard_map/pallas_call | solution.py:18
  2.0 0.5 %collective-permute-start.1 = (f32[72,512]{1,0:T(8,128)S(1)}, f32[72,512]{1,0:T(8,128)S(1)}, u32[]{:S(2)}, u32[]{:S(2)}) collective-permute-start(f32[72,512]{1,0:T(8,128)S(1)} %get-tuple-element.29), channel_id=1, source_target_pairs={{0,4},{1,5},{2,6},{3,7},{4,0},{5,1},{6,2},{7,3},{8,12},{9,13},{10,... | collective-permute-start | bytes 442376 | tf_op jit(solution)/shard_map/ppermute | solution.py:445
  2.6 2.6 %collective-permute-start.2 = (f32[80,512]{1,0:T(8,128)S(1)}, f32[80,512]{1,0:T(8,128)S(1)}, u32[]{:S(2)}, u32[]{:S(2)}) collective-permute-start(f32[80,512]{1,0:T(8,128)S(1)} %get-tuple-element.31), channel_id=1, source_target_pairs={{0,16},{1,17},{2,18},{3,19},{4,8},{5,9},{6,10},{7,11},{8,4},{9,5},... | collective-permute-start | bytes 491528 | tf_op jit(solution)/shard_map/ppermute | solution.py:445
  5.2 0.1 collective-permute-start
  5.2 1.6 %collective-permute-start.3 = (f32[16,128]{1,0:T(8,128)S(1)}, f32[16,128]{1,0:T(8,128)S(1)}, u32[]{:S(2)}, u32[]{:S(2)}) collective-permute-start(f32[16,128]{1,0:T(8,128)S(1)} %get-tuple-element.43), channel_id=1, source_target_pairs={{0,4},{1,17},{2,18},{3,7},{4,0},{5,10},{6,9},{7,3},{8,12},{9,6},{1... | collective-permute-start | bytes 24584 | tf_op jit(solution)/shard_map/ppermute | solution.py:445
  6.8 0.0 collective-permute-done.1.message.bulk_message
  6.8 0.2 shard_map.44
  7.0 1.9 %collective-permute-start.4 = (f32[16,128]{1,0:T(8,128)S(1)}, f32[16,128]{1,0:T(8,128)S(1)}, u32[]{:S(2)}, u32[]{:S(2)}) collective-permute-start(f32[16,128]{1,0:T(8,128)S(1)} %get-tuple-element.45), channel_id=1, source_target_pairs={{0,1},{1,0},{2,3},{3,2},{4,5},{5,4},{6,7},{7,6},{8,9},{9,8},{10,11... | collective-permute-start | bytes 24584 | tf_op jit(solution)/shard_map/ppermute | solution.py:445
  8.9 1.6 %collective-permute-start.5 = (f32[16,128]{1,0:T(8,128)S(1)}, f32[16,128]{1,0:T(8,128)S(1)}, u32[]{:S(2)}, u32[]{:S(2)}) collective-permute-start(f32[16,128]{1,0:T(8,128)S(1)} %get-tuple-element.46), channel_id=1, source_target_pairs={{0,4},{1,2},{2,1},{3,7},{4,0},{5,6},{6,5},{7,3},{8,12},{9,10},{10,... | collective-permute-start | bytes 24584 | tf_op jit(solution)/shard_map/ppermute | solution.py:445
  10.5 0.0 collective-permute-done.diagonal_message
  10.5 1.4 %shard_map.42 = (f32[6,32,512]{2,1,0:T(8,128)S(1)}, bf16[4,96,512]{2,1,0:T(8,128)(2,1)S(1)}, bf16[2,96,512]{2,1,0:T(8,128)(2,1)S(1)}, f32[96,96]{1,0:T(8,128)S(1...) custom-call(f32[8,32,512]{2,1,0:T(8,128)S(1)} %get-tuple-element.26.by_row, ...), custom_call_target="tpu_custom_call" | custom-call | flops 400000000 | bytes 800000 | tf_op jit(solution)/shard_map/pallas_call | solution.py:18
  11.9 0.0 collective-permute-done.2.message
  11.9 0.7 %shard_map.43 = (bf16[4,96,512]{2,1,0:T(8,128)(2,1)S(1)}, f32[32,64]{1,0:T(8,128)S(1)}, f32[40,128]{1,0:T(8,128)S(1)}, f32[40,128]{1,0:T(8,128)S(1)}) custom-call(f32[8,32,512]{2,1,0:T(8,128)S(1)} %get-tuple-element.26.by_row, f32[8,8,512]{2,1,0:T(8,128)S(1)} %get-tuple-element.27.weights_by_row, f32[80,512]{1,0:T(8,128)S(1)} %collective-permute-done.2.message, ...), custom_call_target="tpu_custom_call" | custom-call | tf_op jit(solution)/shard_map/pallas_call | solution.py:18
  12.6 0.0 collective-permute-done.3.rest_0_
  12.6 0.0 collective-permute-done.4.rest_2_
  12.6 0.0 collective-permute-done.5.rest_3_
  12.6 0.7 %shard_map.45 = (f32[16,1,1152]{2,1,0:T(1,128)S(1)}, f32[32,256]{1,0:T(8,128)S(1)}) custom-call(f32[40,128]{1,0:T(8,128)S(1)} %get-tuple-element.39.left, f32[40,128]{1,0:T(8,128)S(1)} %get-tuple-element.40.right, f32[40,128]{1,0:T(8,128)S(1)} %get-tuple-element.41.left_halo, f32[40,128]{1,0:T(8,128)S(1)} %get-tuple-element.42.right_halo, ...), custom_call_target="tpu_custom_call" | custom-call | tf_op jit(solution)/shard_map/pallas_call | solution.py:18
  13.3 8.5 %all_to_all.5.parts = f32[16,1,1152]{2,1,0:T(1,128)S(1)} all-to-all(f32[16,1,1152]{2,1,0:T(1,128)S(1)} %get-tuple-element.49), channel_id=1, replica_groups={{6,0,4,8,12,1,5,9,13,2,10,14,3,7,11,15},{22,16,20,24,28,17,21,25,29,18,..., dimensions={0} | all-to-all | bytes 147456 | tf_op jit(solution)/shard_map/all_to_all | solution.py:508
  21.8 2.0 %shard_map.46 = (f32[32,8,512]{2,1,0:T(8,128)}, f32[32,32]{1,0:T(8,128)}) custom-call(bf16[4,96,512]{2,1,0:T(8,128)(2,1)S(1)} %get-tuple-element.30.inner_second, bf16[4,96,512]{2,1,0:T(8,128)(2,1)S(1)} %get-tuple-element.36.outer_second, f32[32,256]{1,0:T(8,128)S(1)} %get-tuple-element.48.edges, f32[16,1,1152]{2,1,0:T(1,128)S(1)} %all_to_all.5.parts), custom_call_target="tpu_custom_call" | custom-call | tf_op jit(solution)/shard_map/pallas_call | solution.py:18
Async XLA Ops:
  2.0 4.8 %collective-permute-start.1 = (f32[72,512]{1,0:T(8,128)S(1)}, f32[72,512]{1,0:T(8,128)S(1)}, u32[]{:S(2)}, u32[]{:S(2)}) collective-permute-start(f32[72,512]{1,0:T(8,128)S(1)} %get-tuple-element.29), channel_id=1, source_target_pairs={{0,4},{1,5},{2,6},{3,7},{4,0},{5,1},{6,2},{7,3},{8,12},{9,13},{10,... | collective-permute-start | bytes 442376 | tf_op jit(solution)/shard_map/ppermute | solution.py:445
  2.6 9.3 %collective-permute-start.2 = (f32[80,512]{1,0:T(8,128)S(1)}, f32[80,512]{1,0:T(8,128)S(1)}, u32[]{:S(2)}, u32[]{:S(2)}) collective-permute-start(f32[80,512]{1,0:T(8,128)S(1)} %get-tuple-element.31), channel_id=1, source_target_pairs={{0,16},{1,17},{2,18},{3,19},{4,8},{5,9},{6,10},{7,11},{8,4},{9,5},... | collective-permute-start | bytes 491528 | tf_op jit(solution)/shard_map/ppermute | solution.py:445
  5.2 5.3 %collective-permute-start = (f32[16,128]{1,0:T(8,128)S(1)}, f32[16,128]{1,0:T(8,128)S(1)}, u32[]{:S(2)}, u32[]{:S(2)}) collective-permute-start(f32[16,128]{1,0:T(8,128)S(1)} %get-tuple-element.28), channel_id=1, source_target_pairs={{0,16},{1,17},{2,18},{3,19},{4,9},{5,8},{6,11},{7,10},{8,5},{9,4},... | collective-permute-start | bytes 24584 | tf_op jit(solution)/shard_map/ppermute | solution.py:445
  5.2 7.3 %collective-permute-start.3 = (f32[16,128]{1,0:T(8,128)S(1)}, f32[16,128]{1,0:T(8,128)S(1)}, u32[]{:S(2)}, u32[]{:S(2)}) collective-permute-start(f32[16,128]{1,0:T(8,128)S(1)} %get-tuple-element.43), channel_id=1, source_target_pairs={{0,4},{1,17},{2,18},{3,7},{4,0},{5,10},{6,9},{7,3},{8,12},{9,6},{1... | collective-permute-start | bytes 24584 | tf_op jit(solution)/shard_map/ppermute | solution.py:445
  7.0 5.6 %collective-permute-start.4 = (f32[16,128]{1,0:T(8,128)S(1)}, f32[16,128]{1,0:T(8,128)S(1)}, u32[]{:S(2)}, u32[]{:S(2)}) collective-permute-start(f32[16,128]{1,0:T(8,128)S(1)} %get-tuple-element.45), channel_id=1, source_target_pairs={{0,1},{1,0},{2,3},{3,2},{4,5},{5,4},{6,7},{7,6},{8,9},{9,8},{10,11... | collective-permute-start | bytes 24584 | tf_op jit(solution)/shard_map/ppermute | solution.py:445
  8.9 3.6 %collective-permute-start.5 = (f32[16,128]{1,0:T(8,128)S(1)}, f32[16,128]{1,0:T(8,128)S(1)}, u32[]{:S(2)}, u32[]{:S(2)}) collective-permute-start(f32[16,128]{1,0:T(8,128)S(1)} %get-tuple-element.46), channel_id=1, source_target_pairs={{0,4},{1,2},{2,1},{3,7},{4,0},{5,6},{6,5},{7,3},{8,12},{9,10},{10,... | collective-permute-start | bytes 24584 | tf_op jit(solution)/shard_map/ppermute | solution.py:445

commit v17 on v16

--- a/solution.py
+++ b/solution.py
@@ -100,7 +100,7 @@
         totals = [total + jnp.where(present, part, 0.0) for total, part in zip(totals, parts)]
     left[...], right[...] = totals
     to_left, to_right = folded(left[...], 2), folded(right[...], PITCH - 4)
-    for message, up in zip(col_messages, (jnp.logical_not(odd_col), odd_col)):
+    for message, up in zip(col_messages, (odd_col, jnp.logical_not(odd_col))):
         message[...] = jnp.where(up, to_right, to_left)
 
 
@@ -270,7 +270,7 @@
 
 
 def late_kernel(rows, left, right, left_halo, right_halo, *rest):
-    diagonal_messages, col_messages, (early_grams, grams, edges) = rest[:2], rest[3:1:-1], rest[4:]
+    diagonal_messages, col_messages, (early_grams, grams, edges) = rest[:2], rest[2:4], rest[4:]
     planes = early_grams.shape[0]
     odd_row, has_below, has_above = sides_of("row")
     odd_col, has_left, has_right = sides_of("col")
@@ -468,18 +468,18 @@
     left, right, *messages = call(
         functools.partial(strips_kernel, rows), [side, side] + [f32(16, LANES)] * 2, left, right, from_rows[1]
     )
-    from_cols = [swap(messages[1 - at], col_pairing=at) for at in (1, 0)]
+    from_cols = [swap(messages[at], col_pairing=at) for at in range(2)]
     parts_of = functools.partial(jax.ShapeDtypeStruct, dtype=jnp.bfloat16)
     products = f32(3 * planes, 3 * planes)
-    middle, inner_second, side_second, *inner_products, from_diagonals[1] = call(
+    middle, inner_second, side_second, *inner_products, from_diagonals[0] = call(
         inner_rows_kernel,
         [f32(rows - 2, planes, width), parts_of((rows - 4, 3 * planes, width)), parts_of((2, 3 * planes, width))]
         + [products, products, f32(16, LANES)],
         by_row,
         weights_by_row,
-        from_diagonals[1],
+        from_diagonals[0],
         from_rows[1],
-        cost=pl.CostEstimate(flops=400000000, bytes_accessed=800000, transcendentals=0),
+        cost=pl.CostEstimate(flops=20000000, bytes_accessed=40000, transcendentals=0),
     )
     outer_second, early_grams, *halos = call(
         outer_rows_kernel,

time: 24 us -> 24.4 us (1.017)
  waiting for transfers between devices: 0.02 us -> 0.57 us
    ppermute x6, waiting for transfers between devices: 0.02 us -> 0.57 us  [swap(): return lax.ppermute(value, names, pairs)]
  transfers between devices with their start and end apart: 6 -> 6, of which waited for: 0 -> 1; matrix products, arithmetic and copies ran while one was open for 0% -> 0% of each run, Pallas kernels for 9% -> 9%
where the time goes in v17:
time: 24.4 us; the launch traced here: 24.2 us
  starting transfers between devices  8.31 us (34%)
  blocking collectives  8.27 us (34%)
  Pallas kernels  6.36 us (26%)
  between operations  0.67 us (3%)
  waiting for transfers between devices  0.57 us (2%)
    ppermute x6, starting transfers between devices, swap(): return lax.ppermute(value, names, pairs)  8.31 us
    all_to_all x1, blocking collectives, on_device(): lax.all_to_all(grams, ('row', 'col'), 0, 0, axis_index_groups=[order], ti...  8.27 us
    pallas_call x6, Pallas kernels, call(): pl.pallas_call(kernel, out_shape=out_shapes, in_specs=[pl.BlockSpec(memor...  6.36 us
    ppermute x6, waiting for transfers between devices, swap(): return lax.ppermute(value, names, pairs)  0.57 us
  transfers between devices with their start and end apart: 6, of which 1 were waited for; matrix products, arithmetic and copies ran while one was open for 0% of the time, Pallas kernels for 9%

profile of v17, /device:TPU:0, one launch (start us, length us, event | category | flops | bytes accessed | tf_op | source)
XLA Modules:
  0.0 24.2 jit_solution(1054702321019407226)
XLA Ops:
  0.6 1.4 %shard_map.41 = (f32[8,32,512]{2,1,0:T(8,128)S(1)}, f32[8,8,512]{2,1,0:T(8,128)S(1)}, f32[40,128]{1,0:T(8,128)S(1)}, f32[40,128]{1,0:T(8,128)S(1)}, f32[80,512]{...) custom-call(f32[32,8,512]{2,1,0:T(8,128)} %sketch.1, f32[8,8,512]{2,1,0:T(8,128)} %weights.1), custom_call_target="tpu_custom_call" | custom-call | tf_op jit(solution)/shard_map/pallas_call | solution.py:18
  2.0 3.0 %collective-permute-start.2 = (f32[80,512]{1,0:T(8,128)S(1)}, f32[80,512]{1,0:T(8,128)S(1)}, u32[]{:S(2)}, u32[]{:S(2)}) collective-permute-start(f32[80,512]{1,0:T(8,128)S(1)} %get-tuple-element.31), channel_id=1, source_target_pairs={{0,16},{1,17},{2,18},{3,19},{4,8},{5,9},{6,10},{7,11},{8,4},{9,5},... | collective-permute-start | bytes 491528 | tf_op jit(solution)/shard_map/ppermute | solution.py:445
  5.1 0.1 collective-permute-start.1
  5.2 0.4 %collective-permute-start = (f32[16,128]{1,0:T(8,128)S(1)}, f32[16,128]{1,0:T(8,128)S(1)}, u32[]{:S(2)}, u32[]{:S(2)}) collective-permute-start(f32[16,128]{1,0:T(8,128)S(1)} %get-tuple-element.28), channel_id=1, source_target_pairs={{0,4},{1,17},{2,18},{3,7},{4,0},{5,10},{6,9},{7,3},{8,12},{9,6},{1... | collective-permute-start | bytes 24584 | tf_op jit(solution)/shard_map/ppermute | solution.py:445
  5.6 1.1 %collective-permute-start.3 = (f32[16,128]{1,0:T(8,128)S(1)}, f32[16,128]{1,0:T(8,128)S(1)}, u32[]{:S(2)}, u32[]{:S(2)}) collective-permute-start(f32[16,128]{1,0:T(8,128)S(1)} %get-tuple-element.44), channel_id=1, source_target_pairs={{0,16},{1,17},{2,18},{3,19},{4,9},{5,8},{6,11},{7,10},{8,5},{9,4},... | collective-permute-start | bytes 24584 | tf_op jit(solution)/shard_map/ppermute | solution.py:445
  6.7 0.0 collective-permute-done.1.message.bulk_message
  6.7 0.2 shard_map.44
  6.9 2.7 %collective-permute-start.4 = (f32[16,128]{1,0:T(8,128)S(1)}, f32[16,128]{1,0:T(8,128)S(1)}, u32[]{:S(2)}, u32[]{:S(2)}) collective-permute-start(f32[16,128]{1,0:T(8,128)S(1)} %get-tuple-element.45), channel_id=1, source_target_pairs={{0,4},{1,2},{2,1},{3,7},{4,0},{5,6},{6,5},{7,3},{8,12},{9,10},{10,... | collective-permute-start | bytes 24584 | tf_op jit(solution)/shard_map/ppermute | solution.py:445
  9.5 1.0 %collective-permute-start.5 = (f32[16,128]{1,0:T(8,128)S(1)}, f32[16,128]{1,0:T(8,128)S(1)}, u32[]{:S(2)}, u32[]{:S(2)}) collective-permute-start(f32[16,128]{1,0:T(8,128)S(1)} %get-tuple-element.46), channel_id=1, source_target_pairs={{0,1},{1,0},{2,3},{3,2},{4,5},{5,4},{6,7},{7,6},{8,9},{9,8},{10,11... | collective-permute-start | bytes 24584 | tf_op jit(solution)/shard_map/ppermute | solution.py:445
  10.5 0.0 collective-permute-done.diagonal_message
  10.5 1.4 %shard_map.42 = (f32[6,32,512]{2,1,0:T(8,128)S(1)}, bf16[4,96,512]{2,1,0:T(8,128)(2,1)S(1)}, bf16[2,96,512]{2,1,0:T(8,128)(2,1)S(1)}, f32[96,96]{1,0:T(8,128)S(1...) custom-call(f32[8,32,512]{2,1,0:T(8,128)S(1)} %get-tuple-element.26.by_row, ...), custom_call_target="tpu_custom_call" | custom-call | flops 20000000 | bytes 40000 | tf_op jit(solution)/shard_map/pallas_call | solution.py:18
  11.9 0.0 collective-permute-done.2.message
  11.9 0.7 %shard_map.43 = (bf16[4,96,512]{2,1,0:T(8,128)(2,1)S(1)}, f32[32,64]{1,0:T(8,128)S(1)}, f32[40,128]{1,0:T(8,128)S(1)}, f32[40,128]{1,0:T(8,128)S(1)}) custom-call(f32[8,32,512]{2,1,0:T(8,128)S(1)} %get-tuple-element.26.by_row, f32[8,8,512]{2,1,0:T(8,128)S(1)} %get-tuple-element.27.weights_by_row, f32[80,512]{1,0:T(8,128)S(1)} %collective-permute-done.2.message, ...), custom_call_target="tpu_custom_call" | custom-call | tf_op jit(solution)/shard_map/pallas_call | solution.py:18
  12.6 0.0 collective-permute-done.3.rest_1_
  12.6 0.0 collective-permute-done.4.rest_2_
  12.6 0.6 %collective-permute-done.5.rest_3_ = f32[16,128]{1,0:T(8,128)S(1)} collective-permute-done((f32[16,128]{1,0:T(8,128)S(1)}, f32[16,128]{1,0:T(8,128)S(1)}, u32[]{:S(2)}, u32[]{:S(2)}) %collective-permute-start.5) | collective-permute-done | bytes 8224 | tf_op jit(solution)/shard_map/ppermute | solution.py:445
  13.2 0.7 %shard_map.45 = (f32[16,1,1152]{2,1,0:T(1,128)S(1)}, f32[32,256]{1,0:T(8,128)S(1)}) custom-call(f32[40,128]{1,0:T(8,128)S(1)} %get-tuple-element.39.left, f32[40,128]{1,0:T(8,128)S(1)} %get-tuple-element.40.right, f32[40,128]{1,0:T(8,128)S(1)} %get-tuple-element.41.left_halo, f32[40,128]{1,0:T(8,128)S(1)} %get-tuple-element.42.right_halo, ...), custom_call_target="tpu_custom_call" | custom-call | tf_op jit(solution)/shard_map/pallas_call | solution.py:18
  13.9 8.3 %all_to_all.5.parts = f32[16,1,1152]{2,1,0:T(1,128)S(1)} all-to-all(f32[16,1,1152]{2,1,0:T(1,128)S(1)} %get-tuple-element.49), channel_id=1, replica_groups={{6,0,4,8,12,1,5,9,13,2,10,14,3,7,11,15},{22,16,20,24,28,17,21,25,29,18,..., dimensions={0} | all-to-all | bytes 147456 | tf_op jit(solution)/shard_map/all_to_all | solution.py:508
  22.2 2.0 %shard_map.46 = (f32[32,8,512]{2,1,0:T(8,128)}, f32[32,32]{1,0:T(8,128)}) custom-call(bf16[4,96,512]{2,1,0:T(8,128)(2,1)S(1)} %get-tuple-element.30.inner_second, bf16[4,96,512]{2,1,0:T(8,128)(2,1)S(1)} %get-tuple-element.36.outer_second, f32[32,256]{1,0:T(8,128)S(1)} %get-tuple-element.48.edges, f32[16,1,1152]{2,1,0:T(1,128)S(1)} %all_to_all.5.parts), custom_call_target="tpu_custom_call" | custom-call | tf_op jit(solution)/shard_map/pallas_call | solution.py:18
Async XLA Ops:
  2.0 9.9 %collective-permute-start.2 = (f32[80,512]{1,0:T(8,128)S(1)}, f32[80,512]{1,0:T(8,128)S(1)}, u32[]{:S(2)}, u32[]{:S(2)}) collective-permute-start(f32[80,512]{1,0:T(8,128)S(1)} %get-tuple-element.31), channel_id=1, source_target_pairs={{0,16},{1,17},{2,18},{3,19},{4,8},{5,9},{6,10},{7,11},{8,4},{9,5},... | collective-permute-start | bytes 491528 | tf_op jit(solution)/shard_map/ppermute | solution.py:445
  5.1 1.6 %collective-permute-start.1 = (f32[72,512]{1,0:T(8,128)S(1)}, f32[72,512]{1,0:T(8,128)S(1)}, u32[]{:S(2)}, u32[]{:S(2)}) collective-permute-start(f32[72,512]{1,0:T(8,128)S(1)} %get-tuple-element.29), channel_id=1, source_target_pairs={{0,4},{1,5},{2,6},{3,7},{4,0},{5,1},{6,2},{7,3},{8,12},{9,13},{10,... | collective-permute-start | bytes 442376 | tf_op jit(solution)/shard_map/ppermute | solution.py:445
  5.2 5.4 %collective-permute-start = (f32[16,128]{1,0:T(8,128)S(1)}, f32[16,128]{1,0:T(8,128)S(1)}, u32[]{:S(2)}, u32[]{:S(2)}) collective-permute-start(f32[16,128]{1,0:T(8,128)S(1)} %get-tuple-element.28), channel_id=1, source_target_pairs={{0,4},{1,17},{2,18},{3,7},{4,0},{5,10},{6,9},{7,3},{8,12},{9,6},{1... | collective-permute-start | bytes 24584 | tf_op jit(solution)/shard_map/ppermute | solution.py:445
  5.6 7.0 %collective-permute-start.3 = (f32[16,128]{1,0:T(8,128)S(1)}, f32[16,128]{1,0:T(8,128)S(1)}, u32[]{:S(2)}, u32[]{:S(2)}) collective-permute-start(f32[16,128]{1,0:T(8,128)S(1)} %get-tuple-element.44), channel_id=1, source_target_pairs={{0,16},{1,17},{2,18},{3,19},{4,9},{5,8},{6,11},{7,10},{8,5},{9,4},... | collective-permute-start | bytes 24584 | tf_op jit(solution)/shard_map/ppermute | solution.py:445
  6.9 5.8 %collective-permute-start.4 = (f32[16,128]{1,0:T(8,128)S(1)}, f32[16,128]{1,0:T(8,128)S(1)}, u32[]{:S(2)}, u32[]{:S(2)}) collective-permute-start(f32[16,128]{1,0:T(8,128)S(1)} %get-tuple-element.45), channel_id=1, source_target_pairs={{0,4},{1,2},{2,1},{3,7},{4,0},{5,6},{6,5},{7,3},{8,12},{9,10},{10,... | collective-permute-start | bytes 24584 | tf_op jit(solution)/shard_map/ppermute | solution.py:445
  9.5 3.7 %collective-permute-start.5 = (f32[16,128]{1,0:T(8,128)S(1)}, f32[16,128]{1,0:T(8,128)S(1)}, u32[]{:S(2)}, u32[]{:S(2)}) collective-permute-start(f32[16,128]{1,0:T(8,128)S(1)} %get-tuple-element.46), channel_id=1, source_target_pairs={{0,1},{1,0},{2,3},{3,2},{4,5},{5,4},{6,7},{7,6},{8,9},{9,8},{10,11... | collective-permute-start | bytes 24584 | tf_op jit(solution)/shard_map/ppermute | solution.py:445

commit v18 on v16

--- a/solution.py
+++ b/solution.py
@@ -479,7 +479,7 @@
         weights_by_row,
         from_diagonals[1],
         from_rows[1],
-        cost=pl.CostEstimate(flops=400000000, bytes_accessed=800000, transcendentals=0),
+        cost=pl.CostEstimate(flops=20000000, bytes_accessed=40000, transcendentals=0),
     )
     outer_second, early_grams, *halos = call(
         outer_rows_kernel,

time: 24 us -> 24.4 us (1.017)
  starting transfers between devices: 8.28 us -> 8.63 us
    ppermute x6, starting transfers between devices: 8.28 us -> 8.63 us  [swap(): return lax.ppermute(value, names, pairs)]
where the time goes in v18:
time: 24.4 us; the launch traced here: 24.3 us
  starting transfers between devices  8.63 us (35%)
  blocking collectives  8.57 us (35%)
  Pallas kernels  6.38 us (26%)
  between operations  0.68 us (3%)
    ppermute x6, starting transfers between devices, swap(): return lax.ppermute(value, names, pairs)  8.63 us
    all_to_all x1, blocking collectives, on_device(): lax.all_to_all(grams, ('row', 'col'), 0, 0, axis_index_groups=[order], ti...  8.57 us
    pallas_call x6, Pallas kernels, call(): pl.pallas_call(kernel, out_shape=out_shapes, in_specs=[pl.BlockSpec(memor...  6.38 us
  transfers between devices with their start and end apart: 6, of which 0 were waited for; matrix products, arithmetic and copies ran while one was open for 0% of the time, Pallas kernels for 9%

profile of v18, /device:TPU:0, one launch (start us, length us, event | category | flops | bytes accessed | tf_op | source)
XLA Modules:
  0.0 24.3 jit_solution(3627928106858265537)
XLA Ops:
  0.6 1.4 %shard_map.41 = (f32[8,32,512]{2,1,0:T(8,128)S(1)}, f32[8,8,512]{2,1,0:T(8,128)S(1)}, f32[40,128]{1,0:T(8,128)S(1)}, f32[40,128]{1,0:T(8,128)S(1)}, f32[80,512]{...) custom-call(f32[32,8,512]{2,1,0:T(8,128)} %sketch.1, f32[8,8,512]{2,1,0:T(8,128)} %weights.1), custom_call_target="tpu_custom_call" | custom-call | tf_op jit(solution)/shard_map/pallas_call | solution.py:18
  2.0 3.0 %collective-permute-start.2 = (f32[80,512]{1,0:T(8,128)S(1)}, f32[80,512]{1,0:T(8,128)S(1)}, u32[]{:S(2)}, u32[]{:S(2)}) collective-permute-start(f32[80,512]{1,0:T(8,128)S(1)} %get-tuple-element.31), channel_id=1, source_target_pairs={{0,16},{1,17},{2,18},{3,19},{4,8},{5,9},{6,10},{7,11},{8,4},{9,5},... | collective-permute-start | bytes 491528 | tf_op jit(solution)/shard_map/ppermute | solution.py:445
  5.1 0.1 collective-permute-start.1
  5.2 1.5 %collective-permute-start = (f32[16,128]{1,0:T(8,128)S(1)}, f32[16,128]{1,0:T(8,128)S(1)}, u32[]{:S(2)}, u32[]{:S(2)}) collective-permute-start(f32[16,128]{1,0:T(8,128)S(1)} %get-tuple-element.28), channel_id=1, source_target_pairs={{0,16},{1,17},{2,18},{3,19},{4,9},{5,8},{6,11},{7,10},{8,5},{9,4},... | collective-permute-start | bytes 24584 | tf_op jit(solution)/shard_map/ppermute | solution.py:445
  6.7 0.6 %collective-permute-start.3 = (f32[16,128]{1,0:T(8,128)S(1)}, f32[16,128]{1,0:T(8,128)S(1)}, u32[]{:S(2)}, u32[]{:S(2)}) collective-permute-start(f32[16,128]{1,0:T(8,128)S(1)} %get-tuple-element.43), channel_id=1, source_target_pairs={{0,4},{1,17},{2,18},{3,7},{4,0},{5,10},{6,9},{7,3},{8,12},{9,6},{1... | collective-permute-start | bytes 24584 | tf_op jit(solution)/shard_map/ppermute | solution.py:445
  7.2 0.0 collective-permute-done.1.message.bulk_message
  7.3 0.2 shard_map.44
  7.4 1.5 %collective-permute-start.4 = (f32[16,128]{1,0:T(8,128)S(1)}, f32[16,128]{1,0:T(8,128)S(1)}, u32[]{:S(2)}, u32[]{:S(2)}) collective-permute-start(f32[16,128]{1,0:T(8,128)S(1)} %get-tuple-element.45), channel_id=1, source_target_pairs={{0,1},{1,0},{2,3},{3,2},{4,5},{5,4},{6,7},{7,6},{8,9},{9,8},{10,11... | collective-permute-start | bytes 24584 | tf_op jit(solution)/shard_map/ppermute | solution.py:445
  9.0 1.9 %collective-permute-start.5 = (f32[16,128]{1,0:T(8,128)S(1)}, f32[16,128]{1,0:T(8,128)S(1)}, u32[]{:S(2)}, u32[]{:S(2)}) collective-permute-start(f32[16,128]{1,0:T(8,128)S(1)} %get-tuple-element.46), channel_id=1, source_target_pairs={{0,4},{1,2},{2,1},{3,7},{4,0},{5,6},{6,5},{7,3},{8,12},{9,10},{10,... | collective-permute-start | bytes 24584 | tf_op jit(solution)/shard_map/ppermute | solution.py:445
  10.8 0.0 collective-permute-done.diagonal_message
  10.8 1.4 %shard_map.42 = (f32[6,32,512]{2,1,0:T(8,128)S(1)}, bf16[4,96,512]{2,1,0:T(8,128)(2,1)S(1)}, bf16[2,96,512]{2,1,0:T(8,128)(2,1)S(1)}, f32[96,96]{1,0:T(8,128)S(1...) custom-call(f32[8,32,512]{2,1,0:T(8,128)S(1)} %get-tuple-element.26.by_row, ...), custom_call_target="tpu_custom_call" | custom-call | flops 20000000 | bytes 40000 | tf_op jit(solution)/shard_map/pallas_call | solution.py:18
  12.2 0.0 collective-permute-done.2.message
  12.2 0.7 %shard_map.43 = (bf16[4,96,512]{2,1,0:T(8,128)(2,1)S(1)}, f32[32,64]{1,0:T(8,128)S(1)}, f32[40,128]{1,0:T(8,128)S(1)}, f32[40,128]{1,0:T(8,128)S(1)}) custom-call(f32[8,32,512]{2,1,0:T(8,128)S(1)} %get-tuple-element.26.by_row, f32[8,8,512]{2,1,0:T(8,128)S(1)} %get-tuple-element.27.weights_by_row, f32[80,512]{1,0:T(8,128)S(1)} %collective-permute-done.2.message, ...), custom_call_target="tpu_custom_call" | custom-call | tf_op jit(solution)/shard_map/pallas_call | solution.py:18
  12.9 0.0 collective-permute-done.3.rest_0_
  12.9 0.0 collective-permute-done.4.rest_2_
  12.9 0.0 collective-permute-done.5.rest_3_
  13.0 0.7 %shard_map.45 = (f32[16,1,1152]{2,1,0:T(1,128)S(1)}, f32[32,256]{1,0:T(8,128)S(1)}) custom-call(f32[40,128]{1,0:T(8,128)S(1)} %get-tuple-element.39.left, f32[40,128]{1,0:T(8,128)S(1)} %get-tuple-element.40.right, f32[40,128]{1,0:T(8,128)S(1)} %get-tuple-element.41.left_halo, f32[40,128]{1,0:T(8,128)S(1)} %get-tuple-element.42.right_halo, ...), custom_call_target="tpu_custom_call" | custom-call | tf_op jit(solution)/shard_map/pallas_call | solution.py:18
  13.7 8.6 %all_to_all.5.parts = f32[16,1,1152]{2,1,0:T(1,128)S(1)} all-to-all(f32[16,1,1152]{2,1,0:T(1,128)S(1)} %get-tuple-element.49), channel_id=1, replica_groups={{6,0,4,8,12,1,5,9,13,2,10,14,3,7,11,15},{22,16,20,24,28,17,21,25,29,18,..., dimensions={0} | all-to-all | bytes 147456 | tf_op jit(solution)/shard_map/all_to_all | solution.py:508
  22.3 2.0 %shard_map.46 = (f32[32,8,512]{2,1,0:T(8,128)}, f32[32,32]{1,0:T(8,128)}) custom-call(bf16[4,96,512]{2,1,0:T(8,128)(2,1)S(1)} %get-tuple-element.30.inner_second, bf16[4,96,512]{2,1,0:T(8,128)(2,1)S(1)} %get-tuple-element.36.outer_second, f32[32,256]{1,0:T(8,128)S(1)} %get-tuple-element.48.edges, f32[16,1,1152]{2,1,0:T(1,128)S(1)} %all_to_all.5.parts), custom_call_target="tpu_custom_call" | custom-call | tf_op jit(solution)/shard_map/pallas_call | solution.py:18
Async XLA Ops:
  2.0 10.2 %collective-permute-start.2 = (f32[80,512]{1,0:T(8,128)S(1)}, f32[80,512]{1,0:T(8,128)S(1)}, u32[]{:S(2)}, u32[]{:S(2)}) collective-permute-start(f32[80,512]{1,0:T(8,128)S(1)} %get-tuple-element.31), channel_id=1, source_target_pairs={{0,16},{1,17},{2,18},{3,19},{4,8},{5,9},{6,10},{7,11},{8,4},{9,5},... | collective-permute-start | bytes 491528 | tf_op jit(solution)/shard_map/ppermute | solution.py:445
  5.1 2.2 %collective-permute-start.1 = (f32[72,512]{1,0:T(8,128)S(1)}, f32[72,512]{1,0:T(8,128)S(1)}, u32[]{:S(2)}, u32[]{:S(2)}) collective-permute-start(f32[72,512]{1,0:T(8,128)S(1)} %get-tuple-element.29), channel_id=1, source_target_pairs={{0,4},{1,5},{2,6},{3,7},{4,0},{5,1},{6,2},{7,3},{8,12},{9,13},{10,... | collective-permute-start | bytes 442376 | tf_op jit(solution)/shard_map/ppermute | solution.py:445
  5.2 5.7 %collective-permute-start = (f32[16,128]{1,0:T(8,128)S(1)}, f32[16,128]{1,0:T(8,128)S(1)}, u32[]{:S(2)}, u32[]{:S(2)}) collective-permute-start(f32[16,128]{1,0:T(8,128)S(1)} %get-tuple-element.28), channel_id=1, source_target_pairs={{0,16},{1,17},{2,18},{3,19},{4,9},{5,8},{6,11},{7,10},{8,5},{9,4},... | collective-permute-start | bytes 24584 | tf_op jit(solution)/shard_map/ppermute | solution.py:445
  6.7 6.3 %collective-permute-start.3 = (f32[16,128]{1,0:T(8,128)S(1)}, f32[16,128]{1,0:T(8,128)S(1)}, u32[]{:S(2)}, u32[]{:S(2)}) collective-permute-start(f32[16,128]{1,0:T(8,128)S(1)} %get-tuple-element.43), channel_id=1, source_target_pairs={{0,4},{1,17},{2,18},{3,7},{4,0},{5,10},{6,9},{7,3},{8,12},{9,6},{1... | collective-permute-start | bytes 24584 | tf_op jit(solution)/shard_map/ppermute | solution.py:445
  7.4 5.5 %collective-permute-start.4 = (f32[16,128]{1,0:T(8,128)S(1)}, f32[16,128]{1,0:T(8,128)S(1)}, u32[]{:S(2)}, u32[]{:S(2)}) collective-permute-start(f32[16,128]{1,0:T(8,128)S(1)} %get-tuple-element.45), channel_id=1, source_target_pairs={{0,1},{1,0},{2,3},{3,2},{4,5},{5,4},{6,7},{7,6},{8,9},{9,8},{10,11... | collective-permute-start | bytes 24584 | tf_op jit(solution)/shard_map/ppermute | solution.py:445
  9.0 4.0 %collective-permute-start.5 = (f32[16,128]{1,0:T(8,128)S(1)}, f32[16,128]{1,0:T(8,128)S(1)}, u32[]{:S(2)}, u32[]{:S(2)}) collective-permute-start(f32[16,128]{1,0:T(8,128)S(1)} %get-tuple-element.46), channel_id=1, source_target_pairs={{0,4},{1,2},{2,1},{3,7},{4,0},{5,6},{6,5},{7,3},{8,12},{9,10},{10,... | collective-permute-start | bytes 24584 | tf_op jit(solution)/shard_map/ppermute | solution.py:445

commit v19 on v16

--- a/solution.py
+++ b/solution.py
@@ -502,7 +502,7 @@
         early_grams,
     )
     rows_of, cols_of = lax.axis_size("row"), lax.axis_size("col")
-    first = cols_of + cols_of // 2
+    first = cols_of + (cols_of - 1) // 2
     order = [first] + [row * cols_of + col for col in range(cols_of) for row in range(rows_of)]
     order = list(dict.fromkeys(order))
     parts = lax.all_to_all(grams, ("row", "col"), 0, 0, axis_index_groups=[order], tiled=True)

time: 24 us -> 24.6 us (1.025)
  blocking collectives: 8.5 us -> 9.04 us
    all_to_all x1, blocking collectives: 8.5 us -> 9.04 us  [on_device(): lax.all_to_all(grams, ('row', 'col'), 0, 0, axis_index_groups=[order], ti...]
where the time goes in v19:
time: 24.6 us; the launch traced here: 24.4 us
  blocking collectives  9.04 us (37%)
  starting transfers between devices  8.28 us (34%)
  Pallas kernels  6.36 us (26%)
  between operations  0.68 us (3%)
    all_to_all x1, blocking collectives, on_device(): lax.all_to_all(grams, ('row', 'col'), 0, 0, axis_index_groups=[order], ti...  9.04 us
    ppermute x6, starting transfers between devices, swap(): return lax.ppermute(value, names, pairs)  8.28 us
    pallas_call x6, Pallas kernels, call(): pl.pallas_call(kernel, out_shape=out_shapes, in_specs=[pl.BlockSpec(memor...  6.36 us
  transfers between devices with their start and end apart: 6, of which 0 were waited for; matrix products, arithmetic and copies ran while one was open for 0% of the time, Pallas kernels for 9%

profile of v19, /device:TPU:0, one launch (start us, length us, event | category | flops | bytes accessed | tf_op | source)
XLA Modules:
  0.0 24.4 jit_solution(16276910092595369412)
XLA Ops:
  0.6 1.4 %shard_map.41 = (f32[8,32,512]{2,1,0:T(8,128)S(1)}, f32[8,8,512]{2,1,0:T(8,128)S(1)}, f32[40,128]{1,0:T(8,128)S(1)}, f32[40,128]{1,0:T(8,128)S(1)}, f32[80,512]{...) custom-call(f32[32,8,512]{2,1,0:T(8,128)} %sketch.1, f32[8,8,512]{2,1,0:T(8,128)} %weights.1), custom_call_target="tpu_custom_call" | custom-call | tf_op jit(solution)/shard_map/pallas_call | solution.py:18
  2.0 0.5 %collective-permute-start.1 = (f32[72,512]{1,0:T(8,128)S(1)}, f32[72,512]{1,0:T(8,128)S(1)}, u32[]{:S(2)}, u32[]{:S(2)}) collective-permute-start(f32[72,512]{1,0:T(8,128)S(1)} %get-tuple-element.29), channel_id=1, source_target_pairs={{0,4},{1,5},{2,6},{3,7},{4,0},{5,1},{6,2},{7,3},{8,12},{9,13},{10,... | collective-permute-start | bytes 442376 | tf_op jit(solution)/shard_map/ppermute | solution.py:445
  2.6 2.6 %collective-permute-start.2 = (f32[80,512]{1,0:T(8,128)S(1)}, f32[80,512]{1,0:T(8,128)S(1)}, u32[]{:S(2)}, u32[]{:S(2)}) collective-permute-start(f32[80,512]{1,0:T(8,128)S(1)} %get-tuple-element.31), channel_id=1, source_target_pairs={{0,16},{1,17},{2,18},{3,19},{4,8},{5,9},{6,10},{7,11},{8,4},{9,5},... | collective-permute-start | bytes 491528 | tf_op jit(solution)/shard_map/ppermute | solution.py:445
  5.2 0.1 collective-permute-start
  5.2 1.6 %collective-permute-start.3 = (f32[16,128]{1,0:T(8,128)S(1)}, f32[16,128]{1,0:T(8,128)S(1)}, u32[]{:S(2)}, u32[]{:S(2)}) collective-permute-start(f32[16,128]{1,0:T(8,128)S(1)} %get-tuple-element.43), channel_id=1, source_target_pairs={{0,4},{1,17},{2,18},{3,7},{4,0},{5,10},{6,9},{7,3},{8,12},{9,6},{1... | collective-permute-start | bytes 24584 | tf_op jit(solution)/shard_map/ppermute | solution.py:445
  6.8 0.0 collective-permute-done.1.message.bulk_message
  6.8 0.2 shard_map.44
  7.0 1.9 %collective-permute-start.4 = (f32[16,128]{1,0:T(8,128)S(1)}, f32[16,128]{1,0:T(8,128)S(1)}, u32[]{:S(2)}, u32[]{:S(2)}) collective-permute-start(f32[16,128]{1,0:T(8,128)S(1)} %get-tuple-element.45), channel_id=1, source_target_pairs={{0,1},{1,0},{2,3},{3,2},{4,5},{5,4},{6,7},{7,6},{8,9},{9,8},{10,11... | collective-permute-start | bytes 24584 | tf_op jit(solution)/shard_map/ppermute | solution.py:445
  8.9 1.6 %collective-permute-start.5 = (f32[16,128]{1,0:T(8,128)S(1)}, f32[16,128]{1,0:T(8,128)S(1)}, u32[]{:S(2)}, u32[]{:S(2)}) collective-permute-start(f32[16,128]{1,0:T(8,128)S(1)} %get-tuple-element.46), channel_id=1, source_target_pairs={{0,4},{1,2},{2,1},{3,7},{4,0},{5,6},{6,5},{7,3},{8,12},{9,10},{10,... | collective-permute-start | bytes 24584 | tf_op jit(solution)/shard_map/ppermute | solution.py:445
  10.5 0.0 collective-permute-done.diagonal_message
  10.5 1.4 %shard_map.42 = (f32[6,32,512]{2,1,0:T(8,128)S(1)}, bf16[4,96,512]{2,1,0:T(8,128)(2,1)S(1)}, bf16[2,96,512]{2,1,0:T(8,128)(2,1)S(1)}, f32[96,96]{1,0:T(8,128)S(1...) custom-call(f32[8,32,512]{2,1,0:T(8,128)S(1)} %get-tuple-element.26.by_row, ...), custom_call_target="tpu_custom_call" | custom-call | flops 400000000 | bytes 800000 | tf_op jit(solution)/shard_map/pallas_call | solution.py:18
  11.9 0.0 collective-permute-done.2.message
  11.9 0.7 %shard_map.43 = (bf16[4,96,512]{2,1,0:T(8,128)(2,1)S(1)}, f32[32,64]{1,0:T(8,128)S(1)}, f32[40,128]{1,0:T(8,128)S(1)}, f32[40,128]{1,0:T(8,128)S(1)}) custom-call(f32[8,32,512]{2,1,0:T(8,128)S(1)} %get-tuple-element.26.by_row, f32[8,8,512]{2,1,0:T(8,128)S(1)} %get-tuple-element.27.weights_by_row, f32[80,512]{1,0:T(8,128)S(1)} %collective-permute-done.2.message, ...), custom_call_target="tpu_custom_call" | custom-call | tf_op jit(solution)/shard_map/pallas_call | solution.py:18
  12.6 0.0 collective-permute-done.3.rest_0_
  12.6 0.0 collective-permute-done.4.rest_2_
  12.6 0.0 collective-permute-done.5.rest_3_
  12.6 0.7 %shard_map.45 = (f32[16,1,1152]{2,1,0:T(1,128)S(1)}, f32[32,256]{1,0:T(8,128)S(1)}) custom-call(f32[40,128]{1,0:T(8,128)S(1)} %get-tuple-element.39.left, f32[40,128]{1,0:T(8,128)S(1)} %get-tuple-element.40.right, f32[40,128]{1,0:T(8,128)S(1)} %get-tuple-element.41.left_halo, f32[40,128]{1,0:T(8,128)S(1)} %get-tuple-element.42.right_halo, ...), custom_call_target="tpu_custom_call" | custom-call | tf_op jit(solution)/shard_map/pallas_call | solution.py:18
  13.3 9.0 %all_to_all.5.parts = f32[16,1,1152]{2,1,0:T(1,128)S(1)} all-to-all(f32[16,1,1152]{2,1,0:T(1,128)S(1)} %get-tuple-element.49), channel_id=1, replica_groups={{5,0,4,8,12,1,9,13,2,6,10,14,3,7,11,15},{21,16,20,24,28,17,25,29,18,22,..., dimensions={0} | all-to-all | bytes 147456 | tf_op jit(solution)/shard_map/all_to_all | solution.py:508
  22.4 2.0 %shard_map.46 = (f32[32,8,512]{2,1,0:T(8,128)}, f32[32,32]{1,0:T(8,128)}) custom-call(bf16[4,96,512]{2,1,0:T(8,128)(2,1)S(1)} %get-tuple-element.30.inner_second, bf16[4,96,512]{2,1,0:T(8,128)(2,1)S(1)} %get-tuple-element.36.outer_second, f32[32,256]{1,0:T(8,128)S(1)} %get-tuple-element.48.edges, f32[16,1,1152]{2,1,0:T(1,128)S(1)} %all_to_all.5.parts), custom_call_target="tpu_custom_call" | custom-call | tf_op jit(solution)/shard_map/pallas_call | solution.py:18
Async XLA Ops:
  2.0 4.8 %collective-permute-start.1 = (f32[72,512]{1,0:T(8,128)S(1)}, f32[72,512]{1,0:T(8,128)S(1)}, u32[]{:S(2)}, u32[]{:S(2)}) collective-permute-start(f32[72,512]{1,0:T(8,128)S(1)} %get-tuple-element.29), channel_id=1, source_target_pairs={{0,4},{1,5},{2,6},{3,7},{4,0},{5,1},{6,2},{7,3},{8,12},{9,13},{10,... | collective-permute-start | bytes 442376 | tf_op jit(solution)/shard_map/ppermute | solution.py:445
  2.6 9.3 %collective-permute-start.2 = (f32[80,512]{1,0:T(8,128)S(1)}, f32[80,512]{1,0:T(8,128)S(1)}, u32[]{:S(2)}, u32[]{:S(2)}) collective-permute-start(f32[80,512]{1,0:T(8,128)S(1)} %get-tuple-element.31), channel_id=1, source_target_pairs={{0,16},{1,17},{2,18},{3,19},{4,8},{5,9},{6,10},{7,11},{8,4},{9,5},... | collective-permute-start | bytes 491528 | tf_op jit(solution)/shard_map/ppermute | solution.py:445
  5.2 5.3 %collective-permute-start = (f32[16,128]{1,0:T(8,128)S(1)}, f32[16,128]{1,0:T(8,128)S(1)}, u32[]{:S(2)}, u32[]{:S(2)}) collective-permute-start(f32[16,128]{1,0:T(8,128)S(1)} %get-tuple-element.28), channel_id=1, source_target_pairs={{0,16},{1,17},{2,18},{3,19},{4,9},{5,8},{6,11},{7,10},{8,5},{9,4},... | collective-permute-start | bytes 24584 | tf_op jit(solution)/shard_map/ppermute | solution.py:445
  5.2 7.3 %collective-permute-start.3 = (f32[16,128]{1,0:T(8,128)S(1)}, f32[16,128]{1,0:T(8,128)S(1)}, u32[]{:S(2)}, u32[]{:S(2)}) collective-permute-start(f32[16,128]{1,0:T(8,128)S(1)} %get-tuple-element.43), channel_id=1, source_target_pairs={{0,4},{1,17},{2,18},{3,7},{4,0},{5,10},{6,9},{7,3},{8,12},{9,6},{1... | collective-permute-start | bytes 24584 | tf_op jit(solution)/shard_map/ppermute | solution.py:445
  7.0 5.6 %collective-permute-start.4 = (f32[16,128]{1,0:T(8,128)S(1)}, f32[16,128]{1,0:T(8,128)S(1)}, u32[]{:S(2)}, u32[]{:S(2)}) collective-permute-start(f32[16,128]{1,0:T(8,128)S(1)} %get-tuple-element.45), channel_id=1, source_target_pairs={{0,1},{1,0},{2,3},{3,2},{4,5},{5,4},{6,7},{7,6},{8,9},{9,8},{10,11... | collective-permute-start | bytes 24584 | tf_op jit(solution)/shard_map/ppermute | solution.py:445
  8.9 3.6 %collective-permute-start.5 = (f32[16,128]{1,0:T(8,128)S(1)}, f32[16,128]{1,0:T(8,128)S(1)}, u32[]{:S(2)}, u32[]{:S(2)}) collective-permute-start(f32[16,128]{1,0:T(8,128)S(1)} %get-tuple-element.46), channel_id=1, source_target_pairs={{0,4},{1,2},{2,1},{3,7},{4,0},{5,6},{6,5},{7,3},{8,12},{9,10},{10,... | collective-permute-start | bytes 24584 | tf_op jit(solution)/shard_map/ppermute | solution.py:445
